TPU v7x, 256 devices: a whole 4x4x8 slice. The times are simulated.
256 devices in a mesh: tm: 8 (over z), space: 32 (over x, y, core).
Axes of the slice: x: 4, y: 4, z: 8, core: 2. Of those that a mesh axis runs over, the one named last changes fastest.
Arguments:
- increment: float32 [8, 1024, 12, 1024], P('tm', 'space'), may hold values from -6 to 6
- multiplier: float32 [8, 1024, 12, 1024], P('tm', 'space'), may hold values from -6 to 6
- obs_dual: float32 [8, 16384], P('tm', 'space'), may hold values from -6 to 6
- obs_index: int32 [8, 16384], P('tm', 'space'), may hold values from 0 to 6143
- obs_variance: float32 [8, 16384], P('tm', 'space'), may hold values from 0.25 to 4
- winds: float32 [8, 1024, 12, 1024], P('tm', 'space'), may hold values from -1 to 1
- spectral_var: float32 [1024, 12, 1024], P(None, None, 'space'), may hold values from 0.1 to 2
Outputs:
- model_rows: float32 [8, 1024, 12, 1024], P('tm', 'space')
- obs_rows: float32 [8, 16384], P('tm', 'space')
- state_rows: float32 [8, 1024, 12, 1024], P('tm', 'space')
All inputs are finite; a program needn't handle non-finite values.
Results may differ from a plain program's by a relative error of at most 0.0061.
Values may be sent and summed in bfloat16 or wider, within the bound.
No kernel may reach another device: no remote copies, remote signals or barrier semaphores. Data moves between devices by JAX's collectives and lax.ppermute only.
A program may use at most 128 MiB of HBM per device.

v0:
```python
import math

import jax
import jax.numpy as jnp
import numpy as np
from jax import lax
from jax.experimental import pallas as pl
from jax.experimental.pallas import tpu as pltpu
from jax.sharding import PartitionSpec as P
import ml_dtypes

STEPS = 4
HALF = 4
F32 = jnp.float32
BF16 = jnp.bfloat16


def cosine_table(count):
    wave = np.arange(count)[:, None]
    point = np.arange(count)[None, :]
    phase = (2 * point + 1) * wave % (4 * count)
    table = np.cos(phase * (math.pi / (2.0 * count))) * math.sqrt(2.0 / count)
    table = np.where(wave == 0, table * math.sqrt(0.5), table)
    return table.astype(np.float32).astype(ml_dtypes.bfloat16)


def block_permutation():
    perm = np.zeros((512, 512), np.float32)
    for i in range(4):
        for j in range(4):
            for b in range(32):
                perm[i * 128 + j * 32 + b, j * 128 + i * 32 + b] = 1.0
    return perm.astype(ml_dtypes.bfloat16)


def block_sums(levels, rows, width):
    cols = (np.arange(width)[:, None] // 16 == np.arange(width // 16)[None, :]).astype(np.float32)
    out = np.arange(rows // 4 * levels)[:, None]
    inn = np.arange(levels * rows)[None, :]
    lines = ((out % levels == inn // rows) & (out // levels == inn % rows // 4)).astype(np.float32)
    return cols.astype(ml_dtypes.bfloat16), lines.astype(ml_dtypes.bfloat16)


def nt(a, b):
    return lax.dot_general(a, b, (((1,), (1,)), ((), ())), preferred_element_type=F32)


def tn(a, b):
    return lax.dot_general(a, b, (((0,), (0,)), ((), ())), preferred_element_type=F32)


def nn(a, b):
    return jnp.dot(a, b, preferred_element_type=F32)


def parts(a):
    first = a.astype(BF16)
    rest = a - first.astype(F32)
    second = rest.astype(BF16)
    third = (rest - second.astype(F32)).astype(BF16)
    return first, second, third


def low_half(shape):
    return lax.broadcasted_iota(jnp.int32, shape, len(shape) - 2) < HALF


def start_kernel(mult_ref, table_ref, flat_ref, spec_ref, head_ref, tail_ref):
    levels = mult_ref.shape[0]
    rows, width = mult_ref.shape[1:]
    flat = mult_ref[...].reshape(levels * rows, width).astype(BF16)
    flat_ref[...] = flat
    half = levels // 2
    first = mult_ref[:, :8, :]
    last = mult_ref[:, rows - 8 :, :]
    low = low_half((half, 8, width))
    head = jnp.where(low, first[:half], pltpu.roll(first[half:], HALF, 1))
    tail = jnp.where(low, pltpu.roll(last[half:], HALF, 1), last[:half])
    head_ref[...] = head.reshape(half * 8, width).astype(BF16)
    tail_ref[...] = tail.reshape(half * 8, width).astype(BF16)
    spec_ref[...] = nt(table_ref[...], flat).astype(BF16)


def edge_kernel(incr_ref, wind_ref, head_ref, tail_ref):
    levels, rows, width = incr_ref.shape
    low = low_half((levels, 8, width))
    head = jnp.where(low, incr_ref[:, :8, :], pltpu.roll(wind_ref[:, :8, :], HALF, 1))
    tail = jnp.where(low, pltpu.roll(wind_ref[:, rows - 8 :, :], HALF, 1), incr_ref[:, rows - 8 :, :])
    head_ref[...] = head.reshape(levels * 8, width).astype(BF16)
    tail_ref[...] = tail.reshape(levels * 8, width).astype(BF16)


def coefficients(level, levels, edge_ref, wind_ref, head_ref, tail_ref, coef_ref):
    rows, width = wind_ref.shape[1:]
    low = low_half((8, width))
    shape = (rows + 8, width)
    row = lax.broadcasted_iota(jnp.int32, shape, 0)
    col = lax.broadcasted_iota(jnp.int32, shape, 1)

    def extended(index):
        at = pl.ds(pl.multiple_of(index * 8, 8), 8)
        margin = jnp.where(low, tail_ref[at, :], head_ref[at, :])
        return jnp.concatenate([wind_ref[index], pltpu.roll(margin, HALF, 0)], axis=0)

    u = extended(level)
    v = extended(level + levels // 2)
    coef_ref[0] = jnp.where(col == width - 1, 0.0, 1.0 - u)
    coef_ref[1] = jnp.where(col == 0, 0.0, 1.0 + u)
    coef_ref[2] = jnp.where((row == rows - 1) & (edge_ref[1] != 0), 0.0, 1.0 - v)
    coef_ref[3] = jnp.where((row == 0) & (edge_ref[0] != 0), 0.0, 1.0 + v)


def forward_steps(x, coef_ref):
    rows, width = x.shape
    for _ in range(STEPS):
        x = (
            x
            + coef_ref[0] * pltpu.roll(x, width - 1, 1)
            + coef_ref[1] * pltpu.roll(x, 1, 1)
            + coef_ref[2] * pltpu.roll(x, rows - 1, 0)
            + coef_ref[3] * pltpu.roll(x, 1, 0)
        )
    return x * (0.2**STEPS)


def backward_steps(y, coef_ref):
    rows, width = y.shape
    for _ in range(STEPS):
        y = (
            y
            + pltpu.roll(coef_ref[1] * y, width - 1, 1)
            + pltpu.roll(coef_ref[0] * y, 1, 1)
            + pltpu.roll(coef_ref[3] * y, rows - 1, 0)
            + pltpu.roll(coef_ref[2] * y, 1, 0)
        )
    return y * (0.2**STEPS)


def one_hots(index, blocks):
    count = index.shape[1]
    high = lax.broadcasted_iota(jnp.int32, (blocks[0], count), 0) == (index >> 6)
    low = lax.broadcasted_iota(jnp.int32, (blocks[1], count), 0) == (index & 63)
    return high, low


def forward_kernel(
    edge_ref, incr_ref, wind_ref, head_in, tail_in, index_ref, dual_ref, variance_ref, cols_ref, lines_ref,
    ends_ref, obs_ref, head_ref, tail_ref, coef_ref,
):
    levels, rows, width = incr_ref.shape
    head_ref[...] = head_in[...].astype(F32)
    tail_ref[...] = tail_in[...].astype(F32)
    low = low_half((8, width))

    def at_level(level, carry):
        coefficients(level, levels, edge_ref, wind_ref, head_ref, tail_ref, coef_ref)
        for group in range(2):
            index = level + group * (levels // 2)
            at = pl.ds(pl.multiple_of(index * 8, 8), 8)
            margin = jnp.where(low, head_ref[at, :], tail_ref[at, :])
            x = forward_steps(jnp.concatenate([incr_ref[index], margin], axis=0), coef_ref)
            ends_ref[pl.ds(pl.multiple_of(index * rows, rows), rows), :] = x[:rows].astype(BF16)
        return carry

    lax.fori_loop(0, levels // 2, at_level, 0)
    cols, lines = cols_ref[...], lines_ref[...]
    narrow = sum(nn(p, cols) for p in parts(incr_ref[...].reshape(levels * rows, width)))
    sums = sum(nn(lines, p) for p in parts(narrow))
    high, low_hot = one_hots(index_ref[...], sums.shape)
    high = high.astype(BF16)
    picked = sum(tn(p, high) for p in parts(sums))
    observed = jnp.sum(jnp.where(low_hot, picked, 0.0), axis=0, keepdims=True) * 0.125
    obs_ref[...] = variance_ref[...] * dual_ref[...] + observed


def backward_kernel(
    edge_ref, next_ref, next_head, next_tail, wind_ref, head_in, tail_in, mult_ref, index_ref, dual_ref,
    cols_ref, lines_ref, state_ref, head_ref, tail_ref, coef_ref, nhead_ref, ntail_ref,
):
    levels, rows, width = mult_ref.shape
    head_ref[...] = head_in[...].astype(F32)
    tail_ref[...] = tail_in[...].astype(F32)
    nhead_ref[...] = next_head[...].astype(F32)
    ntail_ref[...] = next_tail[...].astype(F32)
    low = low_half((8, width))
    cols, lines = cols_ref[...], lines_ref[...]
    blocks = (lines.shape[0], cols.shape[1])
    high, low_hot = one_hots(index_ref[...], blocks)
    low_hot = low_hot.astype(BF16)
    summed = sum(nt(p, low_hot) for p in parts(jnp.where(high, dual_ref[...], 0.0))) * 0.125
    tall = sum(tn(lines, p) for p in parts(summed))
    spread = sum(nt(p, cols) for p in parts(tall))
    state_ref[...] = mult_ref[...] + spread.reshape(levels, rows, width)

    def at_level(level, carry):
        coefficients(level, levels, edge_ref, wind_ref, head_ref, tail_ref, coef_ref)
        at = pl.ds(pl.multiple_of(level * 8, 8), 8)
        head, tail = nhead_ref[at, :], ntail_ref[at, :]
        for group in range(2):
            index = level + group * (levels // 2)
            if group == 0:
                margin = jnp.where(low, head, tail)
            else:
                margin = pltpu.roll(jnp.where(low, tail, head), HALF, 0)
            main = next_ref[pl.ds(pl.multiple_of(index * rows, rows), rows), :].astype(F32)
            y = backward_steps(jnp.concatenate([main, margin], axis=0), coef_ref)
            state_ref[index] = state_ref[index] - y[:rows]
        return carry

    lax.fori_loop(0, levels // 2, at_level, 0)


def gather_lines(came_ref, perm_ref, lines_ref):
    count, rows, wide = came_ref.shape
    groups, fields = count // 4, wide // 128
    perm = perm_ref[...]
    for g in range(fields):
        piece = came_ref[:, :, g * 128 : (g + 1) * 128].reshape(groups, 4, rows, 128)
        left = jnp.concatenate([piece[:, i].reshape(groups * rows, 128) for i in range(4)], axis=1)
        moved = nn(left, perm).astype(BF16)
        for i in range(4):
            for b in range(groups):
                lines_ref[(4 * g + i) * rows : (4 * g + i + 1) * rows, b * 128 : (b + 1) * 128] = moved[
                    b * rows : (b + 1) * rows, i * 128 : (i + 1) * 128
                ]


def latitude_kernel(came_ref, var_ref, turned_ref, perm_ref, out_ref, lines_ref):
    gather_lines(came_ref, perm_ref, lines_ref)
    scaled = (nn(lines_ref[...], turned_ref[...]) * var_ref[...]).astype(BF16)
    out_ref[...] = nt(turned_ref[...], scaled).astype(BF16)


def finish_kernel(came_ref, incr_ref, prev_ref, table_ref, perm_ref, out_ref, lines_ref):
    gather_lines(came_ref, perm_ref, lines_ref)
    covar = nn(lines_ref[...], table_ref[...])
    out_ref[...] = covar + (incr_ref[...] - prev_ref[...].astype(F32))


VMEM = pl.BlockSpec(memory_space=pltpu.VMEM)
SMEM = pl.BlockSpec(memory_space=pltpu.SMEM)


def call(kernel, outs, ins, scratch=(), name=None):
    specs = [SMEM if a.ndim == 1 else VMEM for a in ins]
    return pl.pallas_call(
        kernel,
        out_shape=outs,
        in_specs=specs,
        out_specs=jax.tree.map(lambda _: VMEM, outs),
        scratch_shapes=list(scratch),
        compiler_params=pltpu.CompilerParams(vmem_limit_bytes=40 * 1024 * 1024),
        name=name,
    )(*ins)


def local(increment, multiplier, obs_dual, obs_index, obs_variance, winds, spectral_var):
    rows, levels, width = increment.shape[1:]
    count = lax.axis_size("space")
    times = lax.axis_size("tm")
    lat = rows * count
    waves = width // count
    incr = jnp.transpose(increment[0], (1, 0, 2))
    mult = jnp.transpose(multiplier[0], (1, 0, 2))
    wind = jnp.transpose(winds[0], (1, 0, 2))
    var = jnp.transpose(spectral_var, (1, 2, 0)).reshape(levels * waves, lat)
    table = cosine_table(width)
    turned = np.ascontiguousarray(table.T)
    cols, lines = block_sums(levels, rows, width)
    perm = block_permutation()
    place = lax.axis_index("space")
    edge = jnp.stack([place == 0, place == count - 1]).astype(jnp.int32)
    full = levels * rows

    def shape(*dims):
        return jax.ShapeDtypeStruct(dims, BF16)

    flat, spec, mult_head, mult_tail = call(
        start_kernel,
        (shape(full, width), shape(width, full), shape(levels * 4, width), shape(levels * 4, width)),
        (mult, table),
        name="start",
    )
    head, tail = call(edge_kernel, (shape(levels * 8, width), shape(levels * 8, width)), (incr, wind), name="edges")

    came = lax.all_to_all(spec.reshape(count, waves, full), "space", 0, 0, tiled=True)
    ring = range(count - 1)
    down = [(i + 1, i) for i in ring]
    up = [(i, i + 1) for i in ring]
    head = lax.ppermute(head, "space", down)
    tail = lax.ppermute(tail, "space", up)
    both = ("tm", "space")
    mult_head = lax.ppermute(
        mult_head, both, [((t + 1) * count + a, t * count + b) for t in range(times - 1) for a, b in down]
    )
    mult_tail = lax.ppermute(
        mult_tail, both, [((t + 1) * count + a, t * count + b) for t in range(times - 1) for a, b in up]
    )
    coming = lax.ppermute(flat, "tm", [(t + 1, t) for t in range(times - 1)])

    margin = [pltpu.VMEM((levels * 8, width), F32)] * 2 + [pltpu.VMEM((4, rows + 8, width), F32)]
    ends, obs_rows = call(
        forward_kernel,
        (shape(full, width), jax.ShapeDtypeStruct(obs_dual.shape, F32)),
        (edge, incr, wind, head, tail, obs_index, obs_dual, obs_variance, cols, lines),
        margin,
        name="forward",
    )
    previous = lax.ppermute(ends, "tm", [(t, t + 1) for t in range(times - 1)])

    back = call(
        latitude_kernel,
        shape(lat, full),
        (came, var, turned, perm),
        [pltpu.VMEM((full, lat), BF16)],
        name="latitude",
    )
    returned = lax.all_to_all(back.reshape(count, rows, full), "space", 0, 0, tiled=True)

    state_rows = call(
        backward_kernel,
        jax.ShapeDtypeStruct((levels, rows, width), F32),
        (edge, coming, mult_head, mult_tail, wind, head, tail, mult, obs_index, obs_dual, cols, lines),
        margin + [pltpu.VMEM((levels * 4, width), F32)] * 2,
        name="backward",
    )
    model_rows = call(
        finish_kernel,
        jax.ShapeDtypeStruct((full, width), F32),
        (returned, incr.reshape(full, width), previous, table, perm),
        [pltpu.VMEM((full, width), BF16)],
        name="finish",
    )

    def placed(field):
        return jnp.transpose(field.reshape(levels, rows, width), (1, 0, 2))[None]

    return (placed(model_rows), obs_rows, placed(state_rows))


def solution(mesh):
    specs = (
        P("tm", "space", None, None),
        P("tm", "space", None, None),
        P("tm", "space"),
        P("tm", "space"),
        P("tm", "space"),
        P("tm", "space", None, None),
        P(None, None, "space"),
    )
    return jax.shard_map(
        local,
        mesh=mesh,
        in_specs=specs,
        out_specs=(P("tm", "space", None, None), P("tm", "space"), P("tm", "space", None, None)),
        check_vma=False,
    )
```

profile of v0, /device:TPU:98, one launch (start us, length us, event | category | flops | bytes accessed | tf_op | source)
XLA Modules:
  0.0 90.8 jit_solution(5550444542245858617)
XLA Ops:
  0.6 1.6 %copy-done.2 = bf16[1024,1024]{1,0:T(8,128)(2,1)S(1)} copy-done((bf16[1024,1024]{1,0:T(8,128)(2,1)S(1)}, bf16[1024,1024]{1,0:T(8,128)(2,1)}, u32[]{:S(2)}) %copy-start.2) | copy-done | bytes 2097176
  2.2 1.4 %copy-done.4 = f32[1,32,12,1024]{3,1,2,0:T(8,128)S(1)} copy-done((f32[1,32,12,1024]{3,1,2,0:T(8,128)S(1)}, f32[1,32,12,1024]{3,1,2,0:T(8,128)}, u32[]{:S(2)}) %copy-start.4) | copy-done | bytes 1572888
  3.6 1.7 %start.1 = (bf16[384,1024]{1,0:T(8,128)(2,1)}, bf16[1024,384]{1,0:T(8,128)(2,1)S(1)}, bf16[48,1024]{1,0:T(8,128)(2,1)S(1)}, bf16[48,1024]{1,0:T(8,128)(2,1)S(1)}) custom-call(f32[12,32,1024]{2,1,0:T(8,128)S(1)} %bitcast.32, bf16[1024,1024]{1,0:T(8,128)(2,1)S(1)} %copy-done.2), custom_call_target="tpu_custom_call" | custom-call | tf_op jit(solution)/shard_map/start/pallas_call | solution.py:246
  6.3 7.8 %all-to-all-start = ((bf16[32,32,384]{2,1,0:T(8,128)(2,1)}), bf16[32,32,384]{2,1,0:T(8,128)(2,1)}, u32[]{:S(2)}, u32[]{:S(2)}) async-start(bf16[32,32,384]{2,1,0:T(8,128)(2,1)} %bitcast.36), calls=%async_computation | async-start | bytes 1572864 | tf_op jit(solution)/shard_map/all_to_all | solution.py:286
  15.0 4.3 %collective-permute-start = (bf16[96,1024]{1,0:T(8,128)(2,1)}, bf16[96,1024]{1,0:T(8,128)(2,1)}, u32[]{:S(2)}, u32[]{:S(2)}) collective-permute-start(bf16[96,1024]{1,0:T(8,128)(2,1)} %get-tuple-element.12), channel_id=1, source_target_pairs={{1,0},{2,1},{3,2},{4,3},{5,4},{6,5},{7,6},{8,7},{9,8},{10,9},{11,1... | collective-permute-start | bytes 589832 | tf_op jit(solution)/shard_map/ppermute | solution.py:290
  19.3 1.9 %collective-permute-start.1 = (bf16[96,1024]{1,0:T(8,128)(2,1)}, bf16[96,1024]{1,0:T(8,128)(2,1)}, u32[]{:S(2)}, u32[]{:S(2)}) collective-permute-start(bf16[96,1024]{1,0:T(8,128)(2,1)} %get-tuple-element.13), channel_id=1, source_target_pairs={{0,1},{1,2},{2,3},{3,4},{4,5},{5,6},{6,7},{7,8},{8,9},{9,10},{10,1... | collective-permute-start | bytes 589832 | tf_op jit(solution)/shard_map/ppermute | solution.py:291
  21.3 2.0 %collective-permute-start.3 = (bf16[384,1024]{1,0:T(8,128)(2,1)}, bf16[384,1024]{1,0:T(8,128)(2,1)}, u32[]{:S(2)}, u32[]{:S(2)}) collective-permute-start(bf16[384,1024]{1,0:T(8,128)(2,1)} %get-tuple-element.16), channel_id=1, source_target_pairs={{32,0},{64,32},{96,64},{128,96},{160,128},{192,160},{224,192},{33,... | collective-permute-start | bytes 2359304 | tf_op jit(solution)/shard_map/ppermute | solution.py:299
  23.4 2.4 %collective-permute-done.head_in = bf16[96,1024]{1,0:T(8,128)(2,1)} collective-permute-done((bf16[96,1024]{1,0:T(8,128)(2,1)}, bf16[96,1024]{1,0:T(8,128)(2,1)}, u32[]{:S(2)}, u32[]{:S(2)}) %collective-permute-start) | collective-permute-done | bytes 196640 | tf_op jit(solution)/shard_map/ppermute | solution.py:290
  25.8 3.4 %collective-permute-done.1.tail_in = bf16[96,1024]{1,0:T(8,128)(2,1)} collective-permute-done((bf16[96,1024]{1,0:T(8,128)(2,1)}, bf16[96,1024]{1,0:T(8,128)(2,1)}, u32[]{:S(2)}, u32[]{:S(2)}) %collective-permute-start.1) | collective-permute-done | bytes 196640 | tf_op jit(solution)/shard_map/ppermute | solution.py:291
  29.2 10.5 %forward.1 = (bf16[384,1024]{1,0:T(8,128)(2,1)}, f32[1,512]{1,0:T(1,128)}) custom-call(s32[2]{0:T(128)S(1)} %add_convert_fusion.edge_ref, f32[12,32,1024]{2,1,0:T(8,128)S(1)} %bitcast.27, f32[12,32,1024]{2,1,0:T(8,128)S(1)} %bitcast.30, bf16[96,1024]{1,0:T(8,128)(2,1)} %collective-permute-done.head_in, bf16[96,1024]{1,0:T(8,128)(2,1)} %collective-permute-done.1.tail_in, ...), custom_call_target="tpu_custom_call" | custom-call | tf_op jit(solution)/shard_map/forward/pallas_call | solution.py:246
  39.7 5.0 %collective-permute-start.2 = (bf16[384,1024]{1,0:T(8,128)(2,1)}, bf16[384,1024]{1,0:T(8,128)(2,1)}, u32[]{:S(2)}, u32[]{:S(2)}) collective-permute-start(bf16[384,1024]{1,0:T(8,128)(2,1)} %get-tuple-element.14), channel_id=1, source_target_pairs={{0,32},{32,64},{64,96},{96,128},{128,160},{160,192},{192,224},{1,3... | collective-permute-start | bytes 2359304 | tf_op jit(solution)/shard_map/ppermute | solution.py:309
  45.8 1.6 %copy-done.9 = bf16[1024,1024]{1,0:T(8,128)(2,1)S(1)} copy-done((bf16[1024,1024]{1,0:T(8,128)(2,1)S(1)}, bf16[1024,1024]{1,0:T(8,128)(2,1)}, u32[]{:S(2)}) %copy-start.9) | copy-done | bytes 2097176
  47.4 1.4 %copy-done.10 = f32[1024,12,32]{0,2,1:T(8,128)S(1)} copy-done((f32[1024,12,32]{0,2,1:T(8,128)S(1)}, f32[1024,12,32]{0,2,1:T(8,128)}, u32[]{:S(2)}) %copy-start.10) | copy-done | bytes 1572888
  48.8 3.6 %latitude.1 = bf16[1024,384]{1,0:T(8,128)(2,1)S(1)} custom-call(bf16[32,32,384]{2,1,0:T(8,128)(2,1)} %all-to-all-done.came_ref, f32[384,1024]{1,0:T(8,128)S(1)} %bitcast.35, bf16[1024,1024]{1,0:T(8,128)(2,1)S(1)} %copy-done.9, bf16[512,512]{1,0:T(8,128)(2,1)S(1)} %copy-done.7), custom_call_target="tpu_custom_call" | custom-call | tf_op jit(solution)/shard_map/latitude/pallas_call | solution.py:246
  53.3 4.9 %all-to-all-start.1 = ((bf16[32,32,384]{2,1,0:T(8,128)(2,1)}), bf16[32,32,384]{2,1,0:T(8,128)(2,1)}, u32[]{:S(2)}, u32[]{:S(2)}) async-start(bf16[32,32,384]{2,1,0:T(8,128)(2,1)} %bitcast.34), calls=%async_computation.1 | async-start | bytes 1572864 | tf_op jit(solution)/shard_map/all_to_all | solution.py:318
  58.2 2.7 %collective-permute-start.4 = (bf16[48,1024]{1,0:T(8,128)(2,1)}, bf16[48,1024]{1,0:T(8,128)(2,1)S(1)}, u32[]{:S(2)}, u32[]{:S(2)}) collective-permute-start(bf16[48,1024]{1,0:T(8,128)(2,1)} %copy-done.18), channel_id=1, source_target_pairs={{33,0},{34,1},{35,2},{36,3},{37,4},{38,5},{39,6},{40,7},{41,8},{42... | collective-permute-start | bytes 294920 | tf_op jit(solution)/shard_map/ppermute | solution.py:293
  60.9 1.9 %collective-permute-start.5 = (bf16[48,1024]{1,0:T(8,128)(2,1)}, bf16[48,1024]{1,0:T(8,128)(2,1)S(1)}, u32[]{:S(2)}, u32[]{:S(2)}) collective-permute-start(bf16[48,1024]{1,0:T(8,128)(2,1)} %copy-done.17), channel_id=1, source_target_pairs={{32,1},{33,2},{34,3},{35,4},{36,5},{37,6},{38,7},{39,8},{40,9},{41... | collective-permute-start | bytes 294920 | tf_op jit(solution)/shard_map/ppermute | solution.py:296
  62.8 2.8 %collective-permute-done.4.next_head = bf16[48,1024]{1,0:T(8,128)(2,1)S(1)} collective-permute-done((bf16[48,1024]{1,0:T(8,128)(2,1)}, bf16[48,1024]{1,0:T(8,128)(2,1)S(1)}, u32[]{:S(2)}, u32[]{:S(2)}) %collective-permute-start.4) | collective-permute-done | bytes 98336 | tf_op jit(solution)/shard_map/ppermute | solution.py:293
  65.5 6.3 %collective-permute-done.5.next_tail = bf16[48,1024]{1,0:T(8,128)(2,1)S(1)} collective-permute-done((bf16[48,1024]{1,0:T(8,128)(2,1)}, bf16[48,1024]{1,0:T(8,128)(2,1)S(1)}, u32[]{:S(2)}, u32[]{:S(2)}) %collective-permute-start.5) | collective-permute-done | bytes 98336 | tf_op jit(solution)/shard_map/ppermute | solution.py:296
  71.9 1.4 %copy-done.5 = f32[1,32,12,1024]{3,1,2,0:T(8,128)S(1)} copy-done((f32[1,32,12,1024]{3,1,2,0:T(8,128)S(1)}, f32[1,32,12,1024]{3,1,2,0:T(8,128)}, u32[]{:S(2)}) %copy-start.5) | copy-done | bytes 1572888
  73.3 10.9 %backward.1 = f32[12,32,1024]{2,1,0:T(8,128)} custom-call(s32[2]{0:T(128)S(1)} %add_convert_fusion.edge_ref, bf16[384,1024]{1,0:T(8,128)(2,1)} %collective-permute-done.3.next_ref, bf16[48,1024]{1,0:T(8,128)(2,1)S(1)} %collective-permute-done.4.next_head, bf16[48,1024]{1,0:T(8,128)(2,1)S(1)} %collective-permute-done.5.next_tail, ...), custom_call_target="tpu_custom_call" | custom-call | tf_op jit(solution)/shard_map/backward/pallas_call | solution.py:246
  84.2 1.6 %copy-done.3 = bf16[1024,1024]{1,0:T(8,128)(2,1)S(1)} copy-done((bf16[1024,1024]{1,0:T(8,128)(2,1)S(1)}, bf16[1024,1024]{1,0:T(8,128)(2,1)}, u32[]{:S(2)}) %copy-start.3) | copy-done | bytes 2097176
  85.8 1.0 %copy-done.8 = bf16[512,512]{1,0:T(8,128)(2,1)S(1)} copy-done((bf16[512,512]{1,0:T(8,128)(2,1)S(1)}, bf16[512,512]{1,0:T(8,128)(2,1)}, u32[]{:S(2)}) %copy-start.8) | copy-done | bytes 524312
  86.9 3.9 %finish.1 = f32[384,1024]{1,0:T(8,128)} custom-call(bf16[32,32,384]{2,1,0:T(8,128)(2,1)} %all-to-all-done.1.came_ref, f32[384,1024]{1,0:T(8,128)S(1)} %bitcast.28, bf16[384,1024]{1,0:T(8,128)(2,1)} %collective-permute-done.2.prev_ref, bf16[1024,1024]{1,0:T(8,128)(2,1)S(1)} %copy-done.3, bf16[512,512]{1,0:T(8,128)(2,1)S(1)} %copy-done.8), custom_call_target="tpu_custom_call" | custom-call | tf_op jit(solution)/shard_map/finish/pallas_call | solution.py:246
  (37 shorter events, 3.8 us)
Async XLA Ops:
  0.6 1.6 %copy-start.2 = (bf16[1024,1024]{1,0:T(8,128)(2,1)S(1)}, bf16[1024,1024]{1,0:T(8,128)(2,1)}, u32[]{:S(2)}) copy-start(bf16[1024,1024]{1,0:T(8,128)(2,1)} %constant.18.clone.table_ref) | copy-start | bytes 6291460
  2.2 1.4 %copy-start.4 = (f32[1,32,12,1024]{3,1,2,0:T(8,128)S(1)}, f32[1,32,12,1024]{3,1,2,0:T(8,128)}, u32[]{:S(2)}) copy-start(f32[1,32,12,1024]{3,1,2,0:T(8,128)} %param.13) | copy-start | bytes 4718596
  3.6 10.5 %copy-start.1 = (f32[1,32,12,1024]{3,1,2,0:T(8,128)S(1)}, f32[1,32,12,1024]{3,1,2,0:T(8,128)}, u32[]{:S(2)}) copy-start(f32[1,32,12,1024]{3,1,2,0:T(8,128)} %param.17) | copy-start | bytes 4718596
  6.3 7.8 %copy-start.17 = (bf16[48,1024]{1,0:T(8,128)(2,1)}, bf16[48,1024]{1,0:T(8,128)(2,1)S(1)}, u32[]{:S(2)}) copy-start(bf16[48,1024]{1,0:T(8,128)(2,1)S(1)} %get-tuple-element.18) | copy-start | bytes 294916
  6.3 7.8 %copy-start.18 = (bf16[48,1024]{1,0:T(8,128)(2,1)}, bf16[48,1024]{1,0:T(8,128)(2,1)S(1)}, u32[]{:S(2)}) copy-start(bf16[48,1024]{1,0:T(8,128)(2,1)S(1)} %get-tuple-element.17) | copy-start | bytes 294916
  6.3 7.8 %copy-start = (f32[1,32,12,1024]{3,1,2,0:T(8,128)S(1)}, f32[1,32,12,1024]{3,1,2,0:T(8,128)}, u32[]{:S(2)}) copy-start(f32[1,32,12,1024]{3,1,2,0:T(8,128)} %param.12) | copy-start | bytes 4718596
  6.3 38.5 %all-to-all-start = ((bf16[32,32,384]{2,1,0:T(8,128)(2,1)}), bf16[32,32,384]{2,1,0:T(8,128)(2,1)}, u32[]{:S(2)}, u32[]{:S(2)}) async-start(bf16[32,32,384]{2,1,0:T(8,128)(2,1)} %bitcast.36), calls=%async_computation | async-start | bytes 1572864 | tf_op jit(solution)/shard_map/all_to_all | solution.py:286
  14.1 15.1 %copy-start.11 = (bf16[1024,64]{1,0:T(8,128)(2,1)S(1)}, bf16[1024,64]{1,0:T(8,128)(2,1)}, u32[]{:S(2)}) copy-start(bf16[1024,64]{1,0:T(8,128)(2,1)} %constant.19.clone.cols_ref) | copy-start | bytes 393220
  14.1 15.0 %copy-start.13 = (bf16[96,384]{1,0:T(8,128)(2,1)S(1)}, bf16[96,384]{1,0:T(8,128)(2,1)}, u32[]{:S(2)}) copy-start(bf16[96,384]{1,0:T(8,128)(2,1)} %constant.20.clone.lines_ref) | copy-start | bytes 221188
  14.1 15.0 %copy-start.14 = (s32[1,512]{1,0:T(1,128)S(1)}, s32[1,512]{1,0:T(1,128)}, u32[]{:S(2)}) copy-start(s32[1,512]{1,0:T(1,128)} %index_ref.3) | copy-start | bytes 6148
  14.2 15.0 %copy-start.15 = (f32[1,512]{1,0:T(1,128)S(1)}, f32[1,512]{1,0:T(1,128)}, u32[]{:S(2)}) copy-start(f32[1,512]{1,0:T(1,128)} %dual_ref.3) | copy-start | bytes 6148
  14.2 15.0 %copy-start.16 = (f32[1,512]{1,0:T(1,128)S(1)}, f32[1,512]{1,0:T(1,128)}, u32[]{:S(2)}) copy-start(f32[1,512]{1,0:T(1,128)} %variance_ref.1) | copy-start | bytes 6148
  15.0 10.8 %collective-permute-start = (bf16[96,1024]{1,0:T(8,128)(2,1)}, bf16[96,1024]{1,0:T(8,128)(2,1)}, u32[]{:S(2)}, u32[]{:S(2)}) collective-permute-start(bf16[96,1024]{1,0:T(8,128)(2,1)} %get-tuple-element.12), channel_id=1, source_target_pairs={{1,0},{2,1},{3,2},{4,3},{5,4},{6,5},{7,6},{8,7},{9,8},{10,9},{11,1... | collective-permute-start | bytes 589832 | tf_op jit(solution)/shard_map/ppermute | solution.py:290
  19.3 9.8 %collective-permute-start.1 = (bf16[96,1024]{1,0:T(8,128)(2,1)}, bf16[96,1024]{1,0:T(8,128)(2,1)}, u32[]{:S(2)}, u32[]{:S(2)}) collective-permute-start(bf16[96,1024]{1,0:T(8,128)(2,1)} %get-tuple-element.13), channel_id=1, source_target_pairs={{0,1},{1,2},{2,3},{3,4},{4,5},{5,6},{6,7},{7,8},{8,9},{9,10},{10,1... | collective-permute-start | bytes 589832 | tf_op jit(solution)/shard_map/ppermute | solution.py:291
  21.3 50.6 %collective-permute-start.3 = (bf16[384,1024]{1,0:T(8,128)(2,1)}, bf16[384,1024]{1,0:T(8,128)(2,1)}, u32[]{:S(2)}, u32[]{:S(2)}) collective-permute-start(bf16[384,1024]{1,0:T(8,128)(2,1)} %get-tuple-element.16), channel_id=1, source_target_pairs={{32,0},{64,32},{96,64},{128,96},{160,128},{192,160},{224,192},{33,... | collective-permute-start | bytes 2359304 | tf_op jit(solution)/shard_map/ppermute | solution.py:299
  39.7 44.5 %collective-permute-start.2 = (bf16[384,1024]{1,0:T(8,128)(2,1)}, bf16[384,1024]{1,0:T(8,128)(2,1)}, u32[]{:S(2)}, u32[]{:S(2)}) collective-permute-start(bf16[384,1024]{1,0:T(8,128)(2,1)} %get-tuple-element.14), channel_id=1, source_target_pairs={{0,32},{32,64},{64,96},{96,128},{128,160},{160,192},{192,224},{1,3... | collective-permute-start | bytes 2359304 | tf_op jit(solution)/shard_map/ppermute | solution.py:309
  44.7 1.0 %copy-start.7 = (bf16[512,512]{1,0:T(8,128)(2,1)S(1)}, bf16[512,512]{1,0:T(8,128)(2,1)}, u32[]{:S(2)}) copy-start(bf16[512,512]{1,0:T(8,128)(2,1)} %constant.22.clone.perm_ref) | copy-start | bytes 1572868
  45.8 1.6 %copy-start.9 = (bf16[1024,1024]{1,0:T(8,128)(2,1)S(1)}, bf16[1024,1024]{1,0:T(8,128)(2,1)}, u32[]{:S(2)}) copy-start(bf16[1024,1024]{1,0:T(8,128)(2,1)} %constant.21.clone.turned_ref) | copy-start | bytes 6291460
  47.4 1.4 %copy-start.10 = (f32[1024,12,32]{0,2,1:T(8,128)S(1)}, f32[1024,12,32]{0,2,1:T(8,128)}, u32[]{:S(2)}) copy-start(f32[1024,12,32]{0,2,1:T(8,128)} %param.18) | copy-start | bytes 4718596
  53.3 30.9 %all-to-all-start.1 = ((bf16[32,32,384]{2,1,0:T(8,128)(2,1)}), bf16[32,32,384]{2,1,0:T(8,128)(2,1)}, u32[]{:S(2)}, u32[]{:S(2)}) async-start(bf16[32,32,384]{2,1,0:T(8,128)(2,1)} %bitcast.34), calls=%async_computation.1 | async-start | bytes 1572864 | tf_op jit(solution)/shard_map/all_to_all | solution.py:318
  58.2 7.4 %collective-permute-start.4 = (bf16[48,1024]{1,0:T(8,128)(2,1)}, bf16[48,1024]{1,0:T(8,128)(2,1)S(1)}, u32[]{:S(2)}, u32[]{:S(2)}) collective-permute-start(bf16[48,1024]{1,0:T(8,128)(2,1)} %copy-done.18), channel_id=1, source_target_pairs={{33,0},{34,1},{35,2},{36,3},{37,4},{38,5},{39,6},{40,7},{41,8},{42... | collective-permute-start | bytes 294920 | tf_op jit(solution)/shard_map/ppermute | solution.py:293
  60.9 11.0 %collective-permute-start.5 = (bf16[48,1024]{1,0:T(8,128)(2,1)}, bf16[48,1024]{1,0:T(8,128)(2,1)S(1)}, u32[]{:S(2)}, u32[]{:S(2)}) collective-permute-start(bf16[48,1024]{1,0:T(8,128)(2,1)} %copy-done.17), channel_id=1, source_target_pairs={{32,1},{33,2},{34,3},{35,4},{36,5},{37,6},{38,7},{39,8},{40,9},{41... | collective-permute-start | bytes 294920 | tf_op jit(solution)/shard_map/ppermute | solution.py:296
  71.9 1.4 %copy-start.5 = (f32[1,32,12,1024]{3,1,2,0:T(8,128)S(1)}, f32[1,32,12,1024]{3,1,2,0:T(8,128)}, u32[]{:S(2)}) copy-start(f32[1,32,12,1024]{3,1,2,0:T(8,128)} %param.13) | copy-start | bytes 4718596
  84.2 1.6 %copy-start.3 = (bf16[1024,1024]{1,0:T(8,128)(2,1)S(1)}, bf16[1024,1024]{1,0:T(8,128)(2,1)}, u32[]{:S(2)}) copy-start(bf16[1024,1024]{1,0:T(8,128)(2,1)} %constant.18.clone.table_ref) | copy-start | bytes 6291460
  (3 other events, 2.8 us)
where the time goes:
time: 91.6 us; the launch traced here: 90.8 us
  Pallas kernels  31.6 us (34%)
  starting transfers between devices  30.5 us (33%)
  waiting for transfers between devices  14.9 us (16%)
  local copies, waits for them, and re-layouts  12.9 us (14%)
    pallas_call x6, Pallas kernels, call(): pl.pallas_call(kernel, out_shape=outs, in_specs=specs, out_specs=jax.tree...  31.6 us
    unnamed x38, local copies, waits for them, and re-layouts  12.9 us
    all_to_all x1, starting transfers between devices, local(): lax.all_to_all(spec.reshape(count, waves, full), 'space', 0, 0, tiled=True)  7.8 us
    ppermute x1, waiting for transfers between devices, local(): lax.ppermute(mult_tail, both, [((t + 1) * count + a, t * count + b) for t...  6.33 us
    ppermute x1, starting transfers between devices, local(): previous = lax.ppermute(ends, 'tm', [(t, t + 1) for t in range(times - 1)])  5.02 us
    all_to_all x1, starting transfers between devices, local(): lax.all_to_all(back.reshape(count, rows, full), 'space', 0, 0, tiled=True)  4.87 us
    ppermute x1, starting transfers between devices, local(): head = lax.ppermute(head, 'space', down)  4.32 us
    ppermute x1, waiting for transfers between devices, local(): tail = lax.ppermute(tail, 'space', up)  3.4 us
  transfers between devices with their start and end apart: 8, of which 4 were waited for; matrix products, arithmetic and copies ran while one was open for 0% of the time, Pallas kernels for 29%

commit v1 on v0

v1 whole, which is shorter than its diff:
```python
import math

import jax
import jax.numpy as jnp
import numpy as np
from jax import lax
from jax.experimental import pallas as pl
from jax.experimental.pallas import tpu as pltpu
from jax.sharding import PartitionSpec as P
import ml_dtypes

STEPS = 4
HALF = 4
F32 = jnp.float32
BF16 = jnp.bfloat16


def cosine_table(count):
    wave = np.arange(count)[:, None]
    point = np.arange(count)[None, :]
    phase = (2 * point + 1) * wave % (4 * count)
    table = np.cos(phase * (math.pi / (2.0 * count))) * math.sqrt(2.0 / count)
    table = np.where(wave == 0, table * math.sqrt(0.5), table)
    return table.astype(np.float32).astype(ml_dtypes.bfloat16)


def block_sums(levels, rows, width):
    cols = (np.arange(width)[:, None] // 16 == np.arange(width // 16)[None, :]).astype(np.float32)
    out = np.arange(rows // 4 * levels)[:, None]
    inn = np.arange(levels * rows)[None, :]
    lines = ((out % levels == inn // rows) & (out // levels == inn % rows // 4)).astype(np.float32)
    return cols.astype(ml_dtypes.bfloat16), lines.astype(ml_dtypes.bfloat16)


def nt(a, b):
    return lax.dot_general(a, b, (((1,), (1,)), ((), ())), preferred_element_type=F32)


def tn(a, b):
    return lax.dot_general(a, b, (((0,), (0,)), ((), ())), preferred_element_type=F32)


def nn(a, b):
    return jnp.dot(a, b, preferred_element_type=F32)


def parts(a):
    first = a.astype(BF16)
    rest = a - first.astype(F32)
    second = rest.astype(BF16)
    third = (rest - second.astype(F32)).astype(BF16)
    return first, second, third


def low_half(shape):
    return lax.broadcasted_iota(jnp.int32, shape, len(shape) - 2) < HALF


class Copies:
    def __init__(self, sems):
        self.sems = sems
        self.count = 0

    def start(self, source, target):
        copy = pltpu.make_async_copy(source, target, self.sems.at[self.count])
        self.count += 1
        copy.start()
        return copy


def start_kernel(
    mult_hbm, table_hbm, incr_hbm, wind_hbm,
    flat_hbm, spec_hbm, mhead_hbm, mtail_hbm, head_hbm, tail_hbm,
    mult_ref, table_ref, edge_ref, flat_ref, spec_ref, mhead_ref, mtail_ref, head_ref, tail_ref, sems,
):
    levels, rows, width = mult_ref.shape
    half = levels // 2
    copies = Copies(sems)
    mult_in = [copies.start(mult_hbm.at[pl.ds(3 * i, 3)], mult_ref.at[pl.ds(3 * i, 3)]) for i in range(4)]
    table_in = [
        copies.start(table_hbm.at[pl.ds(256 * i, 256)], table_ref.at[pl.ds(256 * i, 256)]) for i in range(4)
    ]
    edge_in = [
        copies.start(source.at[:, pl.ds(at, 8), :], edge_ref.at[i])
        for i, (source, at) in enumerate(
            [(incr_hbm, 0), (wind_hbm, 0), (incr_hbm, rows - 8), (wind_hbm, rows - 8)]
        )
    ]
    out = []
    for copy in mult_in:
        copy.wait()
    flat_ref[...] = mult_ref[...].reshape(levels * rows, width).astype(BF16)
    out.append(copies.start(flat_ref, flat_hbm))
    first = mult_ref[:, :8, :]
    last = mult_ref[:, rows - 8 :, :]
    low = low_half((half, 8, width))
    head = jnp.where(low, first[:half], pltpu.roll(first[half:], HALF, 1))
    tail = jnp.where(low, pltpu.roll(last[half:], HALF, 1), last[:half])
    mhead_ref[...] = head.reshape(half * 8, width).astype(BF16)
    mtail_ref[...] = tail.reshape(half * 8, width).astype(BF16)
    out.append(copies.start(mhead_ref, mhead_hbm))
    out.append(copies.start(mtail_ref, mtail_hbm))
    flat = flat_ref[...]
    for i, copy in enumerate(table_in):
        copy.wait()
        part = pl.ds(256 * i, 256)
        spec_ref[part] = nt(table_ref[part], flat).astype(BF16)
        out.append(copies.start(spec_ref.at[part], spec_hbm.at[part]))
    for copy in edge_in:
        copy.wait()
    low = low_half((levels, 8, width))
    head = jnp.where(low, edge_ref[0], pltpu.roll(edge_ref[1], HALF, 1))
    tail = jnp.where(low, pltpu.roll(edge_ref[3], HALF, 1), edge_ref[2])
    head_ref[...] = head.reshape(levels * 8, width).astype(BF16)
    tail_ref[...] = tail.reshape(levels * 8, width).astype(BF16)
    out.append(copies.start(head_ref, head_hbm))
    out.append(copies.start(tail_ref, tail_hbm))
    for copy in out:
        copy.wait()


TILES = 5


def spread_rows(stage_ref, main, margin):
    rows, width = main.shape
    across = width // 128
    for c in range(across):
        stage_ref[c, :rows, :] = main[:, c * 128 : (c + 1) * 128]
        stage_ref[c, rows:, :] = margin[:, c * 128 : (c + 1) * 128]
    return [[stage_ref[c, pl.ds(t, 8, stride=TILES), :] for t in range(TILES)] for c in range(across)]


def join_rows(stage_ref, tiles, rows):
    for c, column in enumerate(tiles):
        for t, tile in enumerate(column):
            stage_ref[c, pl.ds(t, 8, stride=TILES), :] = tile * (0.2**STEPS)
    return jnp.concatenate([stage_ref[c, :rows, :] for c in range(len(tiles))], axis=1)


def coefficients(level, levels, edge_ref, wind_ref, head_ref, tail_ref, stage_ref, coef_ref):
    rows = wind_ref.shape[1]
    low = low_half((8, wind_ref.shape[2]))
    sublane = lax.broadcasted_iota(jnp.int32, (8, 128), 0)

    def extended(index, stage):
        at = pl.ds(pl.multiple_of(index * 8, 8), 8)
        margin = pltpu.roll(jnp.where(low, tail_ref[at, :], head_ref[at, :]), HALF, 0)
        return spread_rows(stage, wind_ref[index], margin)

    u = extended(level, stage_ref.at[0])
    v = extended(level + levels // 2, stage_ref.at[1])
    first = (sublane == 0) & (edge_ref[0] != 0)
    last = (sublane == (rows - 1) // TILES) & (edge_ref[1] != 0)
    for c in range(len(u)):
        for t in range(TILES):
            north, south = 1.0 - v[c][t], 1.0 + v[c][t]
            if t == (rows - 1) % TILES:
                north = jnp.where(last, 0.0, north)
            if t == 0:
                south = jnp.where(first, 0.0, south)
            coef_ref[0, c, t] = 1.0 - u[c][t]
            coef_ref[1, c, t] = 1.0 + u[c][t]
            coef_ref[2, c, t] = north
            coef_ref[3, c, t] = south


def north_of(column, t):
    return column[t + 1] if t < TILES - 1 else pltpu.roll(column[0], 7, 0)


def south_of(column, t):
    return column[t - 1] if t > 0 else pltpu.roll(column[TILES - 1], 1, 0)


def forward_steps(x, coef_ref):
    lane = lax.broadcasted_iota(jnp.int32, (8, 128), 1)
    first, last = lane == 0, lane == 127
    ends = len(x) - 1
    for _ in range(STEPS):
        new = []
        for c in range(len(x)):
            column = []
            for t in range(TILES):
                here = x[c][t]
                east = pltpu.roll(jnp.where(first, x[c + 1][t] if c < ends else 0.0, here), 127, 1)
                west = pltpu.roll(jnp.where(last, x[c - 1][t] if c > 0 else 0.0, here), 1, 1)
                column.append(
                    (here + coef_ref[0, c, t] * east)
                    + coef_ref[1, c, t] * west
                    + (coef_ref[2, c, t] * north_of(x[c], t) + coef_ref[3, c, t] * south_of(x[c], t))
                )
            new.append(column)
        x = new
    return x


def backward_steps(y, coef_ref):
    lane = lax.broadcasted_iota(jnp.int32, (8, 128), 1)
    first, last = lane == 0, lane == 127
    ends = len(y) - 1
    for _ in range(STEPS):
        new = []
        for c in range(len(y)):
            column = []
            up = [coef_ref[3, c, t] * y[c][t] for t in range(TILES)]
            down = [coef_ref[2, c, t] * y[c][t] for t in range(TILES)]
            for t in range(TILES):
                here = y[c][t]
                after = coef_ref[1, c + 1, t] * y[c + 1][t] if c < ends else 0.0
                before = coef_ref[0, c - 1, t] * y[c - 1][t] if c > 0 else 0.0
                east = pltpu.roll(jnp.where(first, after, coef_ref[1, c, t] * here), 127, 1)
                west = pltpu.roll(jnp.where(last, before, coef_ref[0, c, t] * here), 1, 1)
                column.append((here + east) + west + (north_of(up, t) + south_of(down, t)))
            new.append(column)
        y = new
    return y


def one_hots(index, blocks):
    count = index.shape[1]
    high = lax.broadcasted_iota(jnp.int32, (blocks[0], count), 0) == (index >> 6)
    low = lax.broadcasted_iota(jnp.int32, (blocks[1], count), 0) == (index & 63)
    return high, low


def forward_kernel(
    edge_ref, incr_hbm, wind_hbm, head_hbm, tail_hbm, ends_hbm,
    incr_ref, wind_ref, head_in, tail_in, head_ref, tail_ref, stage_ref, coef_ref, ends_ref, sems, level_sems,
):
    levels, rows, width = incr_ref.shape
    half = levels // 2
    copies = Copies(sems)
    margin_in = [copies.start(head_hbm, head_in), copies.start(tail_hbm, tail_in)]

    def fetch(kind, index):
        source, target = ((wind_hbm, wind_ref), (incr_hbm, incr_ref))[kind]
        return pltpu.make_async_copy(source.at[index], target.at[index], level_sems.at[kind, index])

    def put(index):
        part = pl.ds(pl.multiple_of(index * rows, rows), rows)
        return pltpu.make_async_copy(ends_ref.at[part], ends_hbm.at[part], level_sems.at[2, index])

    for level in range(half):
        for index in (level, level + half):
            for kind in range(2):
                fetch(kind, index).start()
    for copy in margin_in:
        copy.wait()
    head_ref[...] = head_in[...].astype(F32)
    tail_ref[...] = tail_in[...].astype(F32)
    low = low_half((8, width))

    def at_level(level, carry):
        for index in (level, level + half):
            for kind in range(2):
                fetch(kind, index).wait()
        coefficients(level, levels, edge_ref, wind_ref, head_ref, tail_ref, stage_ref, coef_ref)
        for group in range(2):
            index = level + group * half
            at = pl.ds(pl.multiple_of(index * 8, 8), 8)
            margin = jnp.where(low, head_ref[at, :], tail_ref[at, :])
            x = forward_steps(spread_rows(stage_ref.at[2 * group], incr_ref[index], margin), coef_ref)
            ends = join_rows(stage_ref.at[2 * group + 1], x, rows)
            ends_ref[pl.ds(pl.multiple_of(index * rows, rows), rows), :] = ends.astype(BF16)
            put(index).start()
        return carry

    lax.fori_loop(0, half, at_level, 0)
    for index in range(levels):
        put(index).wait()


def backward_kernel(
    edge_ref, next_hbm, nhead_hbm, ntail_hbm, wind_hbm, head_hbm, tail_hbm, mult_hbm, incr_hbm,
    index_ref, dual_ref, variance_ref, cols_hbm, lines_hbm,
    state_hbm, obs_ref,
    next_ref, wind_ref, mult_ref, incr_ref, cols_ref, lines_ref, head_in, tail_in, nhead_in, ntail_in,
    head_ref, tail_ref, nhead_ref, ntail_ref, stage_ref, coef_ref, spread_ref, state_ref, sems, level_sems,
):
    levels, rows, width = mult_ref.shape
    half = levels // 2
    copies = Copies(sems)
    block_in = [copies.start(cols_hbm, cols_ref), copies.start(lines_hbm, lines_ref)]
    margin_in = [
        copies.start(source, target)
        for source, target in (
            (head_hbm, head_in), (tail_hbm, tail_in), (nhead_hbm, nhead_in), (ntail_hbm, ntail_in)
        )
    ]
    incr_in = [copies.start(incr_hbm.at[pl.ds(3 * i, 3)], incr_ref.at[pl.ds(3 * i, 3)]) for i in range(4)]
    fields_in = [
        copies.start(source.at[pl.ds(start, size)], target.at[pl.ds(start, size)])
        for source, target, size in ((wind_hbm, wind_ref, 6), (next_hbm, next_ref, 192), (mult_hbm, mult_ref, 6))
        for start in (0, size)
    ]
    for copy in block_in:
        copy.wait()
    cols, lines = cols_ref[...], lines_ref[...]
    blocks = (lines.shape[0], cols.shape[1])
    high, low_hot = one_hots(index_ref[...], blocks)
    weights = low_hot.astype(BF16)
    summed = sum(nt(p, weights) for p in parts(jnp.where(high, dual_ref[...], 0.0))) * 0.125
    tall = sum(tn(lines, p) for p in parts(summed))
    spread_ref[...] = sum(nt(p, cols) for p in parts(tall))
    for copy in incr_in:
        copy.wait()
    narrow = sum(nn(p, cols) for p in parts(incr_ref[...].reshape(levels * rows, width)))
    sums = sum(nn(lines, p) for p in parts(narrow))
    high = high.astype(BF16)
    picked = sum(tn(p, high) for p in parts(sums))
    observed = jnp.sum(jnp.where(low_hot, picked, 0.0), axis=0, keepdims=True) * 0.125
    obs_ref[...] = variance_ref[...] * dual_ref[...] + observed
    for copy in margin_in + fields_in:
        copy.wait()
    head_ref[...] = head_in[...].astype(F32)
    tail_ref[...] = tail_in[...].astype(F32)
    nhead_ref[...] = nhead_in[...].astype(F32)
    ntail_ref[...] = ntail_in[...].astype(F32)
    low = low_half((8, width))

    def put(index):
        return pltpu.make_async_copy(state_ref.at[index], state_hbm.at[index], level_sems.at[index])

    def at_level(level, carry):
        coefficients(level, levels, edge_ref, wind_ref, head_ref, tail_ref, stage_ref, coef_ref)
        at = pl.ds(pl.multiple_of(level * 8, 8), 8)
        head, tail = nhead_ref[at, :], ntail_ref[at, :]
        for group in range(2):
            index = level + group * half
            if group == 0:
                margin = jnp.where(low, head, tail)
            else:
                margin = pltpu.roll(jnp.where(low, tail, head), HALF, 0)
            part = pl.ds(pl.multiple_of(index * rows, rows), rows)
            y = backward_steps(spread_rows(stage_ref.at[2 * group], next_ref[part, :].astype(F32), margin), coef_ref)
            back = join_rows(stage_ref.at[2 * group + 1], y, rows)
            state_ref[index] = (mult_ref[index] - back) + spread_ref[part, :]
            put(index).start()
        return carry

    lax.fori_loop(0, half, at_level, 0)
    for index in range(levels):
        put(index).wait()


def gather_lines(came_in, came_ref, lines_ref):
    count, rows, wide = came_ref.shape
    groups, fields = count // 4, wide // 128
    source = lax.broadcasted_iota(jnp.int32, (512, 512), 0)
    target = lax.broadcasted_iota(jnp.int32, (512, 512), 1)
    swapped = ((target & 127) >> 5) * 128 + (target >> 7) * 32 + (target & 31)
    perm = (source == swapped).astype(BF16)
    for copy in came_in:
        copy.wait()
    for g in range(fields):
        piece = came_ref[:, :, g * 128 : (g + 1) * 128].reshape(groups, 4, rows, 128)
        left = jnp.concatenate([piece[:, i].reshape(groups * rows, 128) for i in range(4)], axis=1)
        moved = nn(left, perm).astype(BF16)
        for i in range(4):
            for b in range(groups):
                lines_ref[(4 * g + i) * rows : (4 * g + i + 1) * rows, b * 128 : (b + 1) * 128] = moved[
                    b * rows : (b + 1) * rows, i * 128 : (i + 1) * 128
                ]


def quarters(copies, source, target):
    size = target.shape[0] // 4
    return [copies.start(source.at[pl.ds(size * i, size)], target.at[pl.ds(size * i, size)]) for i in range(4)]


def quarter_columns(copies, source, target):
    size = target.shape[1] // 4
    return [copies.start(source.at[:, pl.ds(size * i, size)], target.at[:, pl.ds(size * i, size)]) for i in range(4)]


def latitude_kernel(
    came_hbm, var_hbm, turned_hbm, _head, _tail, out_hbm,
    came_ref, var_ref, turned_ref, lines_ref, scaled_ref, out_ref, sems,
):
    copies = Copies(sems)
    came_in = quarters(copies, came_hbm, came_ref)
    turned_in = quarter_columns(copies, turned_hbm, turned_ref)
    var_in = quarter_columns(copies, var_hbm, var_ref)
    gather_lines(came_in, came_ref, lines_ref)
    lines = lines_ref[...]
    for i in range(4):
        turned_in[i].wait()
        var_in[i].wait()
        part = pl.ds(256 * i, 256)
        scaled_ref[:, part] = (nn(lines, turned_ref[:, part]) * var_ref[:, part]).astype(BF16)
    scaled = scaled_ref[...]
    out = []
    for i in range(2):
        part = pl.ds(512 * i, 512)
        out_ref[part] = nt(turned_ref[part], scaled).astype(BF16)
        out.append(copies.start(out_ref.at[part], out_hbm.at[part]))
    for copy in out:
        copy.wait()


def finish_kernel(
    came_hbm, incr_hbm, prev_hbm, table_hbm, out_hbm,
    came_ref, incr_ref, prev_ref, table_ref, lines_ref, out_ref, sems,
):
    copies = Copies(sems)
    came_in = quarters(copies, came_hbm, came_ref)
    table_in = quarter_columns(copies, table_hbm, table_ref)
    incr_in = quarter_columns(copies, incr_hbm, incr_ref)
    prev_in = quarter_columns(copies, prev_hbm, prev_ref)
    gather_lines(came_in, came_ref, lines_ref)
    lines = lines_ref[...]
    out = []
    for i in range(4):
        table_in[i].wait()
        incr_in[i].wait()
        prev_in[i].wait()
        part = pl.ds(256 * i, 256)
        covar = nn(lines, table_ref[:, part])
        out_ref[:, part] = covar + (incr_ref[:, part] - prev_ref[:, part].astype(F32))
        out.append(copies.start(out_ref.at[:, part], out_hbm.at[:, part]))
    for copy in out:
        copy.wait()


VMEM = pl.BlockSpec(memory_space=pltpu.VMEM)
SMEM = pl.BlockSpec(memory_space=pltpu.SMEM)
HBM = pl.BlockSpec(memory_space=pl.ANY)


def call(kernel, outs, ins, scratch, name):
    def place(a):
        if len(a.shape) == 1:
            return SMEM
        return VMEM if a.shape[0] == 1 else HBM

    return pl.pallas_call(
        kernel,
        out_shape=outs,
        in_specs=[place(a) for a in ins],
        out_specs=jax.tree.map(place, outs),
        scratch_shapes=list(scratch),
        compiler_params=pltpu.CompilerParams(vmem_limit_bytes=56 * 1024 * 1024),
        name=name,
    )(*ins)


def local(increment, multiplier, obs_dual, obs_index, obs_variance, winds, spectral_var):
    rows, levels, width = increment.shape[1:]
    count = lax.axis_size("space")
    times = lax.axis_size("tm")
    lat = rows * count
    waves = width // count
    full = levels * rows
    incr = jnp.transpose(increment[0], (1, 0, 2))
    mult = jnp.transpose(multiplier[0], (1, 0, 2))
    wind = jnp.transpose(winds[0], (1, 0, 2))
    var = jnp.transpose(spectral_var, (1, 2, 0)).reshape(full, lat)
    table = cosine_table(width)
    turned = np.ascontiguousarray(table.T)
    cols, lines = block_sums(levels, rows, width)
    place = lax.axis_index("space")
    edge = jnp.stack([place == 0, place == count - 1]).astype(jnp.int32)

    def shape(*dims):
        return jax.ShapeDtypeStruct(dims, BF16)

    def wide(*dims):
        return pltpu.VMEM(dims, F32)

    def short(*dims):
        return pltpu.VMEM(dims, BF16)

    def sems(*dims):
        return pltpu.SemaphoreType.DMA(dims)

    field = (levels, rows, width)
    flat, spec, mult_head, mult_tail, head, tail = call(
        start_kernel,
        (
            shape(full, width), shape(width, full), shape(levels * 4, width), shape(levels * 4, width),
            shape(levels * 8, width), shape(levels * 8, width),
        ),
        (mult, table, incr, wind),
        [
            wide(*field), short(width, width), wide(4, levels, 8, width), short(full, width), short(width, full),
            short(levels * 4, width), short(levels * 4, width), short(levels * 8, width), short(levels * 8, width),
            sems(24),
        ],
        "start",
    )
    came = lax.all_to_all(spec.reshape(count, waves, full), "space", 0, 0, tiled=True)
    ring = range(count - 1)
    down = [(i + 1, i) for i in ring]
    up = [(i, i + 1) for i in ring]
    head = lax.ppermute(head, "space", down)
    tail = lax.ppermute(tail, "space", up)
    both = ("tm", "space")
    mult_head = lax.ppermute(
        mult_head, both, [((t + 1) * count + a, t * count + b) for t in range(times - 1) for a, b in down]
    )
    mult_tail = lax.ppermute(
        mult_tail, both, [((t + 1) * count + a, t * count + b) for t in range(times - 1) for a, b in up]
    )
    coming = lax.ppermute(flat, "tm", [(t + 1, t) for t in range(times - 1)])

    across = width // 128
    stages = [wide(4, across, rows + 8, 128), wide(4, across, TILES, 8, 128)]
    ends = call(
        forward_kernel,
        shape(full, width),
        (edge, incr, wind, head, tail),
        [
            wide(*field), wide(*field), short(levels * 8, width), short(levels * 8, width),
            wide(levels * 8, width), wide(levels * 8, width), *stages, short(full, width), sems(2), sems(3, levels),
        ],
        "forward",
    )
    previous = lax.ppermute(ends, "tm", [(t, t + 1) for t in range(times - 1)])

    back = call(
        latitude_kernel,
        shape(lat, full),
        (came, var, turned, mult_head, mult_tail),
        [
            short(count, waves, full), wide(full, lat), short(lat, lat), short(full, lat), short(full, lat),
            short(lat, full), sems(16),
        ],
        "latitude",
    )
    returned = lax.all_to_all(back.reshape(count, rows, full), "space", 0, 0, tiled=True)

    state_rows, obs_rows = call(
        backward_kernel,
        (jax.ShapeDtypeStruct(field, F32), jax.ShapeDtypeStruct(obs_dual.shape, F32)),
        (
            edge, coming, mult_head, mult_tail, wind, head, tail, mult, incr, obs_index, obs_dual, obs_variance,
            cols, lines,
        ),
        [
            short(full, width), wide(*field), wide(*field), wide(*field), short(*cols.shape), short(*lines.shape),
            short(levels * 8, width), short(levels * 8, width), short(levels * 4, width), short(levels * 4, width),
            wide(levels * 8, width), wide(levels * 8, width), wide(levels * 4, width), wide(levels * 4, width),
            *stages, wide(full, width), wide(*field), sems(16), sems(levels),
        ],
        "backward",
    )
    model_rows = call(
        finish_kernel,
        jax.ShapeDtypeStruct((full, width), F32),
        (returned, incr.reshape(full, width), previous, table),
        [
            short(count, rows, full), wide(full, width), short(full, width), short(width, width),
            short(full, width), wide(full, width), sems(20),
        ],
        "finish",
    )

    def placed(whole):
        return jnp.transpose(whole.reshape(field), (1, 0, 2))[None]

    return (placed(model_rows), obs_rows, placed(state_rows))


def solution(mesh):
    specs = (
        P("tm", "space", None, None),
        P("tm", "space", None, None),
        P("tm", "space"),
        P("tm", "space"),
        P("tm", "space"),
        P("tm", "space", None, None),
        P(None, None, "space"),
    )
    return jax.shard_map(
        local,
        mesh=mesh,
        in_specs=specs,
        out_specs=(P("tm", "space", None, None), P("tm", "space"), P("tm", "space", None, None)),
        check_vma=False,
    )
```

time: 91.6 us -> 80.7 us (0.88)
  the two profiles are of different devices: /device:TPU:98 before, /device:TPU:193 now
where the time goes in v1:
time: 80.7 us; the launch traced here: 80.2 us
  Pallas kernels  36.6 us (45%)
  starting transfers between devices  36.3 us (45%)
  local copies, waits for them, and re-layouts  4.06 us (5%)
  waiting for transfers between devices  1.5 us (2%)
  between operations  1.04 us (1%)
    pallas_call x5, Pallas kernels, call(): pl.pallas_call(kernel, out_shape=outs, in_specs=[place(a) for a in ins],...  36.6 us
    all_to_all x1, starting transfers between devices, local(): lax.all_to_all(back.reshape(count, rows, full), 'space', 0, 0, tiled=True)  11.1 us
    all_to_all x1, starting transfers between devices, local(): lax.all_to_all(spec.reshape(count, waves, full), 'space', 0, 0, tiled=True)  7.91 us
    ppermute x1, starting transfers between devices, local(): lax.ppermute(mult_tail, both, [((t + 1) * count + a, t * count + b) for t...  4.53 us
    unnamed x24, local copies, waits for them, and re-layouts  4.06 us
    ppermute x1, starting transfers between devices, local(): tail = lax.ppermute(tail, 'space', up)  3.42 us
    ppermute x1, starting transfers between devices, local(): previous = lax.ppermute(ends, 'tm', [(t, t + 1) for t in range(times - 1)])  3.41 us
    ppermute x1, starting transfers between devices, local(): head = lax.ppermute(head, 'space', down)  2.14 us
  transfers between devices with their start and end apart: 8, of which 1 were waited for; matrix products, arithmetic and copies ran while one was open for 1% of the time, Pallas kernels for 33%

profile of v1, /device:TPU:193, one launch (start us, length us, event | category | flops | bytes accessed | tf_op | source)
XLA Modules:
  0.0 80.2 jit_solution(7814795726152982757)
XLA Ops:
  0.6 4.4 %start.1 = (bf16[384,1024]{1,0:T(8,128)(2,1)}, bf16[1024,384]{1,0:T(8,128)(2,1)}, bf16[48,1024]{1,0:T(8,128)(2,1)}, bf16[48,1024]{1,0:T(8,128)(2,1)}, bf16[96,10...) custom-call(f32[12,32,1024]{2,1,0:T(8,128)} %bitcast.33, bf16[1024,1024]{1,0:T(8,128)(2,1)} %constant.16.clone.table_hbm, ...), custom_call_target="tpu_custom_call" | custom-call | tf_op jit(solution)/shard_map/start/pallas_call | solution.py:437
  5.1 7.9 %all-to-all-start = ((bf16[32,32,384]{2,1,0:T(8,128)(2,1)}), bf16[32,32,384]{2,1,0:T(8,128)(2,1)S(1)}, u32[]{:S(2)}, u32[]{:S(2)}) async-start(bf16[32,32,384]{2,1,0:T(8,128)(2,1)} %bitcast.38), calls=%async_computation | async-start | bytes 1572864 | tf_op jit(solution)/shard_map/all_to_all | solution.py:492
  13.0 2.1 %collective-permute-start.2 = (bf16[96,1024]{1,0:T(8,128)(2,1)S(1)}, bf16[96,1024]{1,0:T(8,128)(2,1)S(1)}, u32[]{:S(2)}, u32[]{:S(2)}) collective-permute-start(bf16[96,1024]{1,0:T(8,128)(2,1)S(1)} %copy-done.9), channel_id=1, source_target_pairs={{1,0},{2,1},{3,2},{4,3},{5,4},{6,5},{7,6},{8,7},{9,8},{10,9},{11,1... | collective-permute-start | bytes 589832 | tf_op jit(solution)/shard_map/ppermute | solution.py:496
  15.2 3.4 %collective-permute-start.3 = (bf16[96,1024]{1,0:T(8,128)(2,1)S(1)}, bf16[96,1024]{1,0:T(8,128)(2,1)S(1)}, u32[]{:S(2)}, u32[]{:S(2)}) collective-permute-start(bf16[96,1024]{1,0:T(8,128)(2,1)S(1)} %copy-done.8), channel_id=1, source_target_pairs={{0,1},{1,2},{2,3},{3,4},{4,5},{5,6},{6,7},{7,8},{8,9},{9,10},{10,1... | collective-permute-start | bytes 589832 | tf_op jit(solution)/shard_map/ppermute | solution.py:497
  18.6 1.9 %collective-permute-start = (bf16[48,1024]{1,0:T(8,128)(2,1)S(1)}, bf16[48,1024]{1,0:T(8,128)(2,1)S(1)}, u32[]{:S(2)}, u32[]{:S(2)}) collective-permute-start(bf16[48,1024]{1,0:T(8,128)(2,1)S(1)} %copy-done.11), channel_id=1, source_target_pairs={{33,0},{34,1},{35,2},{36,3},{37,4},{38,5},{39,6},{40,7},{41,8},{42... | collective-permute-start | bytes 294920 | tf_op jit(solution)/shard_map/ppermute | solution.py:499
  20.5 4.5 %collective-permute-start.1 = (bf16[48,1024]{1,0:T(8,128)(2,1)S(1)}, bf16[48,1024]{1,0:T(8,128)(2,1)S(1)}, u32[]{:S(2)}, u32[]{:S(2)}) collective-permute-start(bf16[48,1024]{1,0:T(8,128)(2,1)S(1)} %copy-done.10), channel_id=1, source_target_pairs={{32,1},{33,2},{34,3},{35,4},{36,5},{37,6},{38,7},{39,8},{40,9},{41... | collective-permute-start | bytes 294920 | tf_op jit(solution)/shard_map/ppermute | solution.py:502
  25.1 1.9 %collective-permute-start.5 = (bf16[384,1024]{1,0:T(8,128)(2,1)}, bf16[384,1024]{1,0:T(8,128)(2,1)S(1)}, u32[]{:S(2)}, u32[]{:S(2)}) collective-permute-start(bf16[384,1024]{1,0:T(8,128)(2,1)} %get-tuple-element.16), channel_id=1, source_target_pairs={{32,0},{64,32},{96,64},{128,96},{160,128},{192,160},{224,192},{33,... | collective-permute-start | bytes 2359304 | tf_op jit(solution)/shard_map/ppermute | solution.py:505
  27.0 0.6 add_convert_fusion.edge_ref
  27.6 0.7 copy-done.2
  28.3 0.7 copy-done.3
  29.0 8.6 %forward.1 = bf16[384,1024]{1,0:T(8,128)(2,1)} custom-call(s32[2]{0:T(128)} %add_convert_fusion.edge_ref, f32[12,32,1024]{2,1,0:T(8,128)} %bitcast.27, f32[12,32,1024]{2,1,0:T(8,128)} %bitcast.31, bf16[96,1024]{1,0:T(8,128)(2,1)} %copy-done.2, bf16[96,1024]{1,0:T(8,128)(2,1)} %copy-done.3), custom_call_target="tpu_custom_call" | custom-call | tf_op jit(solution)/shard_map/forward/pallas_call | solution.py:437
  37.6 3.4 %collective-permute-start.4 = (bf16[384,1024]{1,0:T(8,128)(2,1)}, bf16[384,1024]{1,0:T(8,128)(2,1)S(1)}, u32[]{:S(2)}, u32[]{:S(2)}) collective-permute-start(bf16[384,1024]{1,0:T(8,128)(2,1)} %forward.1), channel_id=1, source_target_pairs={{0,32},{32,64},{64,96},{96,128},{128,160},{160,192},{192,224},{1,3... | collective-permute-start | bytes 2359304 | tf_op jit(solution)/shard_map/ppermute | solution.py:519
  41.1 0.0 copy-start
  41.1 0.6 copy-done.6
  41.6 0.0 copy-done.7
  41.7 0.3 copy-done
  42.0 6.2 %latitude.1 = bf16[1024,384]{1,0:T(8,128)(2,1)} custom-call(bf16[32,32,384]{2,1,0:T(8,128)(2,1)} %copy-done, f32[384,1024]{1,0:T(8,128)} %bitcast.36, bf16[1024,1024]{1,0:T(8,128)(2,1)} %constant.17.clone.turned_hbm, bf16[48,1024]{1,0:T(8,128)(2,1)} %copy-done.6, bf16[48,1024]{1,0:T(8,128)(2,1)} %copy-done.7), custom_call_target="tpu_custom_call" | custom-call | tf_op jit(solution)/shard_map/latitude/pallas_call | solution.py:437
  48.2 11.1 %all-to-all-start.1 = ((bf16[32,32,384]{2,1,0:T(8,128)(2,1)}), bf16[32,32,384]{2,1,0:T(8,128)(2,1)S(1)}, u32[]{:S(2)}, u32[]{:S(2)}) async-start(bf16[32,32,384]{2,1,0:T(8,128)(2,1)} %bitcast.35), calls=%async_computation.1 | async-start | bytes 1572864 | tf_op jit(solution)/shard_map/all_to_all | solution.py:531
  59.3 0.0 copy-start.4
  59.3 0.9 %copy-done.4 = bf16[384,1024]{1,0:T(8,128)(2,1)} copy-done((bf16[384,1024]{1,0:T(8,128)(2,1)}, bf16[384,1024]{1,0:T(8,128)(2,1)S(1)}, u32[]{:S(2)}) %copy-start.4) | copy-done | bytes 786456
  60.2 11.8 %backward.1 = (f32[12,32,1024]{2,1,0:T(8,128)}, f32[1,512]{1,0:T(1,128)}) custom-call(s32[2]{0:T(128)} %add_convert_fusion.edge_ref, bf16[384,1024]{1,0:T(8,128)(2,1)} %copy-done.4, bf16[48,1024]{1,0:T(8,128)(2,1)} %copy-done.6, bf16[48,1024]{1,0:T(8,128)(2,1)} %copy-done.7, f32[12,32,1024]{2,1,0:T(8,128)} %bitcast.32, bf16[96,1024]{1,0:T(8,128)(2,1)} %copy-done.2, ...), custom_call_target="tpu_custom_call" | custom-call | tf_op jit(solution)/shard_map/backward/pallas_call | solution.py:437
  72.0 1.5 %all-to-all-done.1.came_hbm = bf16[32,32,384]{2,1,0:T(8,128)(2,1)S(1)} async-done(((bf16[32,32,384]{2,1,0:T(8,128)(2,1)}), bf16[32,32,384]{2,1,0:T(8,128)(2,1)S(1)}, u32[]{:S(2)}, u32[]{:S(2)}) %all-to-all-start.1) | async-done | bytes 786464 | tf_op jit(solution)/shard_map/all_to_all | solution.py:531
  73.5 0.9 %copy-done.1 = bf16[32,32,384]{2,1,0:T(8,128)(2,1)} copy-done((bf16[32,32,384]{2,1,0:T(8,128)(2,1)}, bf16[32,32,384]{2,1,0:T(8,128)(2,1)S(1)}, u32[]{:S(2)}) %copy-start.1) | copy-done | bytes 786456
  74.4 5.6 %finish.1 = f32[384,1024]{1,0:T(8,128)} custom-call(bf16[32,32,384]{2,1,0:T(8,128)(2,1)} %copy-done.1, f32[384,1024]{1,0:T(8,128)} %bitcast.29, bf16[384,1024]{1,0:T(8,128)(2,1)} %copy-done.5, bf16[1024,1024]{1,0:T(8,128)(2,1)} %constant.16.clone.table_hbm), custom_call_target="tpu_custom_call" | custom-call | tf_op jit(solution)/shard_map/finish/pallas_call | solution.py:437
  (22 shorter events, 0.0 us)
Async XLA Ops:
  5.0 8.0 %copy-start.9 = (bf16[96,1024]{1,0:T(8,128)(2,1)S(1)}, bf16[96,1024]{1,0:T(8,128)(2,1)}, u32[]{:S(2)}) copy-start(bf16[96,1024]{1,0:T(8,128)(2,1)} %get-tuple-element.14) | copy-start | bytes 589828
  5.0 10.1 %copy-start.8 = (bf16[96,1024]{1,0:T(8,128)(2,1)S(1)}, bf16[96,1024]{1,0:T(8,128)(2,1)}, u32[]{:S(2)}) copy-start(bf16[96,1024]{1,0:T(8,128)(2,1)} %get-tuple-element.15) | copy-start | bytes 589828
  5.1 13.5 %copy-start.11 = (bf16[48,1024]{1,0:T(8,128)(2,1)S(1)}, bf16[48,1024]{1,0:T(8,128)(2,1)}, u32[]{:S(2)}) copy-start(bf16[48,1024]{1,0:T(8,128)(2,1)} %get-tuple-element.12) | copy-start | bytes 294916
  5.1 15.5 %copy-start.10 = (bf16[48,1024]{1,0:T(8,128)(2,1)S(1)}, bf16[48,1024]{1,0:T(8,128)(2,1)}, u32[]{:S(2)}) copy-start(bf16[48,1024]{1,0:T(8,128)(2,1)} %get-tuple-element.13) | copy-start | bytes 294916
  5.1 36.0 %all-to-all-start = ((bf16[32,32,384]{2,1,0:T(8,128)(2,1)}), bf16[32,32,384]{2,1,0:T(8,128)(2,1)S(1)}, u32[]{:S(2)}, u32[]{:S(2)}) async-start(bf16[32,32,384]{2,1,0:T(8,128)(2,1)} %bitcast.38), calls=%async_computation | async-start | bytes 1572864 | tf_op jit(solution)/shard_map/all_to_all | solution.py:492
  13.0 14.6 %collective-permute-start.2 = (bf16[96,1024]{1,0:T(8,128)(2,1)S(1)}, bf16[96,1024]{1,0:T(8,128)(2,1)S(1)}, u32[]{:S(2)}, u32[]{:S(2)}) collective-permute-start(bf16[96,1024]{1,0:T(8,128)(2,1)S(1)} %copy-done.9), channel_id=1, source_target_pairs={{1,0},{2,1},{3,2},{4,3},{5,4},{6,5},{7,6},{8,7},{9,8},{10,9},{11,1... | collective-permute-start | bytes 589832 | tf_op jit(solution)/shard_map/ppermute | solution.py:496
  15.2 12.5 %collective-permute-start.3 = (bf16[96,1024]{1,0:T(8,128)(2,1)S(1)}, bf16[96,1024]{1,0:T(8,128)(2,1)S(1)}, u32[]{:S(2)}, u32[]{:S(2)}) collective-permute-start(bf16[96,1024]{1,0:T(8,128)(2,1)S(1)} %copy-done.8), channel_id=1, source_target_pairs={{0,1},{1,2},{2,3},{3,4},{4,5},{5,6},{6,7},{7,8},{8,9},{9,10},{10,1... | collective-permute-start | bytes 589832 | tf_op jit(solution)/shard_map/ppermute | solution.py:497
  18.6 22.4 %collective-permute-start = (bf16[48,1024]{1,0:T(8,128)(2,1)S(1)}, bf16[48,1024]{1,0:T(8,128)(2,1)S(1)}, u32[]{:S(2)}, u32[]{:S(2)}) collective-permute-start(bf16[48,1024]{1,0:T(8,128)(2,1)S(1)} %copy-done.11), channel_id=1, source_target_pairs={{33,0},{34,1},{35,2},{36,3},{37,4},{38,5},{39,6},{40,7},{41,8},{42... | collective-permute-start | bytes 294920 | tf_op jit(solution)/shard_map/ppermute | solution.py:499
  20.5 20.5 %collective-permute-start.1 = (bf16[48,1024]{1,0:T(8,128)(2,1)S(1)}, bf16[48,1024]{1,0:T(8,128)(2,1)S(1)}, u32[]{:S(2)}, u32[]{:S(2)}) collective-permute-start(bf16[48,1024]{1,0:T(8,128)(2,1)S(1)} %copy-done.10), channel_id=1, source_target_pairs={{32,1},{33,2},{34,3},{35,4},{36,5},{37,6},{38,7},{39,8},{40,9},{41... | collective-permute-start | bytes 294920 | tf_op jit(solution)/shard_map/ppermute | solution.py:502
  25.1 34.2 %collective-permute-start.5 = (bf16[384,1024]{1,0:T(8,128)(2,1)}, bf16[384,1024]{1,0:T(8,128)(2,1)S(1)}, u32[]{:S(2)}, u32[]{:S(2)}) collective-permute-start(bf16[384,1024]{1,0:T(8,128)(2,1)} %get-tuple-element.16), channel_id=1, source_target_pairs={{32,0},{64,32},{96,64},{128,96},{160,128},{192,160},{224,192},{33,... | collective-permute-start | bytes 2359304 | tf_op jit(solution)/shard_map/ppermute | solution.py:505
  27.6 0.7 copy-start.2
  28.3 0.7 copy-start.3
  37.6 34.4 %collective-permute-start.4 = (bf16[384,1024]{1,0:T(8,128)(2,1)}, bf16[384,1024]{1,0:T(8,128)(2,1)S(1)}, u32[]{:S(2)}, u32[]{:S(2)}) collective-permute-start(bf16[384,1024]{1,0:T(8,128)(2,1)} %forward.1), channel_id=1, source_target_pairs={{0,32},{32,64},{64,96},{96,128},{128,160},{160,192},{192,224},{1,3... | collective-permute-start | bytes 2359304 | tf_op jit(solution)/shard_map/ppermute | solution.py:519
  41.0 0.6 copy-start.6
  41.0 0.6 copy-start.7
  41.1 0.9 %copy-start = (bf16[32,32,384]{2,1,0:T(8,128)(2,1)}, bf16[32,32,384]{2,1,0:T(8,128)(2,1)S(1)}, u32[]{:S(2)}) copy-start(bf16[32,32,384]{2,1,0:T(8,128)(2,1)S(1)} %all-to-all-done.came_hbm) | copy-start | bytes 2359300
  48.2 25.3 %all-to-all-start.1 = ((bf16[32,32,384]{2,1,0:T(8,128)(2,1)}), bf16[32,32,384]{2,1,0:T(8,128)(2,1)S(1)}, u32[]{:S(2)}, u32[]{:S(2)}) async-start(bf16[32,32,384]{2,1,0:T(8,128)(2,1)} %bitcast.35), calls=%async_computation.1 | async-start | bytes 1572864 | tf_op jit(solution)/shard_map/all_to_all | solution.py:531
  59.3 0.9 %copy-start.4 = (bf16[384,1024]{1,0:T(8,128)(2,1)}, bf16[384,1024]{1,0:T(8,128)(2,1)S(1)}, u32[]{:S(2)}) copy-start(bf16[384,1024]{1,0:T(8,128)(2,1)S(1)} %collective-permute-done.5.next_hbm) | copy-start | bytes 2359300
  72.0 1.5 %copy-start.5 = (bf16[384,1024]{1,0:T(8,128)(2,1)}, bf16[384,1024]{1,0:T(8,128)(2,1)S(1)}, u32[]{:S(2)}) copy-start(bf16[384,1024]{1,0:T(8,128)(2,1)S(1)} %collective-permute-done.4.prev_hbm) | copy-start | bytes 2359300
  73.5 0.9 %copy-start.1 = (bf16[32,32,384]{2,1,0:T(8,128)(2,1)}, bf16[32,32,384]{2,1,0:T(8,128)(2,1)S(1)}, u32[]{:S(2)}) copy-start(bf16[32,32,384]{2,1,0:T(8,128)(2,1)S(1)} %all-to-all-done.1.came_hbm) | copy-start | bytes 2359300

commit v2 on v1

--- a/solution.py
+++ b/solution.py
@@ -46,10 +46,7 @@
 
 def parts(a):
     first = a.astype(BF16)
-    rest = a - first.astype(F32)
-    second = rest.astype(BF16)
-    third = (rest - second.astype(F32)).astype(BF16)
-    return first, second, third
+    return first, (a - first.astype(F32)).astype(BF16)
 
 
 def low_half(shape):
@@ -70,16 +67,14 @@
 
 def start_kernel(
     mult_hbm, table_hbm, incr_hbm, wind_hbm,
-    flat_hbm, spec_hbm, mhead_hbm, mtail_hbm, head_hbm, tail_hbm,
-    mult_ref, table_ref, edge_ref, flat_ref, spec_ref, mhead_ref, mtail_ref, head_ref, tail_ref, sems,
+    whole_hbm, spec_hbm, head_hbm, tail_hbm,
+    mult_ref, table_ref, edge_ref, flat_ref, spec_ref, head_ref, tail_ref, sems,
 ):
     levels, rows, width = mult_ref.shape
     half = levels // 2
     copies = Copies(sems)
-    mult_in = [copies.start(mult_hbm.at[pl.ds(3 * i, 3)], mult_ref.at[pl.ds(3 * i, 3)]) for i in range(4)]
-    table_in = [
-        copies.start(table_hbm.at[pl.ds(256 * i, 256)], table_ref.at[pl.ds(256 * i, 256)]) for i in range(4)
-    ]
+    mult_in = copies.start(mult_hbm, mult_ref)
+    table_in = copies.start(table_hbm, table_ref)
     edge_in = [
         copies.start(source.at[:, pl.ds(at, 8), :], edge_ref.at[i])
         for i, (source, at) in enumerate(
@@ -87,23 +82,20 @@
         )
     ]
     out = []
-    for copy in mult_in:
-        copy.wait()
+    mult_in.wait()
     flat_ref[...] = mult_ref[...].reshape(levels * rows, width).astype(BF16)
-    out.append(copies.start(flat_ref, flat_hbm))
+    out.append(copies.start(flat_ref, whole_hbm.at[pl.ds(0, levels * rows)]))
     first = mult_ref[:, :8, :]
     last = mult_ref[:, rows - 8 :, :]
     low = low_half((half, 8, width))
     head = jnp.where(low, first[:half], pltpu.roll(first[half:], HALF, 1))
     tail = jnp.where(low, pltpu.roll(last[half:], HALF, 1), last[:half])
-    mhead_ref[...] = head.reshape(half * 8, width).astype(BF16)
-    mtail_ref[...] = tail.reshape(half * 8, width).astype(BF16)
-    out.append(copies.start(mhead_ref, mhead_hbm))
-    out.append(copies.start(mtail_ref, mtail_hbm))
+    head_ref[levels * 8 :] = head.reshape(half * 8, width).astype(BF16)
+    tail_ref[levels * 8 :] = tail.reshape(half * 8, width).astype(BF16)
     flat = flat_ref[...]
-    for i, copy in enumerate(table_in):
-        copy.wait()
-        part = pl.ds(256 * i, 256)
+    table_in.wait()
+    for i in range(2):
+        part = pl.ds(512 * i, 512)
         spec_ref[part] = nt(table_ref[part], flat).astype(BF16)
         out.append(copies.start(spec_ref.at[part], spec_hbm.at[part]))
     for copy in edge_in:
@@ -111,8 +103,8 @@
     low = low_half((levels, 8, width))
     head = jnp.where(low, edge_ref[0], pltpu.roll(edge_ref[1], HALF, 1))
     tail = jnp.where(low, pltpu.roll(edge_ref[3], HALF, 1), edge_ref[2])
-    head_ref[...] = head.reshape(levels * 8, width).astype(BF16)
-    tail_ref[...] = tail.reshape(levels * 8, width).astype(BF16)
+    head_ref[: levels * 8] = head.reshape(levels * 8, width).astype(BF16)
+    tail_ref[: levels * 8] = tail.reshape(levels * 8, width).astype(BF16)
     out.append(copies.start(head_ref, head_hbm))
     out.append(copies.start(tail_ref, tail_hbm))
     for copy in out:
@@ -138,7 +130,7 @@
     return jnp.concatenate([stage_ref[c, :rows, :] for c in range(len(tiles))], axis=1)
 
 
-def coefficients(level, levels, edge_ref, wind_ref, head_ref, tail_ref, stage_ref, coef_ref):
+def coefficients(level, levels, wind_ref, head_ref, tail_ref, stage_ref, coef_ref):
     rows = wind_ref.shape[1]
     low = low_half((8, wind_ref.shape[2]))
     sublane = lax.broadcasted_iota(jnp.int32, (8, 128), 0)
@@ -150,8 +142,9 @@
 
     u = extended(level, stage_ref.at[0])
     v = extended(level + levels // 2, stage_ref.at[1])
-    first = (sublane == 0) & (edge_ref[0] != 0)
-    last = (sublane == (rows - 1) // TILES) & (edge_ref[1] != 0)
+    place = lax.axis_index("space")
+    first = (sublane == 0) & (place == 0)
+    last = (sublane == (rows - 1) // TILES) & (place == lax.axis_size("space") - 1)
     for c in range(len(u)):
         for t in range(TILES):
             north, south = 1.0 - v[c][t], 1.0 + v[c][t]
@@ -225,13 +218,15 @@
 
 
 def forward_kernel(
-    edge_ref, incr_hbm, wind_hbm, head_hbm, tail_hbm, ends_hbm,
-    incr_ref, wind_ref, head_in, tail_in, head_ref, tail_ref, stage_ref, coef_ref, ends_ref, sems, level_sems,
+    incr_hbm, wind_hbm, head_hbm, tail_hbm, _whole_in, ends_hbm, whole_hbm,
+    incr_ref, wind_ref, head_in, tail_in, far_ref, head_ref, tail_ref, stage_ref, coef_ref, ends_ref, sems, level_sems,
 ):
     levels, rows, width = incr_ref.shape
     half = levels // 2
     copies = Copies(sems)
-    margin_in = [copies.start(head_hbm, head_in), copies.start(tail_hbm, tail_in)]
+    full = levels * rows
+    near, far = pl.ds(0, levels * 8), pl.ds(levels * 8, levels * 4)
+    margin_in = [copies.start(head_hbm.at[near], head_in), copies.start(tail_hbm.at[near], tail_in)]
 
     def fetch(kind, index):
         source, target = ((wind_hbm, wind_ref), (incr_hbm, incr_ref))[kind]
@@ -245,6 +240,10 @@
         for index in (level, level + half):
             for kind in range(2):
                 fetch(kind, index).start()
+    far_in = [
+        copies.start(head_hbm.at[far], far_ref.at[pl.ds(0, levels * 4)]),
+        copies.start(tail_hbm.at[far], far_ref.at[pl.ds(levels * 4, levels * 4)]),
+    ]
     for copy in margin_in:
         copy.wait()
     head_ref[...] = head_in[...].astype(F32)
@@ -255,7 +254,7 @@
         for index in (level, level + half):
             for kind in range(2):
                 fetch(kind, index).wait()
-        coefficients(level, levels, edge_ref, wind_ref, head_ref, tail_ref, stage_ref, coef_ref)
+        coefficients(level, levels, wind_ref, head_ref, tail_ref, stage_ref, coef_ref)
         for group in range(2):
             index = level + group * half
             at = pl.ds(pl.multiple_of(index * 8, 8), 8)
@@ -266,13 +265,17 @@
             put(index).start()
         return carry
 
+    for copy in far_in:
+        copy.wait()
+    joined = copies.start(far_ref, whole_hbm.at[pl.ds(full, levels * 8)])
     lax.fori_loop(0, half, at_level, 0)
+    joined.wait()
     for index in range(levels):
         put(index).wait()
 
 
 def backward_kernel(
-    edge_ref, next_hbm, nhead_hbm, ntail_hbm, wind_hbm, head_hbm, tail_hbm, mult_hbm, incr_hbm,
+    whole_hbm, wind_hbm, head_hbm, tail_hbm, mult_hbm, incr_hbm,
     index_ref, dual_ref, variance_ref, cols_hbm, lines_hbm,
     state_hbm, obs_ref,
     next_ref, wind_ref, mult_ref, incr_ref, cols_ref, lines_ref, head_in, tail_in, nhead_in, ntail_in,
@@ -282,17 +285,19 @@
     half = levels // 2
     copies = Copies(sems)
     block_in = [copies.start(cols_hbm, cols_ref), copies.start(lines_hbm, lines_ref)]
+    full = levels * rows
+    near, next_head, next_tail = pl.ds(0, levels * 8), pl.ds(full, levels * 4), pl.ds(full + levels * 4, levels * 4)
     margin_in = [
         copies.start(source, target)
         for source, target in (
-            (head_hbm, head_in), (tail_hbm, tail_in), (nhead_hbm, nhead_in), (ntail_hbm, ntail_in)
+            (head_hbm.at[near], head_in), (tail_hbm.at[near], tail_in),
+            (whole_hbm.at[next_head], nhead_in), (whole_hbm.at[next_tail], ntail_in),
         )
     ]
-    incr_in = [copies.start(incr_hbm.at[pl.ds(3 * i, 3)], incr_ref.at[pl.ds(3 * i, 3)]) for i in range(4)]
+    incr_in = copies.start(incr_hbm, incr_ref)
     fields_in = [
-        copies.start(source.at[pl.ds(start, size)], target.at[pl.ds(start, size)])
-        for source, target, size in ((wind_hbm, wind_ref, 6), (next_hbm, next_ref, 192), (mult_hbm, mult_ref, 6))
-        for start in (0, size)
+        copies.start(source, target)
+        for source, target in ((wind_hbm, wind_ref), (whole_hbm.at[pl.ds(0, full)], next_ref), (mult_hbm, mult_ref))
     ]
     for copy in block_in:
         copy.wait()
@@ -303,8 +308,7 @@
     summed = sum(nt(p, weights) for p in parts(jnp.where(high, dual_ref[...], 0.0))) * 0.125
     tall = sum(tn(lines, p) for p in parts(summed))
     spread_ref[...] = sum(nt(p, cols) for p in parts(tall))
-    for copy in incr_in:
-        copy.wait()
+    incr_in.wait()
     narrow = sum(nn(p, cols) for p in parts(incr_ref[...].reshape(levels * rows, width)))
     sums = sum(nn(lines, p) for p in parts(narrow))
     high = high.astype(BF16)
@@ -323,7 +327,7 @@
         return pltpu.make_async_copy(state_ref.at[index], state_hbm.at[index], level_sems.at[index])
 
     def at_level(level, carry):
-        coefficients(level, levels, edge_ref, wind_ref, head_ref, tail_ref, stage_ref, coef_ref)
+        coefficients(level, levels, wind_ref, head_ref, tail_ref, stage_ref, coef_ref)
         at = pl.ds(pl.multiple_of(level * 8, 8), 8)
         head, tail = nhead_ref[at, :], ntail_ref[at, :]
         for group in range(2):
@@ -351,8 +355,7 @@
     target = lax.broadcasted_iota(jnp.int32, (512, 512), 1)
     swapped = ((target & 127) >> 5) * 128 + (target >> 7) * 32 + (target & 31)
     perm = (source == swapped).astype(BF16)
-    for copy in came_in:
-        copy.wait()
+    came_in.wait()
     for g in range(fields):
         piece = came_ref[:, :, g * 128 : (g + 1) * 128].reshape(groups, 4, rows, 128)
         left = jnp.concatenate([piece[:, i].reshape(groups * rows, 128) for i in range(4)], axis=1)
@@ -364,31 +367,19 @@
                 ]
 
 
-def quarters(copies, source, target):
-    size = target.shape[0] // 4
-    return [copies.start(source.at[pl.ds(size * i, size)], target.at[pl.ds(size * i, size)]) for i in range(4)]
-
-
-def quarter_columns(copies, source, target):
-    size = target.shape[1] // 4
-    return [copies.start(source.at[:, pl.ds(size * i, size)], target.at[:, pl.ds(size * i, size)]) for i in range(4)]
-
-
 def latitude_kernel(
-    came_hbm, var_hbm, turned_hbm, _head, _tail, out_hbm,
+    came_hbm, var_hbm, turned_hbm, out_hbm,
     came_ref, var_ref, turned_ref, lines_ref, scaled_ref, out_ref, sems,
 ):
     copies = Copies(sems)
-    came_in = quarters(copies, came_hbm, came_ref)
-    turned_in = quarter_columns(copies, turned_hbm, turned_ref)
-    var_in = quarter_columns(copies, var_hbm, var_ref)
+    came_in = copies.start(came_hbm, came_ref)
+    turned_in = copies.start(turned_hbm, turned_ref)
+    var_in = copies.start(var_hbm, var_ref)
     gather_lines(came_in, came_ref, lines_ref)
-    lines = lines_ref[...]
-    for i in range(4):
-        turned_in[i].wait()
-        var_in[i].wait()
-        part = pl.ds(256 * i, 256)
-        scaled_ref[:, part] = (nn(lines, turned_ref[:, part]) * var_ref[:, part]).astype(BF16)
+    turned_in.wait()
+    latitude = nn(lines_ref[...], turned_ref[...])
+    var_in.wait()
+    scaled_ref[...] = (latitude * var_ref[...]).astype(BF16)
     scaled = scaled_ref[...]
     out = []
     for i in range(2):
@@ -404,34 +395,32 @@
     came_ref, incr_ref, prev_ref, table_ref, lines_ref, out_ref, sems,
 ):
     copies = Copies(sems)
-    came_in = quarters(copies, came_hbm, came_ref)
-    table_in = quarter_columns(copies, table_hbm, table_ref)
-    incr_in = quarter_columns(copies, incr_hbm, incr_ref)
-    prev_in = quarter_columns(copies, prev_hbm, prev_ref)
+    came_in = copies.start(came_hbm, came_ref)
+    table_in = copies.start(table_hbm, table_ref)
+    prev_in = copies.start(prev_hbm, prev_ref)
+    incr_in = copies.start(incr_hbm, incr_ref)
     gather_lines(came_in, came_ref, lines_ref)
-    lines = lines_ref[...]
+    table_in.wait()
+    table = table_ref[...]
     out = []
-    for i in range(4):
-        table_in[i].wait()
-        incr_in[i].wait()
-        prev_in[i].wait()
-        part = pl.ds(256 * i, 256)
-        covar = nn(lines, table_ref[:, part])
-        out_ref[:, part] = covar + (incr_ref[:, part] - prev_ref[:, part].astype(F32))
-        out.append(copies.start(out_ref.at[:, part], out_hbm.at[:, part]))
+    for i in range(3):
+        part = pl.ds(128 * i, 128)
+        covar = nn(lines_ref[part], table)
+        if i == 0:
+            prev_in.wait()
+            incr_in.wait()
+        out_ref[part] = covar + (incr_ref[part] - prev_ref[part].astype(F32))
+        out.append(copies.start(out_ref.at[part], out_hbm.at[part]))
     for copy in out:
         copy.wait()
 
 
 VMEM = pl.BlockSpec(memory_space=pltpu.VMEM)
-SMEM = pl.BlockSpec(memory_space=pltpu.SMEM)
 HBM = pl.BlockSpec(memory_space=pl.ANY)
 
 
-def call(kernel, outs, ins, scratch, name):
+def call(kernel, outs, ins, scratch, name, aliases=None):
     def place(a):
-        if len(a.shape) == 1:
-            return SMEM
         return VMEM if a.shape[0] == 1 else HBM
 
     return pl.pallas_call(
@@ -440,7 +429,8 @@
         in_specs=[place(a) for a in ins],
         out_specs=jax.tree.map(place, outs),
         scratch_shapes=list(scratch),
-        compiler_params=pltpu.CompilerParams(vmem_limit_bytes=56 * 1024 * 1024),
+        compiler_params=pltpu.CompilerParams(vmem_limit_bytes=60 * 1024 * 1024),
+        input_output_aliases=aliases or {},
         name=name,
     )(*ins)
 
@@ -459,8 +449,6 @@
     table = cosine_table(width)
     turned = np.ascontiguousarray(table.T)
     cols, lines = block_sums(levels, rows, width)
-    place = lax.axis_index("space")
-    edge = jnp.stack([place == 0, place == count - 1]).astype(jnp.int32)
 
     def shape(*dims):
         return jax.ShapeDtypeStruct(dims, BF16)
@@ -475,53 +463,44 @@
         return pltpu.SemaphoreType.DMA(dims)
 
     field = (levels, rows, width)
-    flat, spec, mult_head, mult_tail, head, tail = call(
+    whole, spec, head, tail = call(
         start_kernel,
         (
-            shape(full, width), shape(width, full), shape(levels * 4, width), shape(levels * 4, width),
-            shape(levels * 8, width), shape(levels * 8, width),
+            shape(full + levels * 8, width), shape(width, full), shape(levels * 12, width),
+            shape(levels * 12, width),
         ),
         (mult, table, incr, wind),
         [
             wide(*field), short(width, width), wide(4, levels, 8, width), short(full, width), short(width, full),
-            short(levels * 4, width), short(levels * 4, width), short(levels * 8, width), short(levels * 8, width),
-            sems(24),
+            short(levels * 12, width), short(levels * 12, width), sems(12),
         ],
         "start",
     )
     came = lax.all_to_all(spec.reshape(count, waves, full), "space", 0, 0, tiled=True)
     ring = range(count - 1)
-    down = [(i + 1, i) for i in ring]
-    up = [(i, i + 1) for i in ring]
-    head = lax.ppermute(head, "space", down)
-    tail = lax.ppermute(tail, "space", up)
-    both = ("tm", "space")
-    mult_head = lax.ppermute(
-        mult_head, both, [((t + 1) * count + a, t * count + b) for t in range(times - 1) for a, b in down]
-    )
-    mult_tail = lax.ppermute(
-        mult_tail, both, [((t + 1) * count + a, t * count + b) for t in range(times - 1) for a, b in up]
-    )
-    coming = lax.ppermute(flat, "tm", [(t + 1, t) for t in range(times - 1)])
+    head = lax.ppermute(head, "space", [(i + 1, i) for i in ring])
+    tail = lax.ppermute(tail, "space", [(i, i + 1) for i in ring])
 
     across = width // 128
     stages = [wide(4, across, rows + 8, 128), wide(4, across, TILES, 8, 128)]
-    ends = call(
+    ends, whole = call(
         forward_kernel,
-        shape(full, width),
-        (edge, incr, wind, head, tail),
+        (shape(full, width), shape(full + levels * 8, width)),
+        (incr, wind, head, tail, whole),
         [
-            wide(*field), wide(*field), short(levels * 8, width), short(levels * 8, width),
-            wide(levels * 8, width), wide(levels * 8, width), *stages, short(full, width), sems(2), sems(3, levels),
+            wide(*field), wide(*field), short(levels * 8, width), short(levels * 8, width), short(levels * 8, width),
+            wide(levels * 8, width), wide(levels * 8, width), *stages, short(full, width), sems(5), sems(3, levels),
         ],
         "forward",
-    )
+        {4: 1},
+    )
+    coming = lax.ppermute(whole, "tm", [(t + 1, t) for t in range(times - 1)])
     previous = lax.ppermute(ends, "tm", [(t, t + 1) for t in range(times - 1)])
 
     back = call(
         latitude_kernel,
         shape(lat, full),
-        (came, var, turned, mult_head, mult_tail),
+        (came, var, turned),
         [
             short(count, waves, full), wide(full, lat), short(lat, lat), short(full, lat), short(full, lat),
             short(lat, full), sems(16),
@@ -534,8 +513,7 @@
         backward_kernel,
         (jax.ShapeDtypeStruct(field, F32), jax.ShapeDtypeStruct(obs_dual.shape, F32)),
         (
-            edge, coming, mult_head, mult_tail, wind, head, tail, mult, incr, obs_index, obs_dual, obs_variance,
-            cols, lines,
+            coming, wind, head, tail, mult, incr, obs_index, obs_dual, obs_variance, cols, lines,
         ),
         [
             short(full, width), wide(*field), wide(*field), wide(*field), short(*cols.shape), short(*lines.shape),

time: 80.7 us -> 81.4 us (level)
  the two profiles are of different devices: /device:TPU:193 before, /device:TPU:121 now
where the time goes in v2:
time: 81.4 us; the launch traced here: 81 us
  Pallas kernels  32.7 us (40%)
  starting transfers between devices  28.4 us (35%)
  waiting for transfers between devices  15.3 us (19%)
  local copies, waits for them, and re-layouts  3.79 us (5%)
    pallas_call x5, Pallas kernels, call(): pl.pallas_call(kernel, out_shape=outs, in_specs=[place(a) for a in ins],...  32.7 us
    ppermute x1, waiting for transfers between devices, local(): coming = lax.ppermute(whole, 'tm', [(t + 1, t) for t in range(times - 1)])  8.37 us
    all_to_all x1, starting transfers between devices, local(): lax.all_to_all(spec.reshape(count, waves, full), 'space', 0, 0, tiled=True)  7.77 us
    ppermute x1, waiting for transfers between devices, local(): head = lax.ppermute(head, 'space', [(i + 1, i) for i in ring])  6.89 us
    all_to_all x1, starting transfers between devices, local(): lax.all_to_all(back.reshape(count, rows, full), 'space', 0, 0, tiled=True)  6.31 us
    ppermute x1, starting transfers between devices, local(): tail = lax.ppermute(tail, 'space', [(i, i + 1) for i in ring])  5.4 us
    ppermute x1, starting transfers between devices, local(): previous = lax.ppermute(ends, 'tm', [(t, t + 1) for t in range(times - 1)])  4.75 us
    unnamed x16, local copies, waits for them, and re-layouts  3.79 us
  transfers between devices with their start and end apart: 6, of which 2 were waited for; matrix products, arithmetic and copies ran while one was open for 0% of the time, Pallas kernels for 29%

profile of v2, /device:TPU:121, one launch (start us, length us, event | category | flops | bytes accessed | tf_op | source)
XLA Modules:
  0.0 81.0 jit_solution(8170651317427269323)
XLA Ops:
  0.6 4.4 %start.1 = (bf16[480,1024]{1,0:T(8,128)(2,1)}, bf16[1024,384]{1,0:T(8,128)(2,1)}, bf16[144,1024]{1,0:T(8,128)(2,1)}, bf16[144,1024]{1,0:T(8,128)(2,1)}) custom-call(f32[12,32,1024]{2,1,0:T(8,128)} %bitcast.31, bf16[1024,1024]{1,0:T(8,128)(2,1)} %constant.8.clone.table_hbm, f32[12,32,1024]{2,1,0:T(8,128)} %bitcast.24, f32[12,32,1024]{2,1,0:T(8,128)} %bitcast.28), custom_call_target="tpu_custom_call" | custom-call | tf_op jit(solution)/shard_map/start/pallas_call | solution.py:426
  5.0 7.8 %all-to-all-start = ((bf16[32,32,384]{2,1,0:T(8,128)(2,1)}), bf16[32,32,384]{2,1,0:T(8,128)(2,1)S(1)}, u32[]{:S(2)}, u32[]{:S(2)}) async-start(bf16[32,32,384]{2,1,0:T(8,128)(2,1)} %bitcast.36), calls=%async_computation | async-start | bytes 1572864 | tf_op jit(solution)/shard_map/all_to_all | solution.py:479
  12.8 2.3 %collective-permute-start = (bf16[144,1024]{1,0:T(8,128)(2,1)S(1)}, bf16[144,1024]{1,0:T(8,128)(2,1)S(1)}, u32[]{:S(2)}, u32[]{:S(2)}) collective-permute-start(bf16[144,1024]{1,0:T(8,128)(2,1)S(1)} %copy-done.7), channel_id=1, source_target_pairs={{1,0},{2,1},{3,2},{4,3},{5,4},{6,5},{7,6},{8,7},{9,8},{10,9},{11,1... | collective-permute-start | bytes 884744 | tf_op jit(solution)/shard_map/ppermute | solution.py:481
  15.1 5.4 %collective-permute-start.1 = (bf16[144,1024]{1,0:T(8,128)(2,1)S(1)}, bf16[144,1024]{1,0:T(8,128)(2,1)S(1)}, u32[]{:S(2)}, u32[]{:S(2)}) collective-permute-start(bf16[144,1024]{1,0:T(8,128)(2,1)S(1)} %copy-done.6), channel_id=1, source_target_pairs={{0,1},{1,2},{2,3},{3,4},{4,5},{5,6},{6,7},{7,8},{8,9},{9,10},{10,1... | collective-permute-start | bytes 884744 | tf_op jit(solution)/shard_map/ppermute | solution.py:482
  20.5 6.9 %collective-permute-done.head_hbm = bf16[144,1024]{1,0:T(8,128)(2,1)S(1)} collective-permute-done((bf16[144,1024]{1,0:T(8,128)(2,1)S(1)}, bf16[144,1024]{1,0:T(8,128)(2,1)S(1)}, u32[]{:S(2)}, u32[]{:S(2)}) %collective-permute-start) | collective-permute-done | bytes 294944 | tf_op jit(solution)/shard_map/ppermute | solution.py:481
  27.4 0.0 collective-permute-done.1.tail_hbm
  27.4 0.7 copy-done.2
  28.1 0.1 copy-done.3
  28.3 8.0 %forward.1 = (bf16[384,1024]{1,0:T(8,128)(2,1)}, bf16[480,1024]{1,0:T(8,128)(2,1)}) custom-call(f32[12,32,1024]{2,1,0:T(8,128)} %bitcast.25, f32[12,32,1024]{2,1,0:T(8,128)} %bitcast.29, bf16[144,1024]{1,0:T(8,128)(2,1)} %copy-done.2, bf16[144,1024]{1,0:T(8,128)(2,1)} %copy-done.3, ...), custom_call_target="tpu_custom_call", output_to_operand_aliasing={{1}: (4, {})} | custom-call | tf_op jit(solution)/shard_map/forward/pallas_call | solution.py:426
  36.3 1.9 %collective-permute-start.3 = (bf16[480,1024]{1,0:T(8,128)(2,1)}, bf16[480,1024]{1,0:T(8,128)(2,1)S(1)}, u32[]{:S(2)}, u32[]{:S(2)}) collective-permute-start(bf16[480,1024]{1,0:T(8,128)(2,1)} %get-tuple-element.16), channel_id=1, source_target_pairs={{32,0},{64,32},{96,64},{128,96},{160,128},{192,160},{224,192},{33,... | collective-permute-start | bytes 2949128 | tf_op jit(solution)/shard_map/ppermute | solution.py:497
  38.2 4.8 %collective-permute-start.2 = (bf16[384,1024]{1,0:T(8,128)(2,1)}, bf16[384,1024]{1,0:T(8,128)(2,1)S(1)}, u32[]{:S(2)}, u32[]{:S(2)}) collective-permute-start(bf16[384,1024]{1,0:T(8,128)(2,1)} %get-tuple-element.15), channel_id=1, source_target_pairs={{0,32},{32,64},{64,96},{96,128},{128,160},{160,192},{192,224},{1,3... | collective-permute-start | bytes 2359304 | tf_op jit(solution)/shard_map/ppermute | solution.py:498
  42.9 0.0 all-to-all-done.came_hbm
  43.0 0.0 copy-start
  43.0 0.9 %copy-done = bf16[32,32,384]{2,1,0:T(8,128)(2,1)} copy-done((bf16[32,32,384]{2,1,0:T(8,128)(2,1)}, bf16[32,32,384]{2,1,0:T(8,128)(2,1)S(1)}, u32[]{:S(2)}) %copy-start) | copy-done | bytes 786456
  43.8 5.0 %latitude.1 = bf16[1024,384]{1,0:T(8,128)(2,1)} custom-call(bf16[32,32,384]{2,1,0:T(8,128)(2,1)} %copy-done, f32[384,1024]{1,0:T(8,128)} %bitcast.34, bf16[1024,1024]{1,0:T(8,128)(2,1)} %constant.9.clone.turned_hbm), custom_call_target="tpu_custom_call" | custom-call | tf_op jit(solution)/shard_map/latitude/pallas_call | solution.py:426
  48.8 6.3 %all-to-all-start.1 = ((bf16[32,32,384]{2,1,0:T(8,128)(2,1)}), bf16[32,32,384]{2,1,0:T(8,128)(2,1)S(1)}, u32[]{:S(2)}, u32[]{:S(2)}) async-start(bf16[32,32,384]{2,1,0:T(8,128)(2,1)} %bitcast.33), calls=%async_computation.1 | async-start | bytes 1572864 | tf_op jit(solution)/shard_map/all_to_all | solution.py:510
  55.2 8.4 %collective-permute-done.3.whole_hbm = bf16[480,1024]{1,0:T(8,128)(2,1)S(1)} collective-permute-done((bf16[480,1024]{1,0:T(8,128)(2,1)}, bf16[480,1024]{1,0:T(8,128)(2,1)S(1)}, u32[]{:S(2)}, u32[]{:S(2)}) %collective-permute-start.3) | collective-permute-done | bytes 983072 | tf_op jit(solution)/shard_map/ppermute | solution.py:497
  63.5 0.9 %copy-done.4 = bf16[480,1024]{1,0:T(8,128)(2,1)} copy-done((bf16[480,1024]{1,0:T(8,128)(2,1)}, bf16[480,1024]{1,0:T(8,128)(2,1)S(1)}, u32[]{:S(2)}) %copy-start.4) | copy-done | bytes 983064
  64.5 10.9 %backward.1 = (f32[12,32,1024]{2,1,0:T(8,128)}, f32[1,512]{1,0:T(1,128)}) custom-call(bf16[480,1024]{1,0:T(8,128)(2,1)} %copy-done.4, f32[12,32,1024]{2,1,0:T(8,128)} %bitcast.30, bf16[144,1024]{1,0:T(8,128)(2,1)} %copy-done.2, bf16[144,1024]{1,0:T(8,128)(2,1)} %copy-done.3, f32[12,32,1024]{2,1,0:T(8,128)} %bitcast.32, f32[12,32,1024]{2,1,0:T(8,128)} %bitcast.26, ...), custom_call_target="tpu_custom_call" | custom-call | tf_op jit(solution)/shard_map/backward/pallas_call | solution.py:426
  75.3 0.0 collective-permute-done.2.prev_hbm
  75.4 0.0 all-to-all-done.1.came_hbm
  75.4 0.9 %copy-done.5 = bf16[384,1024]{1,0:T(8,128)(2,1)} copy-done((bf16[384,1024]{1,0:T(8,128)(2,1)}, bf16[384,1024]{1,0:T(8,128)(2,1)S(1)}, u32[]{:S(2)}) %copy-start.5) | copy-done | bytes 786456
  76.3 0.3 copy-done.1
  76.5 4.5 %finish.1 = f32[384,1024]{1,0:T(8,128)} custom-call(bf16[32,32,384]{2,1,0:T(8,128)(2,1)} %copy-done.1, f32[384,1024]{1,0:T(8,128)} %bitcast.27, bf16[384,1024]{1,0:T(8,128)(2,1)} %copy-done.5, bf16[1024,1024]{1,0:T(8,128)(2,1)} %constant.8.clone.table_hbm), custom_call_target="tpu_custom_call" | custom-call | tf_op jit(solution)/shard_map/finish/pallas_call | solution.py:426
  (9 shorter events, 0.0 us)
Async XLA Ops:
  5.0 7.8 %copy-start.7 = (bf16[144,1024]{1,0:T(8,128)(2,1)S(1)}, bf16[144,1024]{1,0:T(8,128)(2,1)}, u32[]{:S(2)}) copy-start(bf16[144,1024]{1,0:T(8,128)(2,1)} %get-tuple-element.12) | copy-start | bytes 884740
  5.0 10.1 %copy-start.6 = (bf16[144,1024]{1,0:T(8,128)(2,1)S(1)}, bf16[144,1024]{1,0:T(8,128)(2,1)}, u32[]{:S(2)}) copy-start(bf16[144,1024]{1,0:T(8,128)(2,1)} %get-tuple-element.13) | copy-start | bytes 884740
  5.0 37.9 %all-to-all-start = ((bf16[32,32,384]{2,1,0:T(8,128)(2,1)}), bf16[32,32,384]{2,1,0:T(8,128)(2,1)S(1)}, u32[]{:S(2)}, u32[]{:S(2)}) async-start(bf16[32,32,384]{2,1,0:T(8,128)(2,1)} %bitcast.36), calls=%async_computation | async-start | bytes 1572864 | tf_op jit(solution)/shard_map/all_to_all | solution.py:479
  12.8 14.6 %collective-permute-start = (bf16[144,1024]{1,0:T(8,128)(2,1)S(1)}, bf16[144,1024]{1,0:T(8,128)(2,1)S(1)}, u32[]{:S(2)}, u32[]{:S(2)}) collective-permute-start(bf16[144,1024]{1,0:T(8,128)(2,1)S(1)} %copy-done.7), channel_id=1, source_target_pairs={{1,0},{2,1},{3,2},{4,3},{5,4},{6,5},{7,6},{8,7},{9,8},{10,9},{11,1... | collective-permute-start | bytes 884744 | tf_op jit(solution)/shard_map/ppermute | solution.py:481
  15.1 12.3 %collective-permute-start.1 = (bf16[144,1024]{1,0:T(8,128)(2,1)S(1)}, bf16[144,1024]{1,0:T(8,128)(2,1)S(1)}, u32[]{:S(2)}, u32[]{:S(2)}) collective-permute-start(bf16[144,1024]{1,0:T(8,128)(2,1)S(1)} %copy-done.6), channel_id=1, source_target_pairs={{0,1},{1,2},{2,3},{3,4},{4,5},{5,6},{6,7},{7,8},{8,9},{9,10},{10,1... | collective-permute-start | bytes 884744 | tf_op jit(solution)/shard_map/ppermute | solution.py:482
  27.4 0.7 copy-start.2
  27.4 0.8 %copy-start.3 = (bf16[144,1024]{1,0:T(8,128)(2,1)}, bf16[144,1024]{1,0:T(8,128)(2,1)S(1)}, u32[]{:S(2)}) copy-start(bf16[144,1024]{1,0:T(8,128)(2,1)S(1)} %collective-permute-done.1.tail_hbm) | copy-start | bytes 884740
  36.3 27.3 %collective-permute-start.3 = (bf16[480,1024]{1,0:T(8,128)(2,1)}, bf16[480,1024]{1,0:T(8,128)(2,1)S(1)}, u32[]{:S(2)}, u32[]{:S(2)}) collective-permute-start(bf16[480,1024]{1,0:T(8,128)(2,1)} %get-tuple-element.16), channel_id=1, source_target_pairs={{32,0},{64,32},{96,64},{128,96},{160,128},{192,160},{224,192},{33,... | collective-permute-start | bytes 2949128 | tf_op jit(solution)/shard_map/ppermute | solution.py:497
  38.2 37.1 %collective-permute-start.2 = (bf16[384,1024]{1,0:T(8,128)(2,1)}, bf16[384,1024]{1,0:T(8,128)(2,1)S(1)}, u32[]{:S(2)}, u32[]{:S(2)}) collective-permute-start(bf16[384,1024]{1,0:T(8,128)(2,1)} %get-tuple-element.15), channel_id=1, source_target_pairs={{0,32},{32,64},{64,96},{96,128},{128,160},{160,192},{192,224},{1,3... | collective-permute-start | bytes 2359304 | tf_op jit(solution)/shard_map/ppermute | solution.py:498
  43.0 0.9 %copy-start = (bf16[32,32,384]{2,1,0:T(8,128)(2,1)}, bf16[32,32,384]{2,1,0:T(8,128)(2,1)S(1)}, u32[]{:S(2)}) copy-start(bf16[32,32,384]{2,1,0:T(8,128)(2,1)S(1)} %all-to-all-done.came_hbm) | copy-start | bytes 2359300
  48.8 26.5 %all-to-all-start.1 = ((bf16[32,32,384]{2,1,0:T(8,128)(2,1)}), bf16[32,32,384]{2,1,0:T(8,128)(2,1)S(1)}, u32[]{:S(2)}, u32[]{:S(2)}) async-start(bf16[32,32,384]{2,1,0:T(8,128)(2,1)} %bitcast.33), calls=%async_computation.1 | async-start | bytes 1572864 | tf_op jit(solution)/shard_map/all_to_all | solution.py:510
  63.5 0.9 %copy-start.4 = (bf16[480,1024]{1,0:T(8,128)(2,1)}, bf16[480,1024]{1,0:T(8,128)(2,1)S(1)}, u32[]{:S(2)}) copy-start(bf16[480,1024]{1,0:T(8,128)(2,1)S(1)} %collective-permute-done.3.whole_hbm) | copy-start | bytes 2949124
  75.3 0.9 %copy-start.5 = (bf16[384,1024]{1,0:T(8,128)(2,1)}, bf16[384,1024]{1,0:T(8,128)(2,1)S(1)}, u32[]{:S(2)}) copy-start(bf16[384,1024]{1,0:T(8,128)(2,1)S(1)} %collective-permute-done.2.prev_hbm) | copy-start | bytes 2359300
  75.4 1.1 %copy-start.1 = (bf16[32,32,384]{2,1,0:T(8,128)(2,1)}, bf16[32,32,384]{2,1,0:T(8,128)(2,1)S(1)}, u32[]{:S(2)}) copy-start(bf16[32,32,384]{2,1,0:T(8,128)(2,1)S(1)} %all-to-all-done.1.came_hbm) | copy-start | bytes 2359300

commit v3 on v2

--- a/solution.py
+++ b/solution.py
@@ -65,50 +65,54 @@
         return copy
 
 
-def start_kernel(
-    mult_hbm, table_hbm, incr_hbm, wind_hbm,
-    whole_hbm, spec_hbm, head_hbm, tail_hbm,
-    mult_ref, table_ref, edge_ref, flat_ref, spec_ref, head_ref, tail_ref, sems,
-):
+def edge_kernel(mult_hbm, incr_hbm, wind_hbm, head_hbm, tail_hbm, edge_ref, head_ref, tail_ref, sems):
+    levels, rows, width = mult_hbm.shape
+    half = levels // 2
+    copies = Copies(sems)
+    coming = [
+        copies.start(source.at[:, pl.ds(at, 8), :], edge_ref.at[3 * end + i])
+        for end, at in enumerate((0, rows - 8))
+        for i, source in enumerate((incr_hbm, wind_hbm, mult_hbm))
+    ]
+    out = []
+    for end, (part_ref, part_hbm) in enumerate(((head_ref, head_hbm), (tail_ref, tail_hbm))):
+        for copy in coming[3 * end : 3 * end + 3]:
+            copy.wait()
+        incr, wind, mult = edge_ref[3 * end], edge_ref[3 * end + 1], edge_ref[3 * end + 2]
+        wind = pltpu.roll(wind, HALF, 1)
+        second = pltpu.roll(mult[half:], HALF, 1)
+        low, less = low_half((levels, 8, width)), low_half((half, 8, width))
+        if end == 0:
+            field, dual = jnp.where(low, incr, wind), jnp.where(less, mult[:half], second)
+        else:
+            field, dual = jnp.where(low, wind, incr), jnp.where(less, second, mult[:half])
+        part_ref[: levels * 8] = field.reshape(levels * 8, width).astype(BF16)
+        part_ref[levels * 8 :] = dual.reshape(half * 8, width).astype(BF16)
+        out.append(copies.start(part_ref, part_hbm))
+    for copy in out:
+        copy.wait()
+
+
+def start_kernel(mult_hbm, table_hbm, _after, flat_hbm, spec_hbm, mult_ref, table_ref, flat_ref, spec_ref, sems):
     levels, rows, width = mult_ref.shape
-    half = levels // 2
     copies = Copies(sems)
     mult_in = copies.start(mult_hbm, mult_ref)
     table_in = copies.start(table_hbm, table_ref)
-    edge_in = [
-        copies.start(source.at[:, pl.ds(at, 8), :], edge_ref.at[i])
-        for i, (source, at) in enumerate(
-            [(incr_hbm, 0), (wind_hbm, 0), (incr_hbm, rows - 8), (wind_hbm, rows - 8)]
-        )
-    ]
-    out = []
     mult_in.wait()
     flat_ref[...] = mult_ref[...].reshape(levels * rows, width).astype(BF16)
-    out.append(copies.start(flat_ref, whole_hbm.at[pl.ds(0, levels * rows)]))
-    first = mult_ref[:, :8, :]
-    last = mult_ref[:, rows - 8 :, :]
-    low = low_half((half, 8, width))
-    head = jnp.where(low, first[:half], pltpu.roll(first[half:], HALF, 1))
-    tail = jnp.where(low, pltpu.roll(last[half:], HALF, 1), last[:half])
-    head_ref[levels * 8 :] = head.reshape(half * 8, width).astype(BF16)
-    tail_ref[levels * 8 :] = tail.reshape(half * 8, width).astype(BF16)
+    out = [copies.start(flat_ref, flat_hbm)]
     flat = flat_ref[...]
     table_in.wait()
     for i in range(2):
         part = pl.ds(512 * i, 512)
         spec_ref[part] = nt(table_ref[part], flat).astype(BF16)
         out.append(copies.start(spec_ref.at[part], spec_hbm.at[part]))
-    for copy in edge_in:
-        copy.wait()
-    low = low_half((levels, 8, width))
-    head = jnp.where(low, edge_ref[0], pltpu.roll(edge_ref[1], HALF, 1))
-    tail = jnp.where(low, pltpu.roll(edge_ref[3], HALF, 1), edge_ref[2])
-    head_ref[: levels * 8] = head.reshape(levels * 8, width).astype(BF16)
-    tail_ref[: levels * 8] = tail.reshape(levels * 8, width).astype(BF16)
-    out.append(copies.start(head_ref, head_hbm))
-    out.append(copies.start(tail_ref, tail_hbm))
     for copy in out:
         copy.wait()
+
+
+def order_kernel(_spec_in, _head, _tail, _spec_out):
+    pass
 
 
 TILES = 5
@@ -218,13 +222,12 @@
 
 
 def forward_kernel(
-    incr_hbm, wind_hbm, head_hbm, tail_hbm, _whole_in, ends_hbm, whole_hbm,
+    incr_hbm, wind_hbm, head_hbm, tail_hbm, ends_hbm, far_hbm,
     incr_ref, wind_ref, head_in, tail_in, far_ref, head_ref, tail_ref, stage_ref, coef_ref, ends_ref, sems, level_sems,
 ):
     levels, rows, width = incr_ref.shape
     half = levels // 2
     copies = Copies(sems)
-    full = levels * rows
     near, far = pl.ds(0, levels * 8), pl.ds(levels * 8, levels * 4)
     margin_in = [copies.start(head_hbm.at[near], head_in), copies.start(tail_hbm.at[near], tail_in)]
 
@@ -255,50 +258,37 @@
             for kind in range(2):
                 fetch(kind, index).wait()
         coefficients(level, levels, wind_ref, head_ref, tail_ref, stage_ref, coef_ref)
-        for group in range(2):
+
+        def at_group(group):
             index = level + group * half
             at = pl.ds(pl.multiple_of(index * 8, 8), 8)
             margin = jnp.where(low, head_ref[at, :], tail_ref[at, :])
-            x = forward_steps(spread_rows(stage_ref.at[2 * group], incr_ref[index], margin), coef_ref)
-            ends = join_rows(stage_ref.at[2 * group + 1], x, rows)
+            x = forward_steps(spread_rows(stage_ref.at[2 + 2 * group], incr_ref[index], margin), coef_ref)
+            ends = join_rows(stage_ref.at[3 + 2 * group], x, rows)
             ends_ref[pl.ds(pl.multiple_of(index * rows, rows), rows), :] = ends.astype(BF16)
             put(index).start()
+
+        for group in range(2):
+            at_group(group)
         return carry
 
     for copy in far_in:
         copy.wait()
-    joined = copies.start(far_ref, whole_hbm.at[pl.ds(full, levels * 8)])
+    joined = copies.start(far_ref, far_hbm)
     lax.fori_loop(0, half, at_level, 0)
     joined.wait()
     for index in range(levels):
         put(index).wait()
 
 
-def backward_kernel(
-    whole_hbm, wind_hbm, head_hbm, tail_hbm, mult_hbm, incr_hbm,
-    index_ref, dual_ref, variance_ref, cols_hbm, lines_hbm,
-    state_hbm, obs_ref,
-    next_ref, wind_ref, mult_ref, incr_ref, cols_ref, lines_ref, head_in, tail_in, nhead_in, ntail_in,
-    head_ref, tail_ref, nhead_ref, ntail_ref, stage_ref, coef_ref, spread_ref, state_ref, sems, level_sems,
+def observe_kernel(
+    incr_hbm, index_ref, dual_ref, variance_ref, cols_hbm, lines_hbm, _after,
+    tall_ref, obs_ref, incr_ref, cols_ref, lines_ref, sems,
 ):
-    levels, rows, width = mult_ref.shape
-    half = levels // 2
+    levels, rows, width = incr_ref.shape
     copies = Copies(sems)
     block_in = [copies.start(cols_hbm, cols_ref), copies.start(lines_hbm, lines_ref)]
-    full = levels * rows
-    near, next_head, next_tail = pl.ds(0, levels * 8), pl.ds(full, levels * 4), pl.ds(full + levels * 4, levels * 4)
-    margin_in = [
-        copies.start(source, target)
-        for source, target in (
-            (head_hbm.at[near], head_in), (tail_hbm.at[near], tail_in),
-            (whole_hbm.at[next_head], nhead_in), (whole_hbm.at[next_tail], ntail_in),
-        )
-    ]
     incr_in = copies.start(incr_hbm, incr_ref)
-    fields_in = [
-        copies.start(source, target)
-        for source, target in ((wind_hbm, wind_ref), (whole_hbm.at[pl.ds(0, full)], next_ref), (mult_hbm, mult_ref))
-    ]
     for copy in block_in:
         copy.wait()
     cols, lines = cols_ref[...], lines_ref[...]
@@ -306,8 +296,7 @@
     high, low_hot = one_hots(index_ref[...], blocks)
     weights = low_hot.astype(BF16)
     summed = sum(nt(p, weights) for p in parts(jnp.where(high, dual_ref[...], 0.0))) * 0.125
-    tall = sum(tn(lines, p) for p in parts(summed))
-    spread_ref[...] = sum(nt(p, cols) for p in parts(tall))
+    tall_ref[...] = sum(tn(lines, p) for p in parts(summed))
     incr_in.wait()
     narrow = sum(nn(p, cols) for p in parts(incr_ref[...].reshape(levels * rows, width)))
     sums = sum(nn(lines, p) for p in parts(narrow))
@@ -315,12 +304,32 @@
     picked = sum(tn(p, high) for p in parts(sums))
     observed = jnp.sum(jnp.where(low_hot, picked, 0.0), axis=0, keepdims=True) * 0.125
     obs_ref[...] = variance_ref[...] * dual_ref[...] + observed
-    for copy in margin_in + fields_in:
+
+
+def backward_kernel(
+    coming_hbm, far_hbm, wind_hbm, head_hbm, tail_hbm, mult_hbm, tall_ref, cols_hbm,
+    state_hbm,
+    next_ref, wind_ref, mult_ref, cols_ref, head_in, tail_in, far_in,
+    head_ref, tail_ref, far_ref, margins_ref, stage_ref, coef_ref, spread_ref, state_ref, sems, level_sems,
+):
+    levels, rows, width = mult_ref.shape
+    half = levels // 2
+    copies = Copies(sems)
+    near = pl.ds(0, levels * 8)
+    arriving = [
+        copies.start(source, target)
+        for source, target in (
+            (cols_hbm, cols_ref), (head_hbm.at[near], head_in), (tail_hbm.at[near], tail_in),
+            (far_hbm, far_in), (wind_hbm, wind_ref), (coming_hbm, next_ref), (mult_hbm, mult_ref),
+        )
+    ]
+    arriving[0].wait()
+    spread_ref[...] = sum(nt(p, cols_ref[...]) for p in parts(tall_ref[...]))
+    for copy in arriving[1:]:
         copy.wait()
     head_ref[...] = head_in[...].astype(F32)
     tail_ref[...] = tail_in[...].astype(F32)
-    nhead_ref[...] = nhead_in[...].astype(F32)
-    ntail_ref[...] = ntail_in[...].astype(F32)
+    far_ref[...] = far_in[...].astype(F32)
     low = low_half((8, width))
 
     def put(index):
@@ -329,18 +338,21 @@
     def at_level(level, carry):
         coefficients(level, levels, wind_ref, head_ref, tail_ref, stage_ref, coef_ref)
         at = pl.ds(pl.multiple_of(level * 8, 8), 8)
-        head, tail = nhead_ref[at, :], ntail_ref[at, :]
-        for group in range(2):
+        head, tail = far_ref[at, :], far_ref[pl.ds(pl.multiple_of(level * 8 + levels * 4, 8), 8), :]
+        margins_ref[0] = jnp.where(low, head, tail)
+        margins_ref[1] = pltpu.roll(jnp.where(low, tail, head), HALF, 0)
+
+        def at_group(group):
             index = level + group * half
-            if group == 0:
-                margin = jnp.where(low, head, tail)
-            else:
-                margin = pltpu.roll(jnp.where(low, tail, head), HALF, 0)
             part = pl.ds(pl.multiple_of(index * rows, rows), rows)
-            y = backward_steps(spread_rows(stage_ref.at[2 * group], next_ref[part, :].astype(F32), margin), coef_ref)
-            back = join_rows(stage_ref.at[2 * group + 1], y, rows)
+            main = next_ref[part, :].astype(F32)
+            y = backward_steps(spread_rows(stage_ref.at[2 + 2 * group], main, margins_ref[group]), coef_ref)
+            back = join_rows(stage_ref.at[3 + 2 * group], y, rows)
             state_ref[index] = (mult_ref[index] - back) + spread_ref[part, :]
             put(index).start()
+
+        for group in range(2):
+            at_group(group)
         return carry
 
     lax.fori_loop(0, half, at_level, 0)
@@ -421,7 +433,7 @@
 
 def call(kernel, outs, ins, scratch, name, aliases=None):
     def place(a):
-        return VMEM if a.shape[0] == 1 else HBM
+        return VMEM if a.shape[0] == 1 or (len(a.shape) == 2 and a.shape[1] < 128 and a.dtype == F32) else HBM
 
     return pl.pallas_call(
         kernel,
@@ -429,7 +441,6 @@
         in_specs=[place(a) for a in ins],
         out_specs=jax.tree.map(place, outs),
         scratch_shapes=list(scratch),
-        compiler_params=pltpu.CompilerParams(vmem_limit_bytes=60 * 1024 * 1024),
         input_output_aliases=aliases or {},
         name=name,
     )(*ins)
@@ -463,38 +474,40 @@
         return pltpu.SemaphoreType.DMA(dims)
 
     field = (levels, rows, width)
-    whole, spec, head, tail = call(
+    head, tail = call(
+        edge_kernel,
+        (shape(levels * 12, width), shape(levels * 12, width)),
+        (mult, incr, wind),
+        [wide(6, levels, 8, width), short(levels * 12, width), short(levels * 12, width), sems(8)],
+        "edges",
+    )
+    flat, spec = call(
         start_kernel,
-        (
-            shape(full + levels * 8, width), shape(width, full), shape(levels * 12, width),
-            shape(levels * 12, width),
-        ),
-        (mult, table, incr, wind),
-        [
-            wide(*field), short(width, width), wide(4, levels, 8, width), short(full, width), short(width, full),
-            short(levels * 12, width), short(levels * 12, width), sems(12),
-        ],
+        (shape(full, width), shape(width, full)),
+        (mult, table, head),
+        [wide(*field), short(width, width), short(full, width), short(width, full), sems(8)],
         "start",
     )
-    came = lax.all_to_all(spec.reshape(count, waves, full), "space", 0, 0, tiled=True)
     ring = range(count - 1)
     head = lax.ppermute(head, "space", [(i + 1, i) for i in ring])
     tail = lax.ppermute(tail, "space", [(i, i + 1) for i in ring])
+    spec = call(order_kernel, shape(width, full), (spec, head, tail), [], "order", {0: 0})
+    came = lax.all_to_all(spec.reshape(count, waves, full), "space", 0, 0, tiled=True)
+    coming = lax.ppermute(flat, "tm", [(t + 1, t) for t in range(times - 1)])
 
     across = width // 128
-    stages = [wide(4, across, rows + 8, 128), wide(4, across, TILES, 8, 128)]
-    ends, whole = call(
+    stages = [wide(6, across, rows + 8, 128), wide(4, across, TILES, 8, 128)]
+    ends, far = call(
         forward_kernel,
-        (shape(full, width), shape(full + levels * 8, width)),
-        (incr, wind, head, tail, whole),
+        (shape(full, width), shape(levels * 8, width)),
+        (incr, wind, head, tail),
         [
             wide(*field), wide(*field), short(levels * 8, width), short(levels * 8, width), short(levels * 8, width),
             wide(levels * 8, width), wide(levels * 8, width), *stages, short(full, width), sems(5), sems(3, levels),
         ],
         "forward",
-        {4: 1},
-    )
-    coming = lax.ppermute(whole, "tm", [(t + 1, t) for t in range(times - 1)])
+    )
+    far = lax.ppermute(far, "tm", [(t + 1, t) for t in range(times - 1)])
     previous = lax.ppermute(ends, "tm", [(t, t + 1) for t in range(times - 1)])
 
     back = call(
@@ -509,17 +522,22 @@
     )
     returned = lax.all_to_all(back.reshape(count, rows, full), "space", 0, 0, tiled=True)
 
-    state_rows, obs_rows = call(
+    tall, obs_rows = call(
+        observe_kernel,
+        (jax.ShapeDtypeStruct((full, cols.shape[1]), F32), jax.ShapeDtypeStruct(obs_dual.shape, F32)),
+        (incr, obs_index, obs_dual, obs_variance, cols, lines, back),
+        [wide(*field), short(*cols.shape), short(*lines.shape), sems(3)],
+        "observe",
+    )
+    state_rows = call(
         backward_kernel,
-        (jax.ShapeDtypeStruct(field, F32), jax.ShapeDtypeStruct(obs_dual.shape, F32)),
-        (
-            coming, wind, head, tail, mult, incr, obs_index, obs_dual, obs_variance, cols, lines,
-        ),
+        jax.ShapeDtypeStruct(field, F32),
+        (coming, far, wind, head, tail, mult, tall, cols),
         [
-            short(full, width), wide(*field), wide(*field), wide(*field), short(*cols.shape), short(*lines.shape),
-            short(levels * 8, width), short(levels * 8, width), short(levels * 4, width), short(levels * 4, width),
-            wide(levels * 8, width), wide(levels * 8, width), wide(levels * 4, width), wide(levels * 4, width),
-            *stages, wide(full, width), wide(*field), sems(16), sems(levels),
+            short(full, width), wide(*field), wide(*field), short(*cols.shape),
+            short(levels * 8, width), short(levels * 8, width), short(levels * 8, width),
+            wide(levels * 8, width), wide(levels * 8, width), wide(levels * 8, width), wide(2, 8, width),
+            *stages, wide(full, width), wide(*field), sems(8), sems(levels),
         ],
         "backward",
     )

time: 81.4 us -> 78.5 us (0.964)
  the two profiles are of different devices: /device:TPU:121 before, /device:TPU:98 now
where the time goes in v3:
time: 78.5 us; the launch traced here: 77.9 us
  Pallas kernels  37.1 us (47%)
  starting transfers between devices  27.9 us (36%)
  waiting for transfers between devices  8.46 us (11%)
  local copies, waits for them, and re-layouts  3.69 us (5%)
  between operations  0.83 us (1%)
    pallas_call x8, Pallas kernels, call(): pl.pallas_call(kernel, out_shape=outs, in_specs=[place(a) for a in ins],...  37.1 us
    all_to_all x1, starting transfers between devices, local(): lax.all_to_all(back.reshape(count, rows, full), 'space', 0, 0, tiled=True)  7.52 us
    all_to_all x1, starting transfers between devices, local(): lax.all_to_all(spec.reshape(count, waves, full), 'space', 0, 0, tiled=True)  5.15 us
    ppermute x1, starting transfers between devices, local(): previous = lax.ppermute(ends, 'tm', [(t, t + 1) for t in range(times - 1)])  5.04 us
    ppermute x1, starting transfers between devices, local(): head = lax.ppermute(head, 'space', [(i + 1, i) for i in ring])  4.33 us
    ppermute x1, waiting for transfers between devices, local(): tail = lax.ppermute(tail, 'space', [(i, i + 1) for i in ring])  4.26 us
    ppermute x1, waiting for transfers between devices, local(): far = lax.ppermute(far, 'tm', [(t + 1, t) for t in range(times - 1)])  4.18 us
    unnamed x18, local copies, waits for them, and re-layouts  3.69 us
  transfers between devices with their start and end apart: 7, of which 2 were waited for; matrix products, arithmetic and copies ran while one was open for 0% of the time, Pallas kernels for 39%

profile of v3, /device:TPU:98, one launch (start us, length us, event | category | flops | bytes accessed | tf_op | source)
XLA Modules:
  0.0 77.9 jit_solution(18315050551781599116)
XLA Ops:
  0.6 2.4 %edges.1 = (bf16[144,1024]{1,0:T(8,128)(2,1)}, bf16[144,1024]{1,0:T(8,128)(2,1)}) custom-call(f32[12,32,1024]{2,1,0:T(8,128)} %bitcast.31, f32[12,32,1024]{2,1,0:T(8,128)} %bitcast.24, f32[12,32,1024]{2,1,0:T(8,128)} %bitcast.28), custom_call_target="tpu_custom_call" | custom-call | tf_op jit(solution)/shard_map/edges/pallas_call | solution.py:438
  3.1 4.3 %collective-permute-start = (bf16[144,1024]{1,0:T(8,128)(2,1)}, bf16[144,1024]{1,0:T(8,128)(2,1)S(1)}, u32[]{:S(2)}, u32[]{:S(2)}) collective-permute-start(bf16[144,1024]{1,0:T(8,128)(2,1)} %get-tuple-element.11._after), channel_id=1, source_target_pairs={{1,0},{2,1},{3,2},{4,3},{5,4},{6,5},{7,6},{8,7},{9,8},{10,9},{11,1... | collective-permute-start | bytes 884744 | tf_op jit(solution)/shard_map/ppermute | solution.py:492
  7.4 1.9 %collective-permute-start.1 = (bf16[144,1024]{1,0:T(8,128)(2,1)}, bf16[144,1024]{1,0:T(8,128)(2,1)S(1)}, u32[]{:S(2)}, u32[]{:S(2)}) collective-permute-start(bf16[144,1024]{1,0:T(8,128)(2,1)} %get-tuple-element.13), channel_id=1, source_target_pairs={{0,1},{1,2},{2,3},{3,4},{4,5},{5,6},{6,7},{7,8},{8,9},{9,10},{10,1... | collective-permute-start | bytes 884744 | tf_op jit(solution)/shard_map/ppermute | solution.py:493
  9.3 4.1 %start.1 = (bf16[384,1024]{1,0:T(8,128)(2,1)}, bf16[1024,384]{1,0:T(8,128)(2,1)}) custom-call(f32[12,32,1024]{2,1,0:T(8,128)} %bitcast.32, bf16[1024,1024]{1,0:T(8,128)(2,1)} %constant.8.clone.table_hbm, bf16[144,1024]{1,0:T(8,128)(2,1)} %get-tuple-element.11._after), custom_call_target="tpu_custom_call" | custom-call | tf_op jit(solution)/shard_map/start/pallas_call | solution.py:438
  13.5 0.0 collective-permute-done._head.head_hbm
  13.5 4.3 %collective-permute-done.1._tail.tail_hbm = bf16[144,1024]{1,0:T(8,128)(2,1)S(1)} collective-permute-done((bf16[144,1024]{1,0:T(8,128)(2,1)}, bf16[144,1024]{1,0:T(8,128)(2,1)S(1)}, u32[]{:S(2)}, u32[]{:S(2)}) %collective-permute-start.1) | collective-permute-done | bytes 294944 | tf_op jit(solution)/shard_map/ppermute | solution.py:493
  17.8 0.7 copy-done.3
  18.5 5.2 %all-to-all-start = ((bf16[32,32,384]{2,1,0:T(8,128)(2,1)}), bf16[32,32,384]{2,1,0:T(8,128)(2,1)S(1)}, u32[]{:S(2)}, u32[]{:S(2)}) async-start(bf16[32,32,384]{2,1,0:T(8,128)(2,1)} %bitcast.35), calls=%async_computation | async-start | bytes 1572864 | tf_op jit(solution)/shard_map/all_to_all | solution.py:495
  23.7 2.0 %collective-permute-start.3 = (bf16[384,1024]{1,0:T(8,128)(2,1)S(1)}, bf16[384,1024]{1,0:T(8,128)(2,1)S(1)}, u32[]{:S(2)}, u32[]{:S(2)}) collective-permute-start(bf16[384,1024]{1,0:T(8,128)(2,1)S(1)} %copy-done.7), channel_id=1, source_target_pairs={{32,0},{64,32},{96,64},{128,96},{160,128},{192,160},{224,192},{33,... | collective-permute-start | bytes 2359304 | tf_op jit(solution)/shard_map/ppermute | solution.py:496
  25.7 7.9 %forward.1 = (bf16[384,1024]{1,0:T(8,128)(2,1)}, bf16[96,1024]{1,0:T(8,128)(2,1)}) custom-call(f32[12,32,1024]{2,1,0:T(8,128)} %bitcast.25, f32[12,32,1024]{2,1,0:T(8,128)} %bitcast.29, bf16[144,1024]{1,0:T(8,128)(2,1)} %copy-done.2, bf16[144,1024]{1,0:T(8,128)(2,1)} %copy-done.3), custom_call_target="tpu_custom_call" | custom-call | tf_op jit(solution)/shard_map/forward/pallas_call | solution.py:438
  33.6 5.0 %collective-permute-start.2 = (bf16[384,1024]{1,0:T(8,128)(2,1)}, bf16[384,1024]{1,0:T(8,128)(2,1)S(1)}, u32[]{:S(2)}, u32[]{:S(2)}) collective-permute-start(bf16[384,1024]{1,0:T(8,128)(2,1)} %get-tuple-element.14), channel_id=1, source_target_pairs={{0,32},{32,64},{64,96},{96,128},{128,160},{160,192},{192,224},{1,3... | collective-permute-start | bytes 2359304 | tf_op jit(solution)/shard_map/ppermute | solution.py:511
  38.6 0.0 copy-start
  38.6 0.9 %copy-done = bf16[32,32,384]{2,1,0:T(8,128)(2,1)} copy-done((bf16[32,32,384]{2,1,0:T(8,128)(2,1)}, bf16[32,32,384]{2,1,0:T(8,128)(2,1)S(1)}, u32[]{:S(2)}) %copy-start) | copy-done | bytes 786456
  39.5 5.0 %latitude.1._after = bf16[1024,384]{1,0:T(8,128)(2,1)} custom-call(bf16[32,32,384]{2,1,0:T(8,128)(2,1)} %copy-done, f32[384,1024]{1,0:T(8,128)} %bitcast.36, bf16[1024,1024]{1,0:T(8,128)(2,1)} %constant.9.clone.turned_hbm), custom_call_target="tpu_custom_call" | custom-call | tf_op jit(solution)/shard_map/latitude/pallas_call | solution.py:438
  44.5 7.5 %all-to-all-start.1 = ((bf16[32,32,384]{2,1,0:T(8,128)(2,1)}), bf16[32,32,384]{2,1,0:T(8,128)(2,1)S(1)}, u32[]{:S(2)}, u32[]{:S(2)}) async-start(bf16[32,32,384]{2,1,0:T(8,128)(2,1)} %bitcast.34), calls=%async_computation.1 | async-start | bytes 1572864 | tf_op jit(solution)/shard_map/all_to_all | solution.py:523
  52.0 1.9 %collective-permute-start.4 = (bf16[96,1024]{1,0:T(8,128)(2,1)S(1)}, bf16[96,1024]{1,0:T(8,128)(2,1)S(1)}, u32[]{:S(2)}, u32[]{:S(2)}) collective-permute-start(bf16[96,1024]{1,0:T(8,128)(2,1)S(1)} %copy-done.8), channel_id=1, source_target_pairs={{32,0},{64,32},{96,64},{128,96},{160,128},{192,160},{224,192},{33,... | collective-permute-start | bytes 589832 | tf_op jit(solution)/shard_map/ppermute | solution.py:510
  54.0 3.9 %observe.1 = (f32[384,64]{1,0:T(8,128)}, f32[1,512]{1,0:T(1,128)}) custom-call(f32[12,32,1024]{2,1,0:T(8,128)} %bitcast.26, s32[1,512]{1,0:T(1,128)} %index_ref.1, f32[1,512]{1,0:T(1,128)} %dual_ref.1, f32[1,512]{1,0:T(1,128)} %variance_ref.1, bf16[1024,64]{1,0:T(8,128)(2,1)} %constant.10.clone.cols_hbm, bf16[96,384]{1,0:T(8,128)(2,1)} %constant.11.clone.lines_hbm, ...), custom_call_target="tpu_custom_call" | custom-call | tf_op jit(solution)/shard_map/observe/pallas_call | solution.py:438
  57.9 4.2 %collective-permute-done.4.far_hbm = bf16[96,1024]{1,0:T(8,128)(2,1)S(1)} collective-permute-done((bf16[96,1024]{1,0:T(8,128)(2,1)S(1)}, bf16[96,1024]{1,0:T(8,128)(2,1)S(1)}, u32[]{:S(2)}, u32[]{:S(2)}) %collective-permute-start.4) | collective-permute-done | bytes 196640 | tf_op jit(solution)/shard_map/ppermute | solution.py:510
  62.1 0.7 copy-done.6
  62.8 0.3 copy-done.4
  63.1 9.2 %backward.1 = f32[12,32,1024]{2,1,0:T(8,128)} custom-call(bf16[384,1024]{1,0:T(8,128)(2,1)} %copy-done.4, bf16[96,1024]{1,0:T(8,128)(2,1)} %copy-done.6, f32[12,32,1024]{2,1,0:T(8,128)} %bitcast.30, bf16[144,1024]{1,0:T(8,128)(2,1)} %copy-done.2, bf16[144,1024]{1,0:T(8,128)(2,1)} %copy-done.3, f32[12,32,1024]{2,1,0:T(8,128)} %bitcast.33, ...), custom_call_target="tpu_custom_call" | custom-call | tf_op jit(solution)/shard_map/backward/pallas_call | solution.py:438
  72.3 0.9 %copy-done.5 = bf16[384,1024]{1,0:T(8,128)(2,1)} copy-done((bf16[384,1024]{1,0:T(8,128)(2,1)}, bf16[384,1024]{1,0:T(8,128)(2,1)S(1)}, u32[]{:S(2)}) %copy-start.5) | copy-done | bytes 786456
  73.2 0.2 copy-done.1
  73.4 4.5 %finish.1 = f32[384,1024]{1,0:T(8,128)} custom-call(bf16[32,32,384]{2,1,0:T(8,128)(2,1)} %copy-done.1, f32[384,1024]{1,0:T(8,128)} %bitcast.27, bf16[384,1024]{1,0:T(8,128)(2,1)} %copy-done.5, bf16[1024,1024]{1,0:T(8,128)(2,1)} %constant.8.clone.table_hbm), custom_call_target="tpu_custom_call" | custom-call | tf_op jit(solution)/shard_map/finish/pallas_call | solution.py:438
  (16 shorter events, 0.0 us)
Async XLA Ops:
  3.1 10.4 %collective-permute-start = (bf16[144,1024]{1,0:T(8,128)(2,1)}, bf16[144,1024]{1,0:T(8,128)(2,1)S(1)}, u32[]{:S(2)}, u32[]{:S(2)}) collective-permute-start(bf16[144,1024]{1,0:T(8,128)(2,1)} %get-tuple-element.11._after), channel_id=1, source_target_pairs={{1,0},{2,1},{3,2},{4,3},{5,4},{6,5},{7,6},{8,7},{9,8},{10,9},{11,1... | collective-permute-start | bytes 884744 | tf_op jit(solution)/shard_map/ppermute | solution.py:492
  7.4 10.4 %collective-permute-start.1 = (bf16[144,1024]{1,0:T(8,128)(2,1)}, bf16[144,1024]{1,0:T(8,128)(2,1)S(1)}, u32[]{:S(2)}, u32[]{:S(2)}) collective-permute-start(bf16[144,1024]{1,0:T(8,128)(2,1)} %get-tuple-element.13), channel_id=1, source_target_pairs={{0,1},{1,2},{2,3},{3,4},{4,5},{5,6},{6,7},{7,8},{8,9},{9,10},{10,1... | collective-permute-start | bytes 884744 | tf_op jit(solution)/shard_map/ppermute | solution.py:493
  13.5 4.3 %copy-start.2 = (bf16[144,1024]{1,0:T(8,128)(2,1)}, bf16[144,1024]{1,0:T(8,128)(2,1)S(1)}, u32[]{:S(2)}) copy-start(bf16[144,1024]{1,0:T(8,128)(2,1)S(1)} %collective-permute-done._head.head_hbm) | copy-start | bytes 884740
  17.8 0.7 copy-start.3
  18.5 5.2 %copy-start.7 = (bf16[384,1024]{1,0:T(8,128)(2,1)S(1)}, bf16[384,1024]{1,0:T(8,128)(2,1)}, u32[]{:S(2)}) copy-start(bf16[384,1024]{1,0:T(8,128)(2,1)} %get-tuple-element.16) | copy-start | bytes 2359300
  18.5 20.1 %all-to-all-start = ((bf16[32,32,384]{2,1,0:T(8,128)(2,1)}), bf16[32,32,384]{2,1,0:T(8,128)(2,1)S(1)}, u32[]{:S(2)}, u32[]{:S(2)}) async-start(bf16[32,32,384]{2,1,0:T(8,128)(2,1)} %bitcast.35), calls=%async_computation | async-start | bytes 1572864 | tf_op jit(solution)/shard_map/all_to_all | solution.py:495
  23.7 38.4 %collective-permute-start.3 = (bf16[384,1024]{1,0:T(8,128)(2,1)S(1)}, bf16[384,1024]{1,0:T(8,128)(2,1)S(1)}, u32[]{:S(2)}, u32[]{:S(2)}) collective-permute-start(bf16[384,1024]{1,0:T(8,128)(2,1)S(1)} %copy-done.7), channel_id=1, source_target_pairs={{32,0},{64,32},{96,64},{128,96},{160,128},{192,160},{224,192},{33,... | collective-permute-start | bytes 2359304 | tf_op jit(solution)/shard_map/ppermute | solution.py:496
  33.6 38.7 %collective-permute-start.2 = (bf16[384,1024]{1,0:T(8,128)(2,1)}, bf16[384,1024]{1,0:T(8,128)(2,1)S(1)}, u32[]{:S(2)}, u32[]{:S(2)}) collective-permute-start(bf16[384,1024]{1,0:T(8,128)(2,1)} %get-tuple-element.14), channel_id=1, source_target_pairs={{0,32},{32,64},{64,96},{96,128},{128,160},{160,192},{192,224},{1,3... | collective-permute-start | bytes 2359304 | tf_op jit(solution)/shard_map/ppermute | solution.py:511
  38.6 0.9 %copy-start = (bf16[32,32,384]{2,1,0:T(8,128)(2,1)}, bf16[32,32,384]{2,1,0:T(8,128)(2,1)S(1)}, u32[]{:S(2)}) copy-start(bf16[32,32,384]{2,1,0:T(8,128)(2,1)S(1)} %all-to-all-done.came_hbm) | copy-start | bytes 2359300
  44.5 7.5 %copy-start.8 = (bf16[96,1024]{1,0:T(8,128)(2,1)S(1)}, bf16[96,1024]{1,0:T(8,128)(2,1)}, u32[]{:S(2)}) copy-start(bf16[96,1024]{1,0:T(8,128)(2,1)} %get-tuple-element.17) | copy-start | bytes 589828
  44.5 27.8 %all-to-all-start.1 = ((bf16[32,32,384]{2,1,0:T(8,128)(2,1)}), bf16[32,32,384]{2,1,0:T(8,128)(2,1)S(1)}, u32[]{:S(2)}, u32[]{:S(2)}) async-start(bf16[32,32,384]{2,1,0:T(8,128)(2,1)} %bitcast.34), calls=%async_computation.1 | async-start | bytes 1572864 | tf_op jit(solution)/shard_map/all_to_all | solution.py:523
  52.0 10.1 %collective-permute-start.4 = (bf16[96,1024]{1,0:T(8,128)(2,1)S(1)}, bf16[96,1024]{1,0:T(8,128)(2,1)S(1)}, u32[]{:S(2)}, u32[]{:S(2)}) collective-permute-start(bf16[96,1024]{1,0:T(8,128)(2,1)S(1)} %copy-done.8), channel_id=1, source_target_pairs={{32,0},{64,32},{96,64},{128,96},{160,128},{192,160},{224,192},{33,... | collective-permute-start | bytes 589832 | tf_op jit(solution)/shard_map/ppermute | solution.py:510
  62.1 0.7 copy-start.6
  62.1 1.0 %copy-start.4 = (bf16[384,1024]{1,0:T(8,128)(2,1)}, bf16[384,1024]{1,0:T(8,128)(2,1)S(1)}, u32[]{:S(2)}) copy-start(bf16[384,1024]{1,0:T(8,128)(2,1)S(1)} %collective-permute-done.3.coming_hbm) | copy-start | bytes 2359300
  72.3 0.9 %copy-start.5 = (bf16[384,1024]{1,0:T(8,128)(2,1)}, bf16[384,1024]{1,0:T(8,128)(2,1)S(1)}, u32[]{:S(2)}) copy-start(bf16[384,1024]{1,0:T(8,128)(2,1)S(1)} %collective-permute-done.2.prev_hbm) | copy-start | bytes 2359300
  72.3 1.1 %copy-start.1 = (bf16[32,32,384]{2,1,0:T(8,128)(2,1)}, bf16[32,32,384]{2,1,0:T(8,128)(2,1)S(1)}, u32[]{:S(2)}) copy-start(bf16[32,32,384]{2,1,0:T(8,128)(2,1)S(1)} %all-to-all-done.1.came_hbm) | copy-start | bytes 2359300

commit v4 on v3

--- a/solution.py
+++ b/solution.py
@@ -65,7 +65,7 @@
         return copy
 
 
-def edge_kernel(mult_hbm, incr_hbm, wind_hbm, head_hbm, tail_hbm, edge_ref, head_ref, tail_ref, sems):
+def edge_kernel(mult_hbm, incr_hbm, wind_hbm, head_ref, tail_ref, edge_ref, sems):
     levels, rows, width = mult_hbm.shape
     half = levels // 2
     copies = Copies(sems)
@@ -74,8 +74,7 @@
         for end, at in enumerate((0, rows - 8))
         for i, source in enumerate((incr_hbm, wind_hbm, mult_hbm))
     ]
-    out = []
-    for end, (part_ref, part_hbm) in enumerate(((head_ref, head_hbm), (tail_ref, tail_hbm))):
+    for end, part_ref in enumerate((head_ref, tail_ref)):
         for copy in coming[3 * end : 3 * end + 3]:
             copy.wait()
         incr, wind, mult = edge_ref[3 * end], edge_ref[3 * end + 1], edge_ref[3 * end + 2]
@@ -88,19 +87,16 @@
             field, dual = jnp.where(low, wind, incr), jnp.where(less, second, mult[:half])
         part_ref[: levels * 8] = field.reshape(levels * 8, width).astype(BF16)
         part_ref[levels * 8 :] = dual.reshape(half * 8, width).astype(BF16)
-        out.append(copies.start(part_ref, part_hbm))
-    for copy in out:
-        copy.wait()
-
-
-def start_kernel(mult_hbm, table_hbm, _after, flat_hbm, spec_hbm, mult_ref, table_ref, flat_ref, spec_ref, sems):
+
+
+def start_kernel(mult_hbm, table_hbm, _after, whole_hbm, spec_hbm, mult_ref, table_ref, flat_ref, spec_ref, sems):
     levels, rows, width = mult_ref.shape
     copies = Copies(sems)
     mult_in = copies.start(mult_hbm, mult_ref)
     table_in = copies.start(table_hbm, table_ref)
     mult_in.wait()
     flat_ref[...] = mult_ref[...].reshape(levels * rows, width).astype(BF16)
-    out = [copies.start(flat_ref, flat_hbm)]
+    out = [copies.start(flat_ref, whole_hbm.at[pl.ds(0, levels * rows)])]
     flat = flat_ref[...]
     table_in.wait()
     for i in range(2):
@@ -113,6 +109,18 @@
 
 def order_kernel(_spec_in, _head, _tail, _spec_out):
     pass
+
+
+def join_kernel(_whole_in, head_ref, tail_ref, whole_hbm, sems):
+    copies = Copies(sems)
+    size = whole_hbm.shape[0] // 10
+    start, far = whole_hbm.shape[0] - 2 * size, head_ref.shape[0] - size
+    out = [
+        copies.start(source.at[pl.ds(far, size)], whole_hbm.at[pl.ds(start + size * i, size)])
+        for i, source in enumerate((head_ref, tail_ref))
+    ]
+    for copy in out:
+        copy.wait()
 
 
 TILES = 5
@@ -222,14 +230,11 @@
 
 
 def forward_kernel(
-    incr_hbm, wind_hbm, head_hbm, tail_hbm, ends_hbm, far_hbm,
-    incr_ref, wind_ref, head_in, tail_in, far_ref, head_ref, tail_ref, stage_ref, coef_ref, ends_ref, sems, level_sems,
+    incr_hbm, wind_hbm, head_in, tail_in, ends_hbm,
+    incr_ref, wind_ref, head_ref, tail_ref, stage_ref, coef_ref, ends_ref, level_sems,
 ):
     levels, rows, width = incr_ref.shape
     half = levels // 2
-    copies = Copies(sems)
-    near, far = pl.ds(0, levels * 8), pl.ds(levels * 8, levels * 4)
-    margin_in = [copies.start(head_hbm.at[near], head_in), copies.start(tail_hbm.at[near], tail_in)]
 
     def fetch(kind, index):
         source, target = ((wind_hbm, wind_ref), (incr_hbm, incr_ref))[kind]
@@ -243,14 +248,8 @@
         for index in (level, level + half):
             for kind in range(2):
                 fetch(kind, index).start()
-    far_in = [
-        copies.start(head_hbm.at[far], far_ref.at[pl.ds(0, levels * 4)]),
-        copies.start(tail_hbm.at[far], far_ref.at[pl.ds(levels * 4, levels * 4)]),
-    ]
-    for copy in margin_in:
-        copy.wait()
-    head_ref[...] = head_in[...].astype(F32)
-    tail_ref[...] = tail_in[...].astype(F32)
+    head_ref[...] = head_in[: levels * 8].astype(F32)
+    tail_ref[...] = tail_in[: levels * 8].astype(F32)
     low = low_half((8, width))
 
     def at_level(level, carry):
@@ -272,11 +271,7 @@
             at_group(group)
         return carry
 
-    for copy in far_in:
-        copy.wait()
-    joined = copies.start(far_ref, far_hbm)
     lax.fori_loop(0, half, at_level, 0)
-    joined.wait()
     for index in range(levels):
         put(index).wait()
 
@@ -307,29 +302,26 @@
 
 
 def backward_kernel(
-    coming_hbm, far_hbm, wind_hbm, head_hbm, tail_hbm, mult_hbm, tall_ref, cols_hbm,
+    coming_ref, wind_hbm, head_in, tail_in, mult_hbm, tall_ref, cols_hbm,
     state_hbm,
-    next_ref, wind_ref, mult_ref, cols_ref, head_in, tail_in, far_in,
+    wind_ref, mult_ref, cols_ref,
     head_ref, tail_ref, far_ref, margins_ref, stage_ref, coef_ref, spread_ref, state_ref, sems, level_sems,
 ):
     levels, rows, width = mult_ref.shape
     half = levels // 2
     copies = Copies(sems)
-    near = pl.ds(0, levels * 8)
+    full = levels * rows
     arriving = [
         copies.start(source, target)
-        for source, target in (
-            (cols_hbm, cols_ref), (head_hbm.at[near], head_in), (tail_hbm.at[near], tail_in),
-            (far_hbm, far_in), (wind_hbm, wind_ref), (coming_hbm, next_ref), (mult_hbm, mult_ref),
-        )
+        for source, target in ((cols_hbm, cols_ref), (wind_hbm, wind_ref), (mult_hbm, mult_ref))
     ]
     arriving[0].wait()
     spread_ref[...] = sum(nt(p, cols_ref[...]) for p in parts(tall_ref[...]))
     for copy in arriving[1:]:
         copy.wait()
-    head_ref[...] = head_in[...].astype(F32)
-    tail_ref[...] = tail_in[...].astype(F32)
-    far_ref[...] = far_in[...].astype(F32)
+    head_ref[...] = head_in[: levels * 8].astype(F32)
+    tail_ref[...] = tail_in[: levels * 8].astype(F32)
+    far_ref[...] = coming_ref[full:].astype(F32)
     low = low_half((8, width))
 
     def put(index):
@@ -345,7 +337,7 @@
         def at_group(group):
             index = level + group * half
             part = pl.ds(pl.multiple_of(index * rows, rows), rows)
-            main = next_ref[part, :].astype(F32)
+            main = coming_ref[part, :].astype(F32)
             y = backward_steps(spread_rows(stage_ref.at[2 + 2 * group], main, margins_ref[group]), coef_ref)
             back = join_rows(stage_ref.at[3 + 2 * group], y, rows)
             state_ref[index] = (mult_ref[index] - back) + spread_ref[part, :]
@@ -360,14 +352,13 @@
         put(index).wait()
 
 
-def gather_lines(came_in, came_ref, lines_ref):
+def gather_lines(came_ref, lines_ref):
     count, rows, wide = came_ref.shape
     groups, fields = count // 4, wide // 128
     source = lax.broadcasted_iota(jnp.int32, (512, 512), 0)
     target = lax.broadcasted_iota(jnp.int32, (512, 512), 1)
     swapped = ((target & 127) >> 5) * 128 + (target >> 7) * 32 + (target & 31)
     perm = (source == swapped).astype(BF16)
-    came_in.wait()
     for g in range(fields):
         piece = came_ref[:, :, g * 128 : (g + 1) * 128].reshape(groups, 4, rows, 128)
         left = jnp.concatenate([piece[:, i].reshape(groups * rows, 128) for i in range(4)], axis=1)
@@ -380,14 +371,13 @@
 
 
 def latitude_kernel(
-    came_hbm, var_hbm, turned_hbm, out_hbm,
-    came_ref, var_ref, turned_ref, lines_ref, scaled_ref, out_ref, sems,
+    came_ref, var_hbm, turned_hbm, out_hbm,
+    var_ref, turned_ref, lines_ref, scaled_ref, out_ref, sems,
 ):
     copies = Copies(sems)
-    came_in = copies.start(came_hbm, came_ref)
     turned_in = copies.start(turned_hbm, turned_ref)
     var_in = copies.start(var_hbm, var_ref)
-    gather_lines(came_in, came_ref, lines_ref)
+    gather_lines(came_ref, lines_ref)
     turned_in.wait()
     latitude = nn(lines_ref[...], turned_ref[...])
     var_in.wait()
@@ -403,15 +393,13 @@
 
 
 def finish_kernel(
-    came_hbm, incr_hbm, prev_hbm, table_hbm, out_hbm,
-    came_ref, incr_ref, prev_ref, table_ref, lines_ref, out_ref, sems,
+    came_ref, incr_hbm, prev_ref, table_hbm, out_hbm,
+    incr_ref, table_ref, lines_ref, out_ref, sems,
 ):
     copies = Copies(sems)
-    came_in = copies.start(came_hbm, came_ref)
     table_in = copies.start(table_hbm, table_ref)
-    prev_in = copies.start(prev_hbm, prev_ref)
     incr_in = copies.start(incr_hbm, incr_ref)
-    gather_lines(came_in, came_ref, lines_ref)
+    gather_lines(came_ref, lines_ref)
     table_in.wait()
     table = table_ref[...]
     out = []
@@ -419,7 +407,6 @@
         part = pl.ds(128 * i, 128)
         covar = nn(lines_ref[part], table)
         if i == 0:
-            prev_in.wait()
             incr_in.wait()
         out_ref[part] = covar + (incr_ref[part] - prev_ref[part].astype(F32))
         out.append(copies.start(out_ref.at[part], out_hbm.at[part]))
@@ -431,16 +418,20 @@
 HBM = pl.BlockSpec(memory_space=pl.ANY)
 
 
-def call(kernel, outs, ins, scratch, name, aliases=None):
-    def place(a):
-        return VMEM if a.shape[0] == 1 or (len(a.shape) == 2 and a.shape[1] < 128 and a.dtype == F32) else HBM
-
+def call(kernel, outs, ins, scratch, name, aliases=None, near=()):
+    def place(index, a):
+        small = a.shape[0] == 1 or (len(a.shape) == 2 and a.shape[1] < 128 and a.dtype == F32)
+        return VMEM if small or index in near else HBM
+
+    single = not isinstance(outs, tuple)
+    out_specs = [place(len(ins) + i, a) for i, a in enumerate((outs,) if single else outs)]
     return pl.pallas_call(
         kernel,
         out_shape=outs,
-        in_specs=[place(a) for a in ins],
-        out_specs=jax.tree.map(place, outs),
+        in_specs=[place(i, a) for i, a in enumerate(ins)],
+        out_specs=out_specs[0] if single else tuple(out_specs),
         scratch_shapes=list(scratch),
+        compiler_params=pltpu.CompilerParams(vmem_limit_bytes=52 * 1024 * 1024),
         input_output_aliases=aliases or {},
         name=name,
     )(*ins)
@@ -478,12 +469,13 @@
         edge_kernel,
         (shape(levels * 12, width), shape(levels * 12, width)),
         (mult, incr, wind),
-        [wide(6, levels, 8, width), short(levels * 12, width), short(levels * 12, width), sems(8)],
+        [wide(6, levels, 8, width), sems(6)],
         "edges",
-    )
-    flat, spec = call(
+        near=(3, 4),
+    )
+    whole, spec = call(
         start_kernel,
-        (shape(full, width), shape(width, full)),
+        (shape(full + levels * 8, width), shape(width, full)),
         (mult, table, head),
         [wide(*field), short(width, width), short(full, width), short(width, full), sems(8)],
         "start",
@@ -491,23 +483,32 @@
     ring = range(count - 1)
     head = lax.ppermute(head, "space", [(i + 1, i) for i in ring])
     tail = lax.ppermute(tail, "space", [(i, i + 1) for i in ring])
-    spec = call(order_kernel, shape(width, full), (spec, head, tail), [], "order", {0: 0})
+    spec = call(order_kernel, shape(width, full), (spec, head, tail), [], "order", {0: 0}, near=(1, 2))
     came = lax.all_to_all(spec.reshape(count, waves, full), "space", 0, 0, tiled=True)
-    coming = lax.ppermute(flat, "tm", [(t + 1, t) for t in range(times - 1)])
+    whole = call(
+        join_kernel,
+        shape(full + levels * 8, width),
+        (whole, head, tail),
+        [sems(2)],
+        "join",
+        {0: 0},
+        near=(1, 2),
+    )
+    coming = lax.ppermute(whole, "tm", [(t + 1, t) for t in range(times - 1)])
 
     across = width // 128
     stages = [wide(6, across, rows + 8, 128), wide(4, across, TILES, 8, 128)]
-    ends, far = call(
+    ends = call(
         forward_kernel,
-        (shape(full, width), shape(levels * 8, width)),
+        shape(full, width),
         (incr, wind, head, tail),
         [
-            wide(*field), wide(*field), short(levels * 8, width), short(levels * 8, width), short(levels * 8, width),
-            wide(levels * 8, width), wide(levels * 8, width), *stages, short(full, width), sems(5), sems(3, levels),
+            wide(*field), wide(*field), wide(levels * 8, width), wide(levels * 8, width), *stages,
+            short(full, width), sems(3, levels),
         ],
         "forward",
-    )
-    far = lax.ppermute(far, "tm", [(t + 1, t) for t in range(times - 1)])
+        near=(2, 3),
+    )
     previous = lax.ppermute(ends, "tm", [(t, t + 1) for t in range(times - 1)])
 
     back = call(
@@ -515,10 +516,11 @@
         shape(lat, full),
         (came, var, turned),
         [
-            short(count, waves, full), wide(full, lat), short(lat, lat), short(full, lat), short(full, lat),
+            wide(full, lat), short(lat, lat), short(full, lat), short(full, lat),
             short(lat, full), sems(16),
         ],
         "latitude",
+        near=(0,),
     )
     returned = lax.all_to_all(back.reshape(count, rows, full), "space", 0, 0, tiled=True)
 
@@ -532,24 +534,25 @@
     state_rows = call(
         backward_kernel,
         jax.ShapeDtypeStruct(field, F32),
-        (coming, far, wind, head, tail, mult, tall, cols),
+        (coming, wind, head, tail, mult, tall, cols),
         [
-            short(full, width), wide(*field), wide(*field), short(*cols.shape),
-            short(levels * 8, width), short(levels * 8, width), short(levels * 8, width),
+            wide(*field), wide(*field), short(*cols.shape),
             wide(levels * 8, width), wide(levels * 8, width), wide(levels * 8, width), wide(2, 8, width),
-            *stages, wide(full, width), wide(*field), sems(8), sems(levels),
+            *stages, wide(full, width), wide(*field), sems(3), sems(levels),
         ],
         "backward",
+        near=(0, 2, 3),
     )
     model_rows = call(
         finish_kernel,
         jax.ShapeDtypeStruct((full, width), F32),
         (returned, incr.reshape(full, width), previous, table),
         [
-            short(count, rows, full), wide(full, width), short(full, width), short(width, width),
+            wide(full, width), short(width, width),
             short(full, width), wide(full, width), sems(20),
         ],
         "finish",
+        near=(0, 2),
     )
 
     def placed(whole):

time: 78.5 us -> 67.7 us (0.86)
  the two profiles are of different devices: /device:TPU:98 before, /device:TPU:1 now
where the time goes in v4:
time: 67.7 us; the launch traced here: 66.9 us
  Pallas kernels  33 us (49%)
  starting transfers between devices  28.5 us (42%)
  waiting for transfers between devices  4.45 us (7%)
  between operations  0.85 us (1%)
    pallas_call x9, Pallas kernels, call(): pl.pallas_call(kernel, out_shape=outs, in_specs=[place(i, a) for i, a in...  33 us
    all_to_all x1, starting transfers between devices, local(): lax.all_to_all(spec.reshape(count, waves, full), 'space', 0, 0, tiled=True)  9.21 us
    all_to_all x1, starting transfers between devices, local(): lax.all_to_all(back.reshape(count, rows, full), 'space', 0, 0, tiled=True)  6.75 us
    ppermute x1, starting transfers between devices, local(): head = lax.ppermute(head, 'space', [(i + 1, i) for i in ring])  5.15 us
    ppermute x1, starting transfers between devices, local(): previous = lax.ppermute(ends, 'tm', [(t, t + 1) for t in range(times - 1)])  4.22 us
    all_to_all x1, waiting for transfers between devices, local(): lax.all_to_all(back.reshape(count, rows, full), 'space', 0, 0, tiled=True)  3.27 us
    ppermute x1, starting transfers between devices, local(): tail = lax.ppermute(tail, 'space', [(i, i + 1) for i in ring])  1.92 us
  transfers between devices with their start and end apart: 6, of which 2 were waited for; matrix products, arithmetic and copies ran while one was open for 0% of the time, Pallas kernels for 41%

profile of v4, /device:TPU:1, one launch (start us, length us, event | category | flops | bytes accessed | tf_op | source)
XLA Modules:
  0.0 66.9 jit_solution(7435847840038172651)
XLA Ops:
  0.6 1.7 %edges.1 = (bf16[144,1024]{1,0:T(8,128)(2,1)S(1)}, bf16[144,1024]{1,0:T(8,128)(2,1)S(1)}) custom-call(f32[12,32,1024]{2,1,0:T(8,128)} %bitcast.31, f32[12,32,1024]{2,1,0:T(8,128)} %bitcast.24, f32[12,32,1024]{2,1,0:T(8,128)} %bitcast.28), custom_call_target="tpu_custom_call" | custom-call | tf_op jit(solution)/shard_map/edges/pallas_call | solution.py:428
  2.3 5.1 %collective-permute-start = (bf16[144,1024]{1,0:T(8,128)(2,1)S(1)}, bf16[144,1024]{1,0:T(8,128)(2,1)S(1)}, u32[]{:S(2)}, u32[]{:S(2)}) collective-permute-start(bf16[144,1024]{1,0:T(8,128)(2,1)S(1)} %get-tuple-element.9._after), channel_id=1, source_target_pairs={{1,0},{2,1},{3,2},{4,3},{5,4},{6,5},{7,6},{8,7},{9,8},{10,9},{11,1... | collective-permute-start | bytes 884744 | tf_op jit(solution)/shard_map/ppermute | solution.py:484
  7.5 1.9 %collective-permute-start.1 = (bf16[144,1024]{1,0:T(8,128)(2,1)S(1)}, bf16[144,1024]{1,0:T(8,128)(2,1)S(1)}, u32[]{:S(2)}, u32[]{:S(2)}) collective-permute-start(bf16[144,1024]{1,0:T(8,128)(2,1)S(1)} %get-tuple-element.11), channel_id=1, source_target_pairs={{0,1},{1,2},{2,3},{3,4},{4,5},{5,6},{6,7},{7,8},{8,9},{9,10},{10,1... | collective-permute-start | bytes 884744 | tf_op jit(solution)/shard_map/ppermute | solution.py:485
  9.4 4.1 %start.1 = (bf16[480,1024]{1,0:T(8,128)(2,1)}, bf16[1024,384]{1,0:T(8,128)(2,1)}) custom-call(f32[12,32,1024]{2,1,0:T(8,128)} %bitcast.32, bf16[1024,1024]{1,0:T(8,128)(2,1)} %constant.8.clone.table_hbm, bf16[144,1024]{1,0:T(8,128)(2,1)S(1)} %get-tuple-element.9._after), custom_call_target="tpu_custom_call" | custom-call | tf_op jit(solution)/shard_map/start/pallas_call | solution.py:428
  13.6 0.0 collective-permute-done._head.head_in.head_ref
  13.6 0.0 collective-permute-done.1._tail.tail_in.tail_ref
  13.6 9.2 %all-to-all-start = ((bf16[32,32,384]{2,1,0:T(8,128)(2,1)}), bf16[32,32,384]{2,1,0:T(8,128)(2,1)S(1)}, u32[]{:S(2)}, u32[]{:S(2)}) async-start(bf16[32,32,384]{2,1,0:T(8,128)(2,1)} %bitcast.7), calls=%async_computation | async-start | bytes 1572864 | tf_op jit(solution)/shard_map/all_to_all | solution.py:487
  22.8 0.7 %join.1 = bf16[480,1024]{1,0:T(8,128)(2,1)} custom-call(bf16[480,1024]{1,0:T(8,128)(2,1)} %get-tuple-element.13._whole_in, bf16[144,1024]{1,0:T(8,128)(2,1)S(1)} %collective-permute-done._head.head_in.head_ref, bf16[144,1024]{1,0:T(8,128)(2,1)S(1)} %collective-permute-done.1._tail.tail_in.tail_ref), custom_call_target="tpu_custom_call", output_to_operand_aliasing={{}: (0, {})} | custom-call | tf_op jit(solution)/shard_map/join/pallas_call | solution.py:428
  23.5 1.3 %collective-permute-start.3 = (bf16[480,1024]{1,0:T(8,128)(2,1)}, bf16[480,1024]{1,0:T(8,128)(2,1)S(1)}, u32[]{:S(2)}, u32[]{:S(2)}) collective-permute-start(bf16[480,1024]{1,0:T(8,128)(2,1)} %join.1), channel_id=1, source_target_pairs={{32,0},{64,32},{96,64},{128,96},{160,128},{192,160},{224,192},{33,... | collective-permute-start | bytes 2949128 | tf_op jit(solution)/shard_map/ppermute | solution.py:497
  24.8 6.8 %forward.1 = bf16[384,1024]{1,0:T(8,128)(2,1)} custom-call(f32[12,32,1024]{2,1,0:T(8,128)} %bitcast.25, f32[12,32,1024]{2,1,0:T(8,128)} %bitcast.29, bf16[144,1024]{1,0:T(8,128)(2,1)S(1)} %collective-permute-done._head.head_in.head_ref, bf16[144,1024]{1,0:T(8,128)(2,1)S(1)} %collective-permute-done.1._tail.tail_in.tail_ref), custom_call_target="tpu_custom_call" | custom-call | tf_op jit(solution)/shard_map/forward/pallas_call | solution.py:428
  31.7 4.2 %collective-permute-start.2 = (bf16[384,1024]{1,0:T(8,128)(2,1)}, bf16[384,1024]{1,0:T(8,128)(2,1)S(1)}, u32[]{:S(2)}, u32[]{:S(2)}) collective-permute-start(bf16[384,1024]{1,0:T(8,128)(2,1)} %forward.1), channel_id=1, source_target_pairs={{0,32},{32,64},{64,96},{96,128},{128,160},{160,192},{192,224},{1,3... | collective-permute-start | bytes 2359304 | tf_op jit(solution)/shard_map/ppermute | solution.py:512
  35.9 1.2 %all-to-all-done.came_ref = bf16[32,32,384]{2,1,0:T(8,128)(2,1)S(1)} async-done(((bf16[32,32,384]{2,1,0:T(8,128)(2,1)}), bf16[32,32,384]{2,1,0:T(8,128)(2,1)S(1)}, u32[]{:S(2)}, u32[]{:S(2)}) %all-to-all-start) | async-done | bytes 786464 | tf_op jit(solution)/shard_map/all_to_all | solution.py:487
  37.1 4.7 %latitude.1._after = bf16[1024,384]{1,0:T(8,128)(2,1)} custom-call(bf16[32,32,384]{2,1,0:T(8,128)(2,1)S(1)} %all-to-all-done.came_ref, f32[384,1024]{1,0:T(8,128)} %bitcast.34, bf16[1024,1024]{1,0:T(8,128)(2,1)} %constant.9.clone.turned_hbm), custom_call_target="tpu_custom_call" | custom-call | tf_op jit(solution)/shard_map/latitude/pallas_call | solution.py:428
  41.8 0.0 copy-start
  41.8 0.0 copy-start.1
  41.8 0.0 copy-start.2
  41.8 0.0 copy-start.3
  41.9 0.0 copy-start.4
  41.9 6.8 %all-to-all-start.1 = ((bf16[32,32,384]{2,1,0:T(8,128)(2,1)}), bf16[32,32,384]{2,1,0:T(8,128)(2,1)S(1)}, u32[]{:S(2)}, u32[]{:S(2)}) async-start(bf16[32,32,384]{2,1,0:T(8,128)(2,1)} %bitcast.10), calls=%async_computation.1 | async-start | bytes 1572864 | tf_op jit(solution)/shard_map/all_to_all | solution.py:525
  48.7 3.2 %observe.1 = (f32[384,64]{1,0:T(8,128)S(1)}, f32[1,512]{1,0:T(1,128)}) custom-call(f32[12,32,1024]{2,1,0:T(8,128)} %bitcast.26, s32[1,512]{1,0:T(1,128)S(1)} %copy-done.2, f32[1,512]{1,0:T(1,128)S(1)} %copy-done.3, f32[1,512]{1,0:T(1,128)S(1)} %copy-done.4, bf16[1024,64]{1,0:T(8,128)(2,1)S(1)} %copy-done, bf16[96,384]{1,0:T(8,128)(2,1)S(1)} %copy-done.1, ...), custom_call_target="tpu_custom_call" | custom-call | tf_op jit(solution)/shard_map/observe/pallas_call | solution.py:428
  51.9 7.7 %backward.1 = f32[12,32,1024]{2,1,0:T(8,128)} custom-call(bf16[480,1024]{1,0:T(8,128)(2,1)S(1)} %collective-permute-done.3.coming_ref, f32[12,32,1024]{2,1,0:T(8,128)} %bitcast.30, bf16[144,1024]{1,0:T(8,128)(2,1)S(1)} %collective-permute-done._head.head_in.head_ref, bf16[144,1024]{1,0:T(8,128)(2,1)S(1)} %collective-permute-done.1._tail.tail_in.tail_ref, ...), custom_call_target="tpu_custom_call" | custom-call | tf_op jit(solution)/shard_map/backward/pallas_call | solution.py:428
  59.6 0.0 collective-permute-done.2.prev_ref
  59.6 3.3 %all-to-all-done.1.came_ref = bf16[32,32,384]{2,1,0:T(8,128)(2,1)S(1)} async-done(((bf16[32,32,384]{2,1,0:T(8,128)(2,1)}), bf16[32,32,384]{2,1,0:T(8,128)(2,1)S(1)}, u32[]{:S(2)}, u32[]{:S(2)}) %all-to-all-start.1) | async-done | bytes 786464 | tf_op jit(solution)/shard_map/all_to_all | solution.py:525
  62.8 4.0 %finish.1 = f32[384,1024]{1,0:T(8,128)} custom-call(bf16[32,32,384]{2,1,0:T(8,128)(2,1)S(1)} %all-to-all-done.1.came_ref, f32[384,1024]{1,0:T(8,128)} %bitcast.27, bf16[384,1024]{1,0:T(8,128)(2,1)S(1)} %collective-permute-done.2.prev_ref, bf16[1024,1024]{1,0:T(8,128)(2,1)} %constant.8.clone.table_hbm), custom_call_target="tpu_custom_call" | custom-call | tf_op jit(solution)/shard_map/finish/pallas_call | solution.py:428
  (7 shorter events, 0.0 us)
Async XLA Ops:
  2.3 11.2 %collective-permute-start = (bf16[144,1024]{1,0:T(8,128)(2,1)S(1)}, bf16[144,1024]{1,0:T(8,128)(2,1)S(1)}, u32[]{:S(2)}, u32[]{:S(2)}) collective-permute-start(bf16[144,1024]{1,0:T(8,128)(2,1)S(1)} %get-tuple-element.9._after), channel_id=1, source_target_pairs={{1,0},{2,1},{3,2},{4,3},{5,4},{6,5},{7,6},{8,7},{9,8},{10,9},{11,1... | collective-permute-start | bytes 884744 | tf_op jit(solution)/shard_map/ppermute | solution.py:484
  7.5 6.1 %collective-permute-start.1 = (bf16[144,1024]{1,0:T(8,128)(2,1)S(1)}, bf16[144,1024]{1,0:T(8,128)(2,1)S(1)}, u32[]{:S(2)}, u32[]{:S(2)}) collective-permute-start(bf16[144,1024]{1,0:T(8,128)(2,1)S(1)} %get-tuple-element.11), channel_id=1, source_target_pairs={{0,1},{1,2},{2,3},{3,4},{4,5},{5,6},{6,7},{7,8},{8,9},{9,10},{10,1... | collective-permute-start | bytes 884744 | tf_op jit(solution)/shard_map/ppermute | solution.py:485
  13.6 23.4 %all-to-all-start = ((bf16[32,32,384]{2,1,0:T(8,128)(2,1)}), bf16[32,32,384]{2,1,0:T(8,128)(2,1)S(1)}, u32[]{:S(2)}, u32[]{:S(2)}) async-start(bf16[32,32,384]{2,1,0:T(8,128)(2,1)} %bitcast.7), calls=%async_computation | async-start | bytes 1572864 | tf_op jit(solution)/shard_map/all_to_all | solution.py:487
  23.5 28.4 %collective-permute-start.3 = (bf16[480,1024]{1,0:T(8,128)(2,1)}, bf16[480,1024]{1,0:T(8,128)(2,1)S(1)}, u32[]{:S(2)}, u32[]{:S(2)}) collective-permute-start(bf16[480,1024]{1,0:T(8,128)(2,1)} %join.1), channel_id=1, source_target_pairs={{32,0},{64,32},{96,64},{128,96},{160,128},{192,160},{224,192},{33,... | collective-permute-start | bytes 2949128 | tf_op jit(solution)/shard_map/ppermute | solution.py:497
  31.7 27.9 %collective-permute-start.2 = (bf16[384,1024]{1,0:T(8,128)(2,1)}, bf16[384,1024]{1,0:T(8,128)(2,1)S(1)}, u32[]{:S(2)}, u32[]{:S(2)}) collective-permute-start(bf16[384,1024]{1,0:T(8,128)(2,1)} %forward.1), channel_id=1, source_target_pairs={{0,32},{32,64},{64,96},{96,128},{128,160},{160,192},{192,224},{1,3... | collective-permute-start | bytes 2359304 | tf_op jit(solution)/shard_map/ppermute | solution.py:512
  41.8 6.8 %copy-start = (bf16[1024,64]{1,0:T(8,128)(2,1)S(1)}, bf16[1024,64]{1,0:T(8,128)(2,1)}, u32[]{:S(2)}) copy-start(bf16[1024,64]{1,0:T(8,128)(2,1)} %constant.10.clone.cols_hbm) | copy-start | bytes 393220
  41.8 6.8 %copy-start.1 = (bf16[96,384]{1,0:T(8,128)(2,1)S(1)}, bf16[96,384]{1,0:T(8,128)(2,1)}, u32[]{:S(2)}) copy-start(bf16[96,384]{1,0:T(8,128)(2,1)} %constant.11.clone.lines_hbm) | copy-start | bytes 221188
  41.8 6.8 %copy-start.2 = (s32[1,512]{1,0:T(1,128)S(1)}, s32[1,512]{1,0:T(1,128)}, u32[]{:S(2)}) copy-start(s32[1,512]{1,0:T(1,128)} %index_ref.1) | copy-start | bytes 6148
  41.8 6.8 %copy-start.3 = (f32[1,512]{1,0:T(1,128)S(1)}, f32[1,512]{1,0:T(1,128)}, u32[]{:S(2)}) copy-start(f32[1,512]{1,0:T(1,128)} %dual_ref.1) | copy-start | bytes 6148
  41.9 6.8 %copy-start.4 = (f32[1,512]{1,0:T(1,128)S(1)}, f32[1,512]{1,0:T(1,128)}, u32[]{:S(2)}) copy-start(f32[1,512]{1,0:T(1,128)} %variance_ref.1) | copy-start | bytes 6148
  41.9 21.0 %all-to-all-start.1 = ((bf16[32,32,384]{2,1,0:T(8,128)(2,1)}), bf16[32,32,384]{2,1,0:T(8,128)(2,1)S(1)}, u32[]{:S(2)}, u32[]{:S(2)}) async-start(bf16[32,32,384]{2,1,0:T(8,128)(2,1)} %bitcast.10), calls=%async_computation.1 | async-start | bytes 1572864 | tf_op jit(solution)/shard_map/all_to_all | solution.py:525

commit v5 on v4

--- a/solution.py
+++ b/solution.py
@@ -89,18 +89,15 @@
         part_ref[levels * 8 :] = dual.reshape(half * 8, width).astype(BF16)
 
 
-def start_kernel(mult_hbm, table_hbm, _after, whole_hbm, spec_hbm, mult_ref, table_ref, flat_ref, spec_ref, sems):
+def start_kernel(mult_ref, table_ref, _after, whole_hbm, spec_hbm, flat_ref, spec_ref, sems):
     levels, rows, width = mult_ref.shape
     copies = Copies(sems)
-    mult_in = copies.start(mult_hbm, mult_ref)
-    table_in = copies.start(table_hbm, table_ref)
-    mult_in.wait()
-    flat_ref[...] = mult_ref[...].reshape(levels * rows, width).astype(BF16)
+    half = table_ref.shape[0] // 2
+    flat = mult_ref[...].reshape(levels * rows, width).astype(BF16)
+    flat_ref[...] = flat
     out = [copies.start(flat_ref, whole_hbm.at[pl.ds(0, levels * rows)])]
-    flat = flat_ref[...]
-    table_in.wait()
     for i in range(2):
-        part = pl.ds(512 * i, 512)
+        part = pl.ds(half * i, half)
         spec_ref[part] = nt(table_ref[part], flat).astype(BF16)
         out.append(copies.start(spec_ref.at[part], spec_hbm.at[part]))
     for copy in out:
@@ -418,7 +415,7 @@
 HBM = pl.BlockSpec(memory_space=pl.ANY)
 
 
-def call(kernel, outs, ins, scratch, name, aliases=None, near=()):
+def call(kernel, outs, ins, scratch, name, aliases=None, near=(), grant=52):
     def place(index, a):
         small = a.shape[0] == 1 or (len(a.shape) == 2 and a.shape[1] < 128 and a.dtype == F32)
         return VMEM if small or index in near else HBM
@@ -431,7 +428,7 @@
         in_specs=[place(i, a) for i, a in enumerate(ins)],
         out_specs=out_specs[0] if single else tuple(out_specs),
         scratch_shapes=list(scratch),
-        compiler_params=pltpu.CompilerParams(vmem_limit_bytes=52 * 1024 * 1024),
+        compiler_params=pltpu.CompilerParams(vmem_limit_bytes=grant * 1024 * 1024),
         input_output_aliases=aliases or {},
         name=name,
     )(*ins)
@@ -472,13 +469,16 @@
         [wide(6, levels, 8, width), sems(6)],
         "edges",
         near=(3, 4),
+        grant=52,
     )
     whole, spec = call(
         start_kernel,
         (shape(full + levels * 8, width), shape(width, full)),
         (mult, table, head),
-        [wide(*field), short(width, width), short(full, width), short(width, full), sems(8)],
+        [short(full, width), short(width, full), sems(3)],
         "start",
+        near=(0,1,2),
+        grant=40,
     )
     ring = range(count - 1)
     head = lax.ppermute(head, "space", [(i + 1, i) for i in ring])

time: 67.7 us -> 67.8 us (level)
  Pallas kernels: 33 us -> 31 us
  waiting for transfers between devices: 4.45 us -> 6.02 us
    pallas_call x9, Pallas kernels: 33 us -> 31 us  [call(): pl.pallas_call(kernel, out_shape=outs, in_specs=[place(i, a) for i, a in...]
    ppermute x1, waiting for transfers between devices: 0.01 us -> 1.56 us  [local(): tail = lax.ppermute(tail, 'space', [(i, i + 1) for i in ring])]
  transfers between devices with their start and end apart: 6 -> 6, of which waited for: 2 -> 3; matrix products, arithmetic and copies ran while one was open for 0% -> 0% of each run, Pallas kernels for 41% -> 38%
where the time goes in v5:
time: 67.8 us; the launch traced here: 67 us
  Pallas kernels  31 us (46%)
  starting transfers between devices  29.1 us (43%)
  waiting for transfers between devices  6.02 us (9%)
  between operations  0.87 us (1%)
    pallas_call x9, Pallas kernels, call(): pl.pallas_call(kernel, out_shape=outs, in_specs=[place(i, a) for i, a in...  31 us
    all_to_all x1, starting transfers between devices, local(): lax.all_to_all(spec.reshape(count, waves, full), 'space', 0, 0, tiled=True)  9.75 us
    all_to_all x1, starting transfers between devices, local(): lax.all_to_all(back.reshape(count, rows, full), 'space', 0, 0, tiled=True)  6.73 us
    ppermute x1, starting transfers between devices, local(): head = lax.ppermute(head, 'space', [(i + 1, i) for i in ring])  5.15 us
    ppermute x1, starting transfers between devices, local(): previous = lax.ppermute(ends, 'tm', [(t, t + 1) for t in range(times - 1)])  4.22 us
    all_to_all x1, waiting for transfers between devices, local(): lax.all_to_all(back.reshape(count, rows, full), 'space', 0, 0, tiled=True)  3.27 us
    ppermute x1, starting transfers between devices, local(): tail = lax.ppermute(tail, 'space', [(i, i + 1) for i in ring])  1.92 us
    ppermute x1, waiting for transfers between devices, local(): tail = lax.ppermute(tail, 'space', [(i, i + 1) for i in ring])  1.56 us
  transfers between devices with their start and end apart: 6, of which 3 were waited for; matrix products, arithmetic and copies ran while one was open for 0% of the time, Pallas kernels for 38%

profile of v5, /device:TPU:1, one launch (start us, length us, event | category | flops | bytes accessed | tf_op | source)
XLA Modules:
  0.0 67.0 jit_solution(8567491989799894033)
XLA Ops:
  0.6 0.0 copy-start
  0.6 0.0 copy-start.1
  0.7 1.9 %edges.1 = (bf16[144,1024]{1,0:T(8,128)(2,1)S(1)}, bf16[144,1024]{1,0:T(8,128)(2,1)S(1)}) custom-call(f32[12,32,1024]{2,1,0:T(8,128)} %bitcast.24, f32[12,32,1024]{2,1,0:T(8,128)} %bitcast.27, f32[12,32,1024]{2,1,0:T(8,128)} %bitcast.31), custom_call_target="tpu_custom_call" | custom-call | tf_op jit(solution)/shard_map/edges/pallas_call | solution.py:425
  2.5 5.1 %collective-permute-start = (bf16[144,1024]{1,0:T(8,128)(2,1)S(1)}, bf16[144,1024]{1,0:T(8,128)(2,1)S(1)}, u32[]{:S(2)}, u32[]{:S(2)}) collective-permute-start(bf16[144,1024]{1,0:T(8,128)(2,1)S(1)} %get-tuple-element.9._after), channel_id=1, source_target_pairs={{1,0},{2,1},{3,2},{4,3},{5,4},{6,5},{7,6},{8,7},{9,8},{10,9},{11,1... | collective-permute-start | bytes 884744 | tf_op jit(solution)/shard_map/ppermute | solution.py:484
  7.7 1.9 %collective-permute-start.1 = (bf16[144,1024]{1,0:T(8,128)(2,1)S(1)}, bf16[144,1024]{1,0:T(8,128)(2,1)S(1)}, u32[]{:S(2)}, u32[]{:S(2)}) collective-permute-start(bf16[144,1024]{1,0:T(8,128)(2,1)S(1)} %get-tuple-element.11), channel_id=1, source_target_pairs={{0,1},{1,2},{2,3},{3,4},{4,5},{5,6},{6,7},{7,8},{8,9},{9,10},{10,1... | collective-permute-start | bytes 884744 | tf_op jit(solution)/shard_map/ppermute | solution.py:485
  9.6 2.0 %start.1 = (bf16[480,1024]{1,0:T(8,128)(2,1)}, bf16[1024,384]{1,0:T(8,128)(2,1)}) custom-call(f32[12,32,1024]{2,1,0:T(8,128)S(1)} %bitcast.26, bf16[1024,1024]{1,0:T(8,128)(2,1)S(1)} %copy-done.1, bf16[144,1024]{1,0:T(8,128)(2,1)S(1)} %get-tuple-element.9._after), custom_call_target="tpu_custom_call" | custom-call | tf_op jit(solution)/shard_map/start/pallas_call | solution.py:425
  11.7 1.6 %collective-permute-done.1._tail.tail_in.tail_ref = bf16[144,1024]{1,0:T(8,128)(2,1)S(1)} collective-permute-done((bf16[144,1024]{1,0:T(8,128)(2,1)S(1)}, bf16[144,1024]{1,0:T(8,128)(2,1)S(1)}, u32[]{:S(2)}, u32[]{:S(2)}) %collective-permute-start.1) | collective-permute-done | bytes 294944 | tf_op jit(solution)/shard_map/ppermute | solution.py:485
  13.2 9.8 %all-to-all-start = ((bf16[32,32,384]{2,1,0:T(8,128)(2,1)}), bf16[32,32,384]{2,1,0:T(8,128)(2,1)S(1)}, u32[]{:S(2)}, u32[]{:S(2)}) async-start(bf16[32,32,384]{2,1,0:T(8,128)(2,1)} %bitcast.7), calls=%async_computation | async-start | bytes 1572864 | tf_op jit(solution)/shard_map/all_to_all | solution.py:487
  23.0 0.7 %join.1 = bf16[480,1024]{1,0:T(8,128)(2,1)} custom-call(bf16[480,1024]{1,0:T(8,128)(2,1)} %get-tuple-element.13._whole_in, bf16[144,1024]{1,0:T(8,128)(2,1)S(1)} %collective-permute-done._head.head_in.head_ref, bf16[144,1024]{1,0:T(8,128)(2,1)S(1)} %collective-permute-done.1._tail.tail_in.tail_ref), custom_call_target="tpu_custom_call", output_to_operand_aliasing={{}: (0, {})} | custom-call | tf_op jit(solution)/shard_map/join/pallas_call | solution.py:425
  23.7 1.3 %collective-permute-start.3 = (bf16[480,1024]{1,0:T(8,128)(2,1)}, bf16[480,1024]{1,0:T(8,128)(2,1)S(1)}, u32[]{:S(2)}, u32[]{:S(2)}) collective-permute-start(bf16[480,1024]{1,0:T(8,128)(2,1)} %join.1), channel_id=1, source_target_pairs={{32,0},{64,32},{96,64},{128,96},{160,128},{192,160},{224,192},{33,... | collective-permute-start | bytes 2949128 | tf_op jit(solution)/shard_map/ppermute | solution.py:497
  25.0 6.8 %forward.1 = bf16[384,1024]{1,0:T(8,128)(2,1)} custom-call(f32[12,32,1024]{2,1,0:T(8,128)} %bitcast.28, f32[12,32,1024]{2,1,0:T(8,128)} %bitcast.32, bf16[144,1024]{1,0:T(8,128)(2,1)S(1)} %collective-permute-done._head.head_in.head_ref, bf16[144,1024]{1,0:T(8,128)(2,1)S(1)} %collective-permute-done.1._tail.tail_in.tail_ref), custom_call_target="tpu_custom_call" | custom-call | tf_op jit(solution)/shard_map/forward/pallas_call | solution.py:425
  31.8 4.2 %collective-permute-start.2 = (bf16[384,1024]{1,0:T(8,128)(2,1)}, bf16[384,1024]{1,0:T(8,128)(2,1)S(1)}, u32[]{:S(2)}, u32[]{:S(2)}) collective-permute-start(bf16[384,1024]{1,0:T(8,128)(2,1)} %forward.1), channel_id=1, source_target_pairs={{0,32},{32,64},{64,96},{96,128},{128,160},{160,192},{192,224},{1,3... | collective-permute-start | bytes 2359304 | tf_op jit(solution)/shard_map/ppermute | solution.py:512
  36.0 1.2 %all-to-all-done.came_ref = bf16[32,32,384]{2,1,0:T(8,128)(2,1)S(1)} async-done(((bf16[32,32,384]{2,1,0:T(8,128)(2,1)}), bf16[32,32,384]{2,1,0:T(8,128)(2,1)S(1)}, u32[]{:S(2)}, u32[]{:S(2)}) %all-to-all-start) | async-done | bytes 786464 | tf_op jit(solution)/shard_map/all_to_all | solution.py:487
  37.2 4.7 %latitude.1._after = bf16[1024,384]{1,0:T(8,128)(2,1)} custom-call(bf16[32,32,384]{2,1,0:T(8,128)(2,1)S(1)} %all-to-all-done.came_ref, f32[384,1024]{1,0:T(8,128)} %bitcast.34, bf16[1024,1024]{1,0:T(8,128)(2,1)} %constant.9.clone.turned_hbm), custom_call_target="tpu_custom_call" | custom-call | tf_op jit(solution)/shard_map/latitude/pallas_call | solution.py:425
  42.0 0.0 copy-start.2
  42.0 0.0 copy-start.3
  42.0 0.0 copy-start.4
  42.0 0.0 copy-start.5
  42.0 0.0 copy-start.6
  42.0 6.7 %all-to-all-start.1 = ((bf16[32,32,384]{2,1,0:T(8,128)(2,1)}), bf16[32,32,384]{2,1,0:T(8,128)(2,1)S(1)}, u32[]{:S(2)}, u32[]{:S(2)}) async-start(bf16[32,32,384]{2,1,0:T(8,128)(2,1)} %bitcast.10), calls=%async_computation.1 | async-start | bytes 1572864 | tf_op jit(solution)/shard_map/all_to_all | solution.py:525
  48.8 3.2 %observe.1 = (f32[384,64]{1,0:T(8,128)S(1)}, f32[1,512]{1,0:T(1,128)}) custom-call(f32[12,32,1024]{2,1,0:T(8,128)} %bitcast.29, s32[1,512]{1,0:T(1,128)S(1)} %copy-done.4, f32[1,512]{1,0:T(1,128)S(1)} %copy-done.5, f32[1,512]{1,0:T(1,128)S(1)} %copy-done.6, bf16[1024,64]{1,0:T(8,128)(2,1)S(1)} %copy-done.2, bf16[96,384]{1,0:T(8,128)(2,1)S(1)} %copy-done.3, ...), custom_call_target="tpu_custom_call" | custom-call | tf_op jit(solution)/shard_map/observe/pallas_call | solution.py:425
  52.1 7.7 %backward.1 = f32[12,32,1024]{2,1,0:T(8,128)} custom-call(bf16[480,1024]{1,0:T(8,128)(2,1)S(1)} %collective-permute-done.3.coming_ref, f32[12,32,1024]{2,1,0:T(8,128)} %bitcast.33, bf16[144,1024]{1,0:T(8,128)(2,1)S(1)} %collective-permute-done._head.head_in.head_ref, bf16[144,1024]{1,0:T(8,128)(2,1)S(1)} %collective-permute-done.1._tail.tail_in.tail_ref, ...), custom_call_target="tpu_custom_call" | custom-call | tf_op jit(solution)/shard_map/backward/pallas_call | solution.py:425
  59.7 3.3 %all-to-all-done.1.came_ref = bf16[32,32,384]{2,1,0:T(8,128)(2,1)S(1)} async-done(((bf16[32,32,384]{2,1,0:T(8,128)(2,1)}), bf16[32,32,384]{2,1,0:T(8,128)(2,1)S(1)}, u32[]{:S(2)}, u32[]{:S(2)}) %all-to-all-start.1) | async-done | bytes 786464 | tf_op jit(solution)/shard_map/all_to_all | solution.py:525
  63.0 4.0 %finish.1 = f32[384,1024]{1,0:T(8,128)} custom-call(bf16[32,32,384]{2,1,0:T(8,128)(2,1)S(1)} %all-to-all-done.1.came_ref, f32[384,1024]{1,0:T(8,128)} %bitcast.30, bf16[384,1024]{1,0:T(8,128)(2,1)S(1)} %collective-permute-done.2.prev_ref, bf16[1024,1024]{1,0:T(8,128)(2,1)} %constant.8.clone.table_ref.table_hbm), custom_call_target="tpu_custom_call" | custom-call | tf_op jit(solution)/shard_map/finish/pallas_call | solution.py:425
  (11 shorter events, 0.0 us)
Async XLA Ops:
  0.6 9.0 %copy-start = (f32[1,32,12,1024]{3,1,2,0:T(8,128)S(1)}, f32[1,32,12,1024]{3,1,2,0:T(8,128)}, u32[]{:S(2)}) copy-start(f32[1,32,12,1024]{3,1,2,0:T(8,128)} %param.12) | copy-start | bytes 4718596
  0.6 9.0 %copy-start.1 = (bf16[1024,1024]{1,0:T(8,128)(2,1)S(1)}, bf16[1024,1024]{1,0:T(8,128)(2,1)}, u32[]{:S(2)}) copy-start(bf16[1024,1024]{1,0:T(8,128)(2,1)} %constant.8.clone.table_ref.table_hbm) | copy-start | bytes 6291460
  2.5 9.2 %collective-permute-start = (bf16[144,1024]{1,0:T(8,128)(2,1)S(1)}, bf16[144,1024]{1,0:T(8,128)(2,1)S(1)}, u32[]{:S(2)}, u32[]{:S(2)}) collective-permute-start(bf16[144,1024]{1,0:T(8,128)(2,1)S(1)} %get-tuple-element.9._after), channel_id=1, source_target_pairs={{1,0},{2,1},{3,2},{4,3},{5,4},{6,5},{7,6},{8,7},{9,8},{10,9},{11,1... | collective-permute-start | bytes 884744 | tf_op jit(solution)/shard_map/ppermute | solution.py:484
  7.7 5.6 %collective-permute-start.1 = (bf16[144,1024]{1,0:T(8,128)(2,1)S(1)}, bf16[144,1024]{1,0:T(8,128)(2,1)S(1)}, u32[]{:S(2)}, u32[]{:S(2)}) collective-permute-start(bf16[144,1024]{1,0:T(8,128)(2,1)S(1)} %get-tuple-element.11), channel_id=1, source_target_pairs={{0,1},{1,2},{2,3},{3,4},{4,5},{5,6},{6,7},{7,8},{8,9},{9,10},{10,1... | collective-permute-start | bytes 884744 | tf_op jit(solution)/shard_map/ppermute | solution.py:485
  13.2 24.0 %all-to-all-start = ((bf16[32,32,384]{2,1,0:T(8,128)(2,1)}), bf16[32,32,384]{2,1,0:T(8,128)(2,1)S(1)}, u32[]{:S(2)}, u32[]{:S(2)}) async-start(bf16[32,32,384]{2,1,0:T(8,128)(2,1)} %bitcast.7), calls=%async_computation | async-start | bytes 1572864 | tf_op jit(solution)/shard_map/all_to_all | solution.py:487
  23.7 28.3 %collective-permute-start.3 = (bf16[480,1024]{1,0:T(8,128)(2,1)}, bf16[480,1024]{1,0:T(8,128)(2,1)S(1)}, u32[]{:S(2)}, u32[]{:S(2)}) collective-permute-start(bf16[480,1024]{1,0:T(8,128)(2,1)} %join.1), channel_id=1, source_target_pairs={{32,0},{64,32},{96,64},{128,96},{160,128},{192,160},{224,192},{33,... | collective-permute-start | bytes 2949128 | tf_op jit(solution)/shard_map/ppermute | solution.py:497
  31.8 27.9 %collective-permute-start.2 = (bf16[384,1024]{1,0:T(8,128)(2,1)}, bf16[384,1024]{1,0:T(8,128)(2,1)S(1)}, u32[]{:S(2)}, u32[]{:S(2)}) collective-permute-start(bf16[384,1024]{1,0:T(8,128)(2,1)} %forward.1), channel_id=1, source_target_pairs={{0,32},{32,64},{64,96},{96,128},{128,160},{160,192},{192,224},{1,3... | collective-permute-start | bytes 2359304 | tf_op jit(solution)/shard_map/ppermute | solution.py:512
  42.0 6.8 %copy-start.2 = (bf16[1024,64]{1,0:T(8,128)(2,1)S(1)}, bf16[1024,64]{1,0:T(8,128)(2,1)}, u32[]{:S(2)}) copy-start(bf16[1024,64]{1,0:T(8,128)(2,1)} %constant.10.clone.cols_hbm) | copy-start | bytes 393220
  42.0 6.8 %copy-start.3 = (bf16[96,384]{1,0:T(8,128)(2,1)S(1)}, bf16[96,384]{1,0:T(8,128)(2,1)}, u32[]{:S(2)}) copy-start(bf16[96,384]{1,0:T(8,128)(2,1)} %constant.11.clone.lines_hbm) | copy-start | bytes 221188
  42.0 6.8 %copy-start.4 = (s32[1,512]{1,0:T(1,128)S(1)}, s32[1,512]{1,0:T(1,128)}, u32[]{:S(2)}) copy-start(s32[1,512]{1,0:T(1,128)} %index_ref.1) | copy-start | bytes 6148
  42.0 6.8 %copy-start.5 = (f32[1,512]{1,0:T(1,128)S(1)}, f32[1,512]{1,0:T(1,128)}, u32[]{:S(2)}) copy-start(f32[1,512]{1,0:T(1,128)} %dual_ref.1) | copy-start | bytes 6148
  42.0 6.8 %copy-start.6 = (f32[1,512]{1,0:T(1,128)S(1)}, f32[1,512]{1,0:T(1,128)}, u32[]{:S(2)}) copy-start(f32[1,512]{1,0:T(1,128)} %variance_ref.1) | copy-start | bytes 6148
  42.0 21.0 %all-to-all-start.1 = ((bf16[32,32,384]{2,1,0:T(8,128)(2,1)}), bf16[32,32,384]{2,1,0:T(8,128)(2,1)S(1)}, u32[]{:S(2)}, u32[]{:S(2)}) async-start(bf16[32,32,384]{2,1,0:T(8,128)(2,1)} %bitcast.10), calls=%async_computation.1 | async-start | bytes 1572864 | tf_op jit(solution)/shard_map/all_to_all | solution.py:525

commit v6 on v5

--- a/solution.py
+++ b/solution.py
@@ -152,15 +152,16 @@
     u = extended(level, stage_ref.at[0])
     v = extended(level + levels // 2, stage_ref.at[1])
     place = lax.axis_index("space")
-    first = (sublane == 0) & (place == 0)
-    last = (sublane == (rows - 1) // TILES) & (place == lax.axis_size("space") - 1)
+    start, end = place == 0, place == lax.axis_size("space") - 1
+
+    def cut(value, row, t, edge):
+        return jnp.where((sublane == row // TILES) & edge, 0.0, value) if t == row % TILES else value
+
     for c in range(len(u)):
         for t in range(TILES):
             north, south = 1.0 - v[c][t], 1.0 + v[c][t]
-            if t == (rows - 1) % TILES:
-                north = jnp.where(last, 0.0, north)
-            if t == 0:
-                south = jnp.where(first, 0.0, south)
+            north = cut(cut(north, rows - 1, t, end), rows + 7, t, start)
+            south = cut(cut(south, 0, t, start), rows, t, end)
             coef_ref[0, c, t] = 1.0 - u[c][t]
             coef_ref[1, c, t] = 1.0 + u[c][t]
             coef_ref[2, c, t] = north
@@ -480,9 +481,9 @@
         near=(0,1,2),
         grant=40,
     )
-    ring = range(count - 1)
-    head = lax.ppermute(head, "space", [(i + 1, i) for i in ring])
-    tail = lax.ppermute(tail, "space", [(i, i + 1) for i in ring])
+    ring = [(i, (i + 1) % count) for i in range(count)]
+    head = lax.ppermute(head, "space", [(b, a) for a, b in ring])
+    tail = lax.ppermute(tail, "space", ring)
     spec = call(order_kernel, shape(width, full), (spec, head, tail), [], "order", {0: 0}, near=(1, 2))
     came = lax.all_to_all(spec.reshape(count, waves, full), "space", 0, 0, tiled=True)
     whole = call(

time: 67.8 us -> 66.6 us (0.982)
  starting transfers between devices: 29.1 us -> 27.5 us
    ppermute x2, starting transfers between devices: 7.07 us -> 3.32 us  [the longest x1 3.32 us: local(): head = lax.ppermute(head, 'space', [(b, a) for a, b in ring])]
    all_to_all x1, starting transfers between devices: 9.75 us -> 12 us  [local(): lax.all_to_all(spec.reshape(count, waves, full), 'space', 0, 0, tiled=True)]
  transfers between devices with their start and end apart: 6 -> 6, of which waited for: 3 -> 4; matrix products, arithmetic and copies ran while one was open for 0% -> 0% of each run, Pallas kernels for 38% -> 38%
where the time goes in v6:
time: 66.6 us; the launch traced here: 65.9 us
  Pallas kernels  31 us (47%)
  starting transfers between devices  27.5 us (41%)
  waiting for transfers between devices  6.48 us (10%)
  between operations  0.83 us (1%)
    pallas_call x9, Pallas kernels, call(): pl.pallas_call(kernel, out_shape=outs, in_specs=[place(i, a) for i, a in...  31 us
    all_to_all x1, starting transfers between devices, local(): lax.all_to_all(spec.reshape(count, waves, full), 'space', 0, 0, tiled=True)  12 us
    all_to_all x1, starting transfers between devices, local(): lax.all_to_all(back.reshape(count, rows, full), 'space', 0, 0, tiled=True)  6.74 us
    ppermute x1, starting transfers between devices, local(): previous = lax.ppermute(ends, 'tm', [(t, t + 1) for t in range(times - 1)])  4.22 us
    ppermute x1, starting transfers between devices, local(): head = lax.ppermute(head, 'space', [(b, a) for a, b in ring])  3.32 us
    all_to_all x1, waiting for transfers between devices, local(): lax.all_to_all(back.reshape(count, rows, full), 'space', 0, 0, tiled=True)  3.28 us
    ppermute x1, waiting for transfers between devices, local(): head = lax.ppermute(head, 'space', [(b, a) for a, b in ring])  1.78 us
  transfers between devices with their start and end apart: 6, of which 4 were waited for; matrix products, arithmetic and copies ran while one was open for 0% of the time, Pallas kernels for 38%

profile of v6, /device:TPU:1, one launch (start us, length us, event | category | flops | bytes accessed | tf_op | source)
XLA Modules:
  0.0 65.9 jit_solution(16685118481672247244)
XLA Ops:
  0.6 0.0 copy-start
  0.6 0.0 copy-start.1
  0.7 1.9 %edges.1 = (bf16[144,1024]{1,0:T(8,128)(2,1)S(1)}, bf16[144,1024]{1,0:T(8,128)(2,1)S(1)}) custom-call(f32[12,32,1024]{2,1,0:T(8,128)} %bitcast.24, f32[12,32,1024]{2,1,0:T(8,128)} %bitcast.27, f32[12,32,1024]{2,1,0:T(8,128)} %bitcast.31), custom_call_target="tpu_custom_call" | custom-call | tf_op jit(solution)/shard_map/edges/pallas_call | solution.py:426
  2.5 3.3 %collective-permute-start = (bf16[144,1024]{1,0:T(8,128)(2,1)S(1)}, bf16[144,1024]{1,0:T(8,128)(2,1)S(1)}, u32[]{:S(2)}, u32[]{:S(2)}) collective-permute-start(bf16[144,1024]{1,0:T(8,128)(2,1)S(1)} %get-tuple-element.9._after), channel_id=1, source_target_pairs={{1,0},{2,1},{3,2},{4,3},{5,4},{6,5},{7,6},{8,7},{9,8},{10,9},{11,1... | collective-permute-start | bytes 884744 | tf_op jit(solution)/shard_map/ppermute | solution.py:485
  5.8 2.1 %start.1 = (bf16[480,1024]{1,0:T(8,128)(2,1)}, bf16[1024,384]{1,0:T(8,128)(2,1)}) custom-call(f32[12,32,1024]{2,1,0:T(8,128)S(1)} %bitcast.26, bf16[1024,1024]{1,0:T(8,128)(2,1)S(1)} %copy-done.1, bf16[144,1024]{1,0:T(8,128)(2,1)S(1)} %get-tuple-element.9._after), custom_call_target="tpu_custom_call" | custom-call | tf_op jit(solution)/shard_map/start/pallas_call | solution.py:426
  7.9 1.8 %collective-permute-done._head.head_in.head_ref = bf16[144,1024]{1,0:T(8,128)(2,1)S(1)} collective-permute-done((bf16[144,1024]{1,0:T(8,128)(2,1)S(1)}, bf16[144,1024]{1,0:T(8,128)(2,1)S(1)}, u32[]{:S(2)}, u32[]{:S(2)}) %collective-permute-start) | collective-permute-done | bytes 294944 | tf_op jit(solution)/shard_map/ppermute | solution.py:485
  9.7 0.1 collective-permute-done.1._tail.tail_in.tail_ref
  9.8 12.0 %all-to-all-start = ((bf16[32,32,384]{2,1,0:T(8,128)(2,1)}), bf16[32,32,384]{2,1,0:T(8,128)(2,1)S(1)}, u32[]{:S(2)}, u32[]{:S(2)}) async-start(bf16[32,32,384]{2,1,0:T(8,128)(2,1)} %bitcast.7), calls=%async_computation | async-start | bytes 1572864 | tf_op jit(solution)/shard_map/all_to_all | solution.py:488
  21.8 0.7 %join.1 = bf16[480,1024]{1,0:T(8,128)(2,1)} custom-call(bf16[480,1024]{1,0:T(8,128)(2,1)} %get-tuple-element.13._whole_in, bf16[144,1024]{1,0:T(8,128)(2,1)S(1)} %collective-permute-done._head.head_in.head_ref, bf16[144,1024]{1,0:T(8,128)(2,1)S(1)} %collective-permute-done.1._tail.tail_in.tail_ref), custom_call_target="tpu_custom_call", output_to_operand_aliasing={{}: (0, {})} | custom-call | tf_op jit(solution)/shard_map/join/pallas_call | solution.py:426
  22.5 1.3 %collective-permute-start.3 = (bf16[480,1024]{1,0:T(8,128)(2,1)}, bf16[480,1024]{1,0:T(8,128)(2,1)S(1)}, u32[]{:S(2)}, u32[]{:S(2)}) collective-permute-start(bf16[480,1024]{1,0:T(8,128)(2,1)} %join.1), channel_id=1, source_target_pairs={{32,0},{64,32},{96,64},{128,96},{160,128},{192,160},{224,192},{33,... | collective-permute-start | bytes 2949128 | tf_op jit(solution)/shard_map/ppermute | solution.py:498
  23.8 6.8 %forward.1 = bf16[384,1024]{1,0:T(8,128)(2,1)} custom-call(f32[12,32,1024]{2,1,0:T(8,128)} %bitcast.28, f32[12,32,1024]{2,1,0:T(8,128)} %bitcast.32, bf16[144,1024]{1,0:T(8,128)(2,1)S(1)} %collective-permute-done._head.head_in.head_ref, bf16[144,1024]{1,0:T(8,128)(2,1)S(1)} %collective-permute-done.1._tail.tail_in.tail_ref), custom_call_target="tpu_custom_call" | custom-call | tf_op jit(solution)/shard_map/forward/pallas_call | solution.py:426
  30.6 4.2 %collective-permute-start.2 = (bf16[384,1024]{1,0:T(8,128)(2,1)}, bf16[384,1024]{1,0:T(8,128)(2,1)S(1)}, u32[]{:S(2)}, u32[]{:S(2)}) collective-permute-start(bf16[384,1024]{1,0:T(8,128)(2,1)} %forward.1), channel_id=1, source_target_pairs={{0,32},{32,64},{64,96},{96,128},{128,160},{160,192},{192,224},{1,3... | collective-permute-start | bytes 2359304 | tf_op jit(solution)/shard_map/ppermute | solution.py:513
  34.8 1.3 %all-to-all-done.came_ref = bf16[32,32,384]{2,1,0:T(8,128)(2,1)S(1)} async-done(((bf16[32,32,384]{2,1,0:T(8,128)(2,1)}), bf16[32,32,384]{2,1,0:T(8,128)(2,1)S(1)}, u32[]{:S(2)}, u32[]{:S(2)}) %all-to-all-start) | async-done | bytes 786464 | tf_op jit(solution)/shard_map/all_to_all | solution.py:488
  36.1 4.7 %latitude.1._after = bf16[1024,384]{1,0:T(8,128)(2,1)} custom-call(bf16[32,32,384]{2,1,0:T(8,128)(2,1)S(1)} %all-to-all-done.came_ref, f32[384,1024]{1,0:T(8,128)} %bitcast.34, bf16[1024,1024]{1,0:T(8,128)(2,1)} %constant.9.clone.turned_hbm), custom_call_target="tpu_custom_call" | custom-call | tf_op jit(solution)/shard_map/latitude/pallas_call | solution.py:426
  40.9 0.0 copy-start.2
  40.9 0.0 copy-start.3
  40.9 0.0 copy-start.4
  40.9 0.0 copy-start.5
  40.9 0.0 copy-start.6
  40.9 6.7 %all-to-all-start.1 = ((bf16[32,32,384]{2,1,0:T(8,128)(2,1)}), bf16[32,32,384]{2,1,0:T(8,128)(2,1)S(1)}, u32[]{:S(2)}, u32[]{:S(2)}) async-start(bf16[32,32,384]{2,1,0:T(8,128)(2,1)} %bitcast.10), calls=%async_computation.1 | async-start | bytes 1572864 | tf_op jit(solution)/shard_map/all_to_all | solution.py:526
  47.7 3.2 %observe.1 = (f32[384,64]{1,0:T(8,128)S(1)}, f32[1,512]{1,0:T(1,128)}) custom-call(f32[12,32,1024]{2,1,0:T(8,128)} %bitcast.29, s32[1,512]{1,0:T(1,128)S(1)} %copy-done.4, f32[1,512]{1,0:T(1,128)S(1)} %copy-done.5, f32[1,512]{1,0:T(1,128)S(1)} %copy-done.6, bf16[1024,64]{1,0:T(8,128)(2,1)S(1)} %copy-done.2, bf16[96,384]{1,0:T(8,128)(2,1)S(1)} %copy-done.3, ...), custom_call_target="tpu_custom_call" | custom-call | tf_op jit(solution)/shard_map/observe/pallas_call | solution.py:426
  51.0 7.7 %backward.1 = f32[12,32,1024]{2,1,0:T(8,128)} custom-call(bf16[480,1024]{1,0:T(8,128)(2,1)S(1)} %collective-permute-done.3.coming_ref, f32[12,32,1024]{2,1,0:T(8,128)} %bitcast.33, bf16[144,1024]{1,0:T(8,128)(2,1)S(1)} %collective-permute-done._head.head_in.head_ref, bf16[144,1024]{1,0:T(8,128)(2,1)S(1)} %collective-permute-done.1._tail.tail_in.tail_ref, ...), custom_call_target="tpu_custom_call" | custom-call | tf_op jit(solution)/shard_map/backward/pallas_call | solution.py:426
  58.6 3.3 %all-to-all-done.1.came_ref = bf16[32,32,384]{2,1,0:T(8,128)(2,1)S(1)} async-done(((bf16[32,32,384]{2,1,0:T(8,128)(2,1)}), bf16[32,32,384]{2,1,0:T(8,128)(2,1)S(1)}, u32[]{:S(2)}, u32[]{:S(2)}) %all-to-all-start.1) | async-done | bytes 786464 | tf_op jit(solution)/shard_map/all_to_all | solution.py:526
  61.9 4.0 %finish.1 = f32[384,1024]{1,0:T(8,128)} custom-call(bf16[32,32,384]{2,1,0:T(8,128)(2,1)S(1)} %all-to-all-done.1.came_ref, f32[384,1024]{1,0:T(8,128)} %bitcast.30, bf16[384,1024]{1,0:T(8,128)(2,1)S(1)} %collective-permute-done.2.prev_ref, bf16[1024,1024]{1,0:T(8,128)(2,1)} %constant.8.clone.table_ref.table_hbm), custom_call_target="tpu_custom_call" | custom-call | tf_op jit(solution)/shard_map/finish/pallas_call | solution.py:426
  (11 shorter events, 0.0 us)
Async XLA Ops:
  0.6 5.2 %copy-start = (f32[1,32,12,1024]{3,1,2,0:T(8,128)S(1)}, f32[1,32,12,1024]{3,1,2,0:T(8,128)}, u32[]{:S(2)}) copy-start(f32[1,32,12,1024]{3,1,2,0:T(8,128)} %param.12) | copy-start | bytes 4718596
  0.6 5.2 %copy-start.1 = (bf16[1024,1024]{1,0:T(8,128)(2,1)S(1)}, bf16[1024,1024]{1,0:T(8,128)(2,1)}, u32[]{:S(2)}) copy-start(bf16[1024,1024]{1,0:T(8,128)(2,1)} %constant.8.clone.table_ref.table_hbm) | copy-start | bytes 6291460
  2.5 7.2 %collective-permute-start = (bf16[144,1024]{1,0:T(8,128)(2,1)S(1)}, bf16[144,1024]{1,0:T(8,128)(2,1)S(1)}, u32[]{:S(2)}, u32[]{:S(2)}) collective-permute-start(bf16[144,1024]{1,0:T(8,128)(2,1)S(1)} %get-tuple-element.9._after), channel_id=1, source_target_pairs={{1,0},{2,1},{3,2},{4,3},{5,4},{6,5},{7,6},{8,7},{9,8},{10,9},{11,1... | collective-permute-start | bytes 884744 | tf_op jit(solution)/shard_map/ppermute | solution.py:485
  5.8 4.0 %collective-permute-start.1 = (bf16[144,1024]{1,0:T(8,128)(2,1)S(1)}, bf16[144,1024]{1,0:T(8,128)(2,1)S(1)}, u32[]{:S(2)}, u32[]{:S(2)}) collective-permute-start(bf16[144,1024]{1,0:T(8,128)(2,1)S(1)} %get-tuple-element.11), channel_id=1, source_target_pairs={{0,1},{1,2},{2,3},{3,4},{4,5},{5,6},{6,7},{7,8},{8,9},{9,10},{10,1... | collective-permute-start | bytes 884744 | tf_op jit(solution)/shard_map/ppermute | solution.py:486
  9.8 26.3 %all-to-all-start = ((bf16[32,32,384]{2,1,0:T(8,128)(2,1)}), bf16[32,32,384]{2,1,0:T(8,128)(2,1)S(1)}, u32[]{:S(2)}, u32[]{:S(2)}) async-start(bf16[32,32,384]{2,1,0:T(8,128)(2,1)} %bitcast.7), calls=%async_computation | async-start | bytes 1572864 | tf_op jit(solution)/shard_map/all_to_all | solution.py:488
  22.5 28.5 %collective-permute-start.3 = (bf16[480,1024]{1,0:T(8,128)(2,1)}, bf16[480,1024]{1,0:T(8,128)(2,1)S(1)}, u32[]{:S(2)}, u32[]{:S(2)}) collective-permute-start(bf16[480,1024]{1,0:T(8,128)(2,1)} %join.1), channel_id=1, source_target_pairs={{32,0},{64,32},{96,64},{128,96},{160,128},{192,160},{224,192},{33,... | collective-permute-start | bytes 2949128 | tf_op jit(solution)/shard_map/ppermute | solution.py:498
  30.6 28.0 %collective-permute-start.2 = (bf16[384,1024]{1,0:T(8,128)(2,1)}, bf16[384,1024]{1,0:T(8,128)(2,1)S(1)}, u32[]{:S(2)}, u32[]{:S(2)}) collective-permute-start(bf16[384,1024]{1,0:T(8,128)(2,1)} %forward.1), channel_id=1, source_target_pairs={{0,32},{32,64},{64,96},{96,128},{128,160},{160,192},{192,224},{1,3... | collective-permute-start | bytes 2359304 | tf_op jit(solution)/shard_map/ppermute | solution.py:513
  40.9 6.8 %copy-start.2 = (bf16[1024,64]{1,0:T(8,128)(2,1)S(1)}, bf16[1024,64]{1,0:T(8,128)(2,1)}, u32[]{:S(2)}) copy-start(bf16[1024,64]{1,0:T(8,128)(2,1)} %constant.10.clone.cols_hbm) | copy-start | bytes 393220
  40.9 6.8 %copy-start.3 = (bf16[96,384]{1,0:T(8,128)(2,1)S(1)}, bf16[96,384]{1,0:T(8,128)(2,1)}, u32[]{:S(2)}) copy-start(bf16[96,384]{1,0:T(8,128)(2,1)} %constant.11.clone.lines_hbm) | copy-start | bytes 221188
  40.9 6.8 %copy-start.4 = (s32[1,512]{1,0:T(1,128)S(1)}, s32[1,512]{1,0:T(1,128)}, u32[]{:S(2)}) copy-start(s32[1,512]{1,0:T(1,128)} %index_ref.1) | copy-start | bytes 6148
  40.9 6.8 %copy-start.5 = (f32[1,512]{1,0:T(1,128)S(1)}, f32[1,512]{1,0:T(1,128)}, u32[]{:S(2)}) copy-start(f32[1,512]{1,0:T(1,128)} %dual_ref.1) | copy-start | bytes 6148
  40.9 6.8 %copy-start.6 = (f32[1,512]{1,0:T(1,128)S(1)}, f32[1,512]{1,0:T(1,128)}, u32[]{:S(2)}) copy-start(f32[1,512]{1,0:T(1,128)} %variance_ref.1) | copy-start | bytes 6148
  40.9 21.0 %all-to-all-start.1 = ((bf16[32,32,384]{2,1,0:T(8,128)(2,1)}), bf16[32,32,384]{2,1,0:T(8,128)(2,1)S(1)}, u32[]{:S(2)}, u32[]{:S(2)}) async-start(bf16[32,32,384]{2,1,0:T(8,128)(2,1)} %bitcast.10), calls=%async_computation.1 | async-start | bytes 1572864 | tf_op jit(solution)/shard_map/all_to_all | solution.py:526

commit v7 on v6

--- a/solution.py
+++ b/solution.py
@@ -65,7 +65,11 @@
         return copy
 
 
-def edge_kernel(mult_hbm, incr_hbm, wind_hbm, head_ref, tail_ref, edge_ref, sems):
+def by_parity(even, odd):
+    return jnp.where(lax.axis_index("space") % 2 == 0, even, odd)
+
+
+def edge_kernel(mult_hbm, incr_hbm, wind_hbm, mate_ref, other_ref, edge_ref, sems):
     levels, rows, width = mult_hbm.shape
     half = levels // 2
     copies = Copies(sems)
@@ -74,7 +78,8 @@
         for end, at in enumerate((0, rows - 8))
         for i, source in enumerate((incr_hbm, wind_hbm, mult_hbm))
     ]
-    for end, part_ref in enumerate((head_ref, tail_ref)):
+    messages = []
+    for end in range(2):
         for copy in coming[3 * end : 3 * end + 3]:
             copy.wait()
         incr, wind, mult = edge_ref[3 * end], edge_ref[3 * end + 1], edge_ref[3 * end + 2]
@@ -85,8 +90,10 @@
             field, dual = jnp.where(low, incr, wind), jnp.where(less, mult[:half], second)
         else:
             field, dual = jnp.where(low, wind, incr), jnp.where(less, second, mult[:half])
-        part_ref[: levels * 8] = field.reshape(levels * 8, width).astype(BF16)
-        part_ref[levels * 8 :] = dual.reshape(half * 8, width).astype(BF16)
+        messages.append((field.reshape(levels * 8, width), dual.reshape(half * 8, width)))
+    for part, (head, tail) in zip((pl.ds(0, levels * 8), pl.ds(levels * 8, half * 8)), zip(*messages)):
+        mate_ref[part] = by_parity(tail, head).astype(BF16)
+        other_ref[part] = by_parity(head, tail).astype(BF16)
 
 
 def start_kernel(mult_ref, table_ref, _after, whole_hbm, spec_hbm, flat_ref, spec_ref, sems):
@@ -108,13 +115,14 @@
     pass
 
 
-def join_kernel(_whole_in, head_ref, tail_ref, whole_hbm, sems):
+def join_kernel(_whole_in, mate_ref, other_ref, whole_hbm, sems):
     copies = Copies(sems)
     size = whole_hbm.shape[0] // 10
-    start, far = whole_hbm.shape[0] - 2 * size, head_ref.shape[0] - size
+    start, far = whole_hbm.shape[0] - 2 * size, mate_ref.shape[0] - size
+    odd = lax.axis_index("space") % 2
     out = [
-        copies.start(source.at[pl.ds(far, size)], whole_hbm.at[pl.ds(start + size * i, size)])
-        for i, source in enumerate((head_ref, tail_ref))
+        copies.start(source.at[pl.ds(far, size)], whole_hbm.at[pl.ds(pl.multiple_of(start + size * at, 16), size)])
+        for source, at in ((mate_ref, odd), (other_ref, 1 - odd))
     ]
     for copy in out:
         copy.wait()
@@ -132,10 +140,10 @@
     return [[stage_ref[c, pl.ds(t, 8, stride=TILES), :] for t in range(TILES)] for c in range(across)]
 
 
-def join_rows(stage_ref, tiles, rows):
+def join_rows(stage_ref, tiles, rows, factor=0.2**STEPS):
     for c, column in enumerate(tiles):
         for t, tile in enumerate(column):
-            stage_ref[c, pl.ds(t, 8, stride=TILES), :] = tile * (0.2**STEPS)
+            stage_ref[c, pl.ds(t, 8, stride=TILES), :] = tile * factor
     return jnp.concatenate([stage_ref[c, :rows, :] for c in range(len(tiles))], axis=1)
 
 
@@ -228,7 +236,7 @@
 
 
 def forward_kernel(
-    incr_hbm, wind_hbm, head_in, tail_in, ends_hbm,
+    incr_hbm, wind_hbm, mate_ref, other_ref, ends_hbm,
     incr_ref, wind_ref, head_ref, tail_ref, stage_ref, coef_ref, ends_ref, level_sems,
 ):
     levels, rows, width = incr_ref.shape
@@ -246,8 +254,9 @@
         for index in (level, level + half):
             for kind in range(2):
                 fetch(kind, index).start()
-    head_ref[...] = head_in[: levels * 8].astype(F32)
-    tail_ref[...] = tail_in[: levels * 8].astype(F32)
+    mate, other = mate_ref[: levels * 8].astype(F32), other_ref[: levels * 8].astype(F32)
+    head_ref[...] = by_parity(mate, other)
+    tail_ref[...] = by_parity(other, mate)
     low = low_half((8, width))
 
     def at_level(level, carry):
@@ -300,7 +309,7 @@
 
 
 def backward_kernel(
-    coming_ref, wind_hbm, head_in, tail_in, mult_hbm, tall_ref, cols_hbm,
+    coming_ref, wind_hbm, mate_ref, other_ref, mult_hbm, tall_ref, cols_hbm,
     state_hbm,
     wind_ref, mult_ref, cols_ref,
     head_ref, tail_ref, far_ref, margins_ref, stage_ref, coef_ref, spread_ref, state_ref, sems, level_sems,
@@ -317,13 +326,16 @@
     spread_ref[...] = sum(nt(p, cols_ref[...]) for p in parts(tall_ref[...]))
     for copy in arriving[1:]:
         copy.wait()
-    head_ref[...] = head_in[: levels * 8].astype(F32)
-    tail_ref[...] = tail_in[: levels * 8].astype(F32)
+    mate, other = mate_ref[: levels * 8].astype(F32), other_ref[: levels * 8].astype(F32)
+    head_ref[...] = by_parity(mate, other)
+    tail_ref[...] = by_parity(other, mate)
     far_ref[...] = coming_ref[full:].astype(F32)
     low = low_half((8, width))
 
     def put(index):
         return pltpu.make_async_copy(state_ref.at[index], state_hbm.at[index], level_sems.at[index])
+
+    factor = jnp.where(lax.axis_index("tm") == lax.axis_size("tm") - 1, 0.0, 0.2**STEPS)
 
     def at_level(level, carry):
         coefficients(level, levels, wind_ref, head_ref, tail_ref, stage_ref, coef_ref)
@@ -337,7 +349,7 @@
             part = pl.ds(pl.multiple_of(index * rows, rows), rows)
             main = coming_ref[part, :].astype(F32)
             y = backward_steps(spread_rows(stage_ref.at[2 + 2 * group], main, margins_ref[group]), coef_ref)
-            back = join_rows(stage_ref.at[3 + 2 * group], y, rows)
+            back = join_rows(stage_ref.at[3 + 2 * group], y, rows, factor)
             state_ref[index] = (mult_ref[index] - back) + spread_ref[part, :]
             put(index).start()
 
@@ -394,6 +406,7 @@
     came_ref, incr_hbm, prev_ref, table_hbm, out_hbm,
     incr_ref, table_ref, lines_ref, out_ref, sems,
 ):
+    after = jnp.where(lax.axis_index("tm") == 0, 0.0, 1.0)
     copies = Copies(sems)
     table_in = copies.start(table_hbm, table_ref)
     incr_in = copies.start(incr_hbm, incr_ref)
@@ -406,7 +419,7 @@
         covar = nn(lines_ref[part], table)
         if i == 0:
             incr_in.wait()
-        out_ref[part] = covar + (incr_ref[part] - prev_ref[part].astype(F32))
+        out_ref[part] = covar + (incr_ref[part] - prev_ref[part].astype(F32) * after)
         out.append(copies.start(out_ref.at[part], out_hbm.at[part]))
     for copy in out:
         copy.wait()
@@ -463,7 +476,7 @@
         return pltpu.SemaphoreType.DMA(dims)
 
     field = (levels, rows, width)
-    head, tail = call(
+    mate, other = call(
         edge_kernel,
         (shape(levels * 12, width), shape(levels * 12, width)),
         (mult, incr, wind),
@@ -475,34 +488,35 @@
     whole, spec = call(
         start_kernel,
         (shape(full + levels * 8, width), shape(width, full)),
-        (mult, table, head),
+        (mult, table, mate),
         [short(full, width), short(width, full), sems(3)],
         "start",
         near=(0,1,2),
         grant=40,
     )
-    ring = [(i, (i + 1) % count) for i in range(count)]
-    head = lax.ppermute(head, "space", [(b, a) for a, b in ring])
-    tail = lax.ppermute(tail, "space", ring)
-    spec = call(order_kernel, shape(width, full), (spec, head, tail), [], "order", {0: 0}, near=(1, 2))
+    mates = [(i, i ^ 1) for i in range(count)]
+    others = [(i, min(max(((i + 1) ^ 1) - 1, 0), count - 1)) for i in range(count)]
+    mate = lax.ppermute(mate, "space", mates)
+    other = lax.ppermute(other, "space", others)
+    spec = call(order_kernel, shape(width, full), (spec, mate, other), [], "order", {0: 0}, near=(1, 2))
     came = lax.all_to_all(spec.reshape(count, waves, full), "space", 0, 0, tiled=True)
     whole = call(
         join_kernel,
         shape(full + levels * 8, width),
-        (whole, head, tail),
+        (whole, mate, other),
         [sems(2)],
         "join",
         {0: 0},
         near=(1, 2),
     )
-    coming = lax.ppermute(whole, "tm", [(t + 1, t) for t in range(times - 1)])
+    coming = lax.ppermute(whole, "tm", [((t + 1) % times, t) for t in range(times)])
 
     across = width // 128
     stages = [wide(6, across, rows + 8, 128), wide(4, across, TILES, 8, 128)]
     ends = call(
         forward_kernel,
         shape(full, width),
-        (incr, wind, head, tail),
+        (incr, wind, mate, other),
         [
             wide(*field), wide(*field), wide(levels * 8, width), wide(levels * 8, width), *stages,
             short(full, width), sems(3, levels),
@@ -510,7 +524,7 @@
         "forward",
         near=(2, 3),
     )
-    previous = lax.ppermute(ends, "tm", [(t, t + 1) for t in range(times - 1)])
+    previous = lax.ppermute(ends, "tm", [(t, (t + 1) % times) for t in range(times)])
 
     back = call(
         latitude_kernel,
@@ -535,7 +549,7 @@
     state_rows = call(
         backward_kernel,
         jax.ShapeDtypeStruct(field, F32),
-        (coming, wind, head, tail, mult, tall, cols),
+        (coming, wind, mate, other, mult, tall, cols),
         [
             wide(*field), wide(*field), short(*cols.shape),
             wide(levels * 8, width), wide(levels * 8, width), wide(levels * 8, width), wide(2, 8, width),

time: 66.6 us -> 66.3 us (level)
  starting transfers between devices: 27.5 us -> 25.2 us
  waiting for transfers between devices: 6.48 us -> 8.19 us
  Pallas kernels: 31 us -> 31.7 us
    all_to_all x1, starting transfers between devices: 12 us -> 7.39 us  [local(): lax.all_to_all(spec.reshape(count, waves, full), 'space', 0, 0, tiled=True)]
    ppermute x4, starting transfers between devices: 8.83 us -> 11 us  [the longest x1 5.65 us: local(): lax.ppermute(whole, 'tm', [((t + 1) % times, t) for t in range(times)])]
    ppermute x4, waiting for transfers between devices: 1.92 us -> 4.04 us  [the longest x1 4.03 us: local(): other = lax.ppermute(other, 'space', others)]
  transfers between devices with their start and end apart: 6 -> 6, of which waited for: 4 -> 3; matrix products, arithmetic and copies ran while one was open for 0% -> 0% of each run, Pallas kernels for 38% -> 38%
where the time goes in v7:
time: 66.3 us; the launch traced here: 66 us
  Pallas kernels  31.7 us (48%)
  starting transfers between devices  25.2 us (38%)
  waiting for transfers between devices  8.19 us (12%)
  between operations  0.85 us (1%)
    pallas_call x9, Pallas kernels, call(): pl.pallas_call(kernel, out_shape=outs, in_specs=[place(i, a) for i, a in...  31.7 us
    all_to_all x1, starting transfers between devices, local(): lax.all_to_all(spec.reshape(count, waves, full), 'space', 0, 0, tiled=True)  7.39 us
    all_to_all x1, starting transfers between devices, local(): lax.all_to_all(back.reshape(count, rows, full), 'space', 0, 0, tiled=True)  6.87 us
    ppermute x1, starting transfers between devices, local(): lax.ppermute(whole, 'tm', [((t + 1) % times, t) for t in range(times)])  5.65 us
    ppermute x1, waiting for transfers between devices, local(): other = lax.ppermute(other, 'space', others)  4.03 us
    ppermute x1, starting transfers between devices, local(): mate = lax.ppermute(mate, 'space', mates)  3.33 us
    all_to_all x1, waiting for transfers between devices, local(): lax.all_to_all(back.reshape(count, rows, full), 'space', 0, 0, tiled=True)  3.2 us
    ppermute x1, starting transfers between devices, local(): other = lax.ppermute(other, 'space', others)  1.91 us
  transfers between devices with their start and end apart: 6, of which 3 were waited for; matrix products, arithmetic and copies ran while one was open for 0% of the time, Pallas kernels for 38%

profile of v7, /device:TPU:1, one launch (start us, length us, event | category | flops | bytes accessed | tf_op | source)
XLA Modules:
  0.0 66.0 jit_solution(5145184552427473704)
XLA Ops:
  0.6 0.0 copy-start
  0.6 0.0 copy-start.1
  0.7 1.9 %edges.1 = (bf16[144,1024]{1,0:T(8,128)(2,1)S(1)}, bf16[144,1024]{1,0:T(8,128)(2,1)S(1)}) custom-call(f32[12,32,1024]{2,1,0:T(8,128)} %bitcast.24, f32[12,32,1024]{2,1,0:T(8,128)} %bitcast.27, f32[12,32,1024]{2,1,0:T(8,128)} %bitcast.31), custom_call_target="tpu_custom_call" | custom-call | tf_op jit(solution)/shard_map/edges/pallas_call | solution.py:439
  2.6 3.3 %collective-permute-start = (bf16[144,1024]{1,0:T(8,128)(2,1)S(1)}, bf16[144,1024]{1,0:T(8,128)(2,1)S(1)}, u32[]{:S(2)}, u32[]{:S(2)}) collective-permute-start(bf16[144,1024]{1,0:T(8,128)(2,1)S(1)} %get-tuple-element.9._after), channel_id=1, source_target_pairs={{0,1},{1,0},{2,3},{3,2},{4,5},{5,4},{6,7},{7,6},{8,9},{9,8},{10,11... | collective-permute-start | bytes 884744 | tf_op jit(solution)/shard_map/ppermute | solution.py:499
  5.9 1.9 %collective-permute-start.1 = (bf16[144,1024]{1,0:T(8,128)(2,1)S(1)}, bf16[144,1024]{1,0:T(8,128)(2,1)S(1)}, u32[]{:S(2)}, u32[]{:S(2)}) collective-permute-start(bf16[144,1024]{1,0:T(8,128)(2,1)S(1)} %get-tuple-element.11), channel_id=1, source_target_pairs={{0,0},{1,2},{2,1},{3,4},{4,3},{5,6},{6,5},{7,8},{8,7},{9,10},{10,9... | collective-permute-start | bytes 884744 | tf_op jit(solution)/shard_map/ppermute | solution.py:500
  7.9 2.0 %start.1 = (bf16[480,1024]{1,0:T(8,128)(2,1)}, bf16[1024,384]{1,0:T(8,128)(2,1)}) custom-call(f32[12,32,1024]{2,1,0:T(8,128)S(1)} %bitcast.26, bf16[1024,1024]{1,0:T(8,128)(2,1)S(1)} %copy-done.1, bf16[144,1024]{1,0:T(8,128)(2,1)S(1)} %get-tuple-element.9._after), custom_call_target="tpu_custom_call" | custom-call | tf_op jit(solution)/shard_map/start/pallas_call | solution.py:439
  9.9 4.0 %collective-permute-done.1._tail.other_ref = bf16[144,1024]{1,0:T(8,128)(2,1)S(1)} collective-permute-done((bf16[144,1024]{1,0:T(8,128)(2,1)S(1)}, bf16[144,1024]{1,0:T(8,128)(2,1)S(1)}, u32[]{:S(2)}, u32[]{:S(2)}) %collective-permute-start.1) | collective-permute-done | bytes 294944 | tf_op jit(solution)/shard_map/ppermute | solution.py:500
  13.9 7.4 %all-to-all-start = ((bf16[32,32,384]{2,1,0:T(8,128)(2,1)}), bf16[32,32,384]{2,1,0:T(8,128)(2,1)S(1)}, u32[]{:S(2)}, u32[]{:S(2)}) async-start(bf16[32,32,384]{2,1,0:T(8,128)(2,1)} %bitcast.7), calls=%async_computation | async-start | bytes 1572864 | tf_op jit(solution)/shard_map/all_to_all | solution.py:502
  21.3 0.7 %join.1 = bf16[480,1024]{1,0:T(8,128)(2,1)} custom-call(bf16[480,1024]{1,0:T(8,128)(2,1)} %get-tuple-element.13._whole_in, bf16[144,1024]{1,0:T(8,128)(2,1)S(1)} %collective-permute-done._head.mate_ref, bf16[144,1024]{1,0:T(8,128)(2,1)S(1)} %collective-permute-done.1._tail.other_ref), custom_call_target="tpu_custom_call", output_to_operand_aliasing={{}: (0, {})} | custom-call | tf_op jit(solution)/shard_map/join/pallas_call | solution.py:439
  22.1 5.7 %collective-permute-start.3 = (bf16[480,1024]{1,0:T(8,128)(2,1)}, bf16[480,1024]{1,0:T(8,128)(2,1)S(1)}, u32[]{:S(2)}, u32[]{:S(2)}) collective-permute-start(bf16[480,1024]{1,0:T(8,128)(2,1)} %join.1), channel_id=1, source_target_pairs={{32,0},{64,32},{96,64},{128,96},{160,128},{192,160},{224,192},{0,2... | collective-permute-start | bytes 2949128 | tf_op jit(solution)/shard_map/ppermute | solution.py:512
  27.7 6.8 %forward.1 = bf16[384,1024]{1,0:T(8,128)(2,1)} custom-call(f32[12,32,1024]{2,1,0:T(8,128)} %bitcast.28, f32[12,32,1024]{2,1,0:T(8,128)} %bitcast.32, bf16[144,1024]{1,0:T(8,128)(2,1)S(1)} %collective-permute-done._head.mate_ref, bf16[144,1024]{1,0:T(8,128)(2,1)S(1)} %collective-permute-done.1._tail.other_ref), custom_call_target="tpu_custom_call" | custom-call | tf_op jit(solution)/shard_map/forward/pallas_call | solution.py:439
  34.5 0.1 collective-permute-start.2
  34.6 0.9 %all-to-all-done.came_ref = bf16[32,32,384]{2,1,0:T(8,128)(2,1)S(1)} async-done(((bf16[32,32,384]{2,1,0:T(8,128)(2,1)}), bf16[32,32,384]{2,1,0:T(8,128)(2,1)S(1)}, u32[]{:S(2)}, u32[]{:S(2)}) %all-to-all-start) | async-done | bytes 786464 | tf_op jit(solution)/shard_map/all_to_all | solution.py:502
  35.6 4.7 %latitude.1._after = bf16[1024,384]{1,0:T(8,128)(2,1)} custom-call(bf16[32,32,384]{2,1,0:T(8,128)(2,1)S(1)} %all-to-all-done.came_ref, f32[384,1024]{1,0:T(8,128)} %bitcast.34, bf16[1024,1024]{1,0:T(8,128)(2,1)} %constant.9.clone.turned_hbm), custom_call_target="tpu_custom_call" | custom-call | tf_op jit(solution)/shard_map/latitude/pallas_call | solution.py:439
  40.3 0.0 copy-start.2
  40.3 0.0 copy-start.3
  40.3 0.0 copy-start.4
  40.4 0.0 copy-start.5
  40.4 0.0 copy-start.6
  40.4 6.9 %all-to-all-start.1 = ((bf16[32,32,384]{2,1,0:T(8,128)(2,1)}), bf16[32,32,384]{2,1,0:T(8,128)(2,1)S(1)}, u32[]{:S(2)}, u32[]{:S(2)}) async-start(bf16[32,32,384]{2,1,0:T(8,128)(2,1)} %bitcast.10), calls=%async_computation.1 | async-start | bytes 1572864 | tf_op jit(solution)/shard_map/all_to_all | solution.py:540
  47.3 3.2 %observe.1 = (f32[384,64]{1,0:T(8,128)S(1)}, f32[1,512]{1,0:T(1,128)}) custom-call(f32[12,32,1024]{2,1,0:T(8,128)} %bitcast.29, s32[1,512]{1,0:T(1,128)S(1)} %copy-done.4, f32[1,512]{1,0:T(1,128)S(1)} %copy-done.5, f32[1,512]{1,0:T(1,128)S(1)} %copy-done.6, bf16[1024,64]{1,0:T(8,128)(2,1)S(1)} %copy-done.2, bf16[96,384]{1,0:T(8,128)(2,1)S(1)} %copy-done.3, ...), custom_call_target="tpu_custom_call" | custom-call | tf_op jit(solution)/shard_map/observe/pallas_call | solution.py:439
  50.5 7.7 %backward.1 = f32[12,32,1024]{2,1,0:T(8,128)} custom-call(bf16[480,1024]{1,0:T(8,128)(2,1)S(1)} %collective-permute-done.3.coming_ref, f32[12,32,1024]{2,1,0:T(8,128)} %bitcast.33, bf16[144,1024]{1,0:T(8,128)(2,1)S(1)} %collective-permute-done._head.mate_ref, bf16[144,1024]{1,0:T(8,128)(2,1)S(1)} %collective-permute-done.1._tail.other_ref, ...), custom_call_target="tpu_custom_call" | custom-call | tf_op jit(solution)/shard_map/backward/pallas_call | solution.py:439
  58.3 3.2 %all-to-all-done.1.came_ref = bf16[32,32,384]{2,1,0:T(8,128)(2,1)S(1)} async-done(((bf16[32,32,384]{2,1,0:T(8,128)(2,1)}), bf16[32,32,384]{2,1,0:T(8,128)(2,1)S(1)}, u32[]{:S(2)}, u32[]{:S(2)}) %all-to-all-start.1) | async-done | bytes 786464 | tf_op jit(solution)/shard_map/all_to_all | solution.py:540
  61.5 4.5 %finish.1 = f32[384,1024]{1,0:T(8,128)} custom-call(bf16[32,32,384]{2,1,0:T(8,128)(2,1)S(1)} %all-to-all-done.1.came_ref, f32[384,1024]{1,0:T(8,128)} %bitcast.30, bf16[384,1024]{1,0:T(8,128)(2,1)S(1)} %collective-permute-done.2.prev_ref, bf16[1024,1024]{1,0:T(8,128)(2,1)} %constant.8.clone.table_ref.table_hbm), custom_call_target="tpu_custom_call" | custom-call | tf_op jit(solution)/shard_map/finish/pallas_call | solution.py:439
  (11 shorter events, 0.0 us)
Async XLA Ops:
  0.6 7.2 %copy-start = (f32[1,32,12,1024]{3,1,2,0:T(8,128)S(1)}, f32[1,32,12,1024]{3,1,2,0:T(8,128)}, u32[]{:S(2)}) copy-start(f32[1,32,12,1024]{3,1,2,0:T(8,128)} %param.12) | copy-start | bytes 4718596
  0.6 7.2 %copy-start.1 = (bf16[1024,1024]{1,0:T(8,128)(2,1)S(1)}, bf16[1024,1024]{1,0:T(8,128)(2,1)}, u32[]{:S(2)}) copy-start(bf16[1024,1024]{1,0:T(8,128)(2,1)} %constant.8.clone.table_ref.table_hbm) | copy-start | bytes 6291460
  2.6 7.3 %collective-permute-start = (bf16[144,1024]{1,0:T(8,128)(2,1)S(1)}, bf16[144,1024]{1,0:T(8,128)(2,1)S(1)}, u32[]{:S(2)}, u32[]{:S(2)}) collective-permute-start(bf16[144,1024]{1,0:T(8,128)(2,1)S(1)} %get-tuple-element.9._after), channel_id=1, source_target_pairs={{0,1},{1,0},{2,3},{3,2},{4,5},{5,4},{6,7},{7,6},{8,9},{9,8},{10,11... | collective-permute-start | bytes 884744 | tf_op jit(solution)/shard_map/ppermute | solution.py:499
  5.9 8.0 %collective-permute-start.1 = (bf16[144,1024]{1,0:T(8,128)(2,1)S(1)}, bf16[144,1024]{1,0:T(8,128)(2,1)S(1)}, u32[]{:S(2)}, u32[]{:S(2)}) collective-permute-start(bf16[144,1024]{1,0:T(8,128)(2,1)S(1)} %get-tuple-element.11), channel_id=1, source_target_pairs={{0,0},{1,2},{2,1},{3,4},{4,3},{5,6},{6,5},{7,8},{8,7},{9,10},{10,9... | collective-permute-start | bytes 884744 | tf_op jit(solution)/shard_map/ppermute | solution.py:500
  13.9 21.6 %all-to-all-start = ((bf16[32,32,384]{2,1,0:T(8,128)(2,1)}), bf16[32,32,384]{2,1,0:T(8,128)(2,1)S(1)}, u32[]{:S(2)}, u32[]{:S(2)}) async-start(bf16[32,32,384]{2,1,0:T(8,128)(2,1)} %bitcast.7), calls=%async_computation | async-start | bytes 1572864 | tf_op jit(solution)/shard_map/all_to_all | solution.py:502
  22.1 28.5 %collective-permute-start.3 = (bf16[480,1024]{1,0:T(8,128)(2,1)}, bf16[480,1024]{1,0:T(8,128)(2,1)S(1)}, u32[]{:S(2)}, u32[]{:S(2)}) collective-permute-start(bf16[480,1024]{1,0:T(8,128)(2,1)} %join.1), channel_id=1, source_target_pairs={{32,0},{64,32},{96,64},{128,96},{160,128},{192,160},{224,192},{0,2... | collective-permute-start | bytes 2949128 | tf_op jit(solution)/shard_map/ppermute | solution.py:512
  34.5 23.7 %collective-permute-start.2 = (bf16[384,1024]{1,0:T(8,128)(2,1)}, bf16[384,1024]{1,0:T(8,128)(2,1)S(1)}, u32[]{:S(2)}, u32[]{:S(2)}) collective-permute-start(bf16[384,1024]{1,0:T(8,128)(2,1)} %forward.1), channel_id=1, source_target_pairs={{0,32},{32,64},{64,96},{96,128},{128,160},{160,192},{192,224},{224... | collective-permute-start | bytes 2359304 | tf_op jit(solution)/shard_map/ppermute | solution.py:527
  40.3 6.9 %copy-start.2 = (bf16[1024,64]{1,0:T(8,128)(2,1)S(1)}, bf16[1024,64]{1,0:T(8,128)(2,1)}, u32[]{:S(2)}) copy-start(bf16[1024,64]{1,0:T(8,128)(2,1)} %constant.10.clone.cols_hbm) | copy-start | bytes 393220
  40.3 6.9 %copy-start.3 = (bf16[96,384]{1,0:T(8,128)(2,1)S(1)}, bf16[96,384]{1,0:T(8,128)(2,1)}, u32[]{:S(2)}) copy-start(bf16[96,384]{1,0:T(8,128)(2,1)} %constant.11.clone.lines_hbm) | copy-start | bytes 221188
  40.3 6.9 %copy-start.4 = (s32[1,512]{1,0:T(1,128)S(1)}, s32[1,512]{1,0:T(1,128)}, u32[]{:S(2)}) copy-start(s32[1,512]{1,0:T(1,128)} %index_ref.1) | copy-start | bytes 6148
  40.4 6.9 %copy-start.5 = (f32[1,512]{1,0:T(1,128)S(1)}, f32[1,512]{1,0:T(1,128)}, u32[]{:S(2)}) copy-start(f32[1,512]{1,0:T(1,128)} %dual_ref.1) | copy-start | bytes 6148
  40.4 6.9 %copy-start.6 = (f32[1,512]{1,0:T(1,128)S(1)}, f32[1,512]{1,0:T(1,128)}, u32[]{:S(2)}) copy-start(f32[1,512]{1,0:T(1,128)} %variance_ref.1) | copy-start | bytes 6148
  40.4 21.1 %all-to-all-start.1 = ((bf16[32,32,384]{2,1,0:T(8,128)(2,1)}), bf16[32,32,384]{2,1,0:T(8,128)(2,1)S(1)}, u32[]{:S(2)}, u32[]{:S(2)}) async-start(bf16[32,32,384]{2,1,0:T(8,128)(2,1)} %bitcast.10), calls=%async_computation.1 | async-start | bytes 1572864 | tf_op jit(solution)/shard_map/all_to_all | solution.py:540

commit v8 on v7

--- a/solution.py
+++ b/solution.py
@@ -259,6 +259,8 @@
     tail_ref[...] = by_parity(other, mate)
     low = low_half((8, width))
 
+    factor = jnp.where(lax.axis_index("tm") == lax.axis_size("tm") - 1, 0.0, 0.2**STEPS)
+
     def at_level(level, carry):
         for index in (level, level + half):
             for kind in range(2):
@@ -270,7 +272,7 @@
             at = pl.ds(pl.multiple_of(index * 8, 8), 8)
             margin = jnp.where(low, head_ref[at, :], tail_ref[at, :])
             x = forward_steps(spread_rows(stage_ref.at[2 + 2 * group], incr_ref[index], margin), coef_ref)
-            ends = join_rows(stage_ref.at[3 + 2 * group], x, rows)
+            ends = join_rows(stage_ref.at[3 + 2 * group], x, rows, factor)
             ends_ref[pl.ds(pl.multiple_of(index * rows, rows), rows), :] = ends.astype(BF16)
             put(index).start()
 
@@ -406,7 +408,6 @@
     came_ref, incr_hbm, prev_ref, table_hbm, out_hbm,
     incr_ref, table_ref, lines_ref, out_ref, sems,
 ):
-    after = jnp.where(lax.axis_index("tm") == 0, 0.0, 1.0)
     copies = Copies(sems)
     table_in = copies.start(table_hbm, table_ref)
     incr_in = copies.start(incr_hbm, incr_ref)
@@ -419,7 +420,7 @@
         covar = nn(lines_ref[part], table)
         if i == 0:
             incr_in.wait()
-        out_ref[part] = covar + (incr_ref[part] - prev_ref[part].astype(F32) * after)
+        out_ref[part] = covar + (incr_ref[part] - prev_ref[part].astype(F32))
         out.append(copies.start(out_ref.at[part], out_hbm.at[part]))
     for copy in out:
         copy.wait()

time: 66.3 us -> 65.9 us (level)
  transfers between devices with their start and end apart: 6 -> 6, of which waited for: 3 -> 3; matrix products, arithmetic and copies ran while one was open for 0% -> 0% of each run, Pallas kernels for 38% -> 39%
where the time goes in v8:
time: 65.9 us; the launch traced here: 65.5 us
  Pallas kernels  31.2 us (47%)
  starting transfers between devices  25.2 us (38%)
  waiting for transfers between devices  8.19 us (12%)
  between operations  0.85 us (1%)
    pallas_call x9, Pallas kernels, call(): pl.pallas_call(kernel, out_shape=outs, in_specs=[place(i, a) for i, a in...  31.2 us
    all_to_all x1, starting transfers between devices, local(): lax.all_to_all(spec.reshape(count, waves, full), 'space', 0, 0, tiled=True)  7.39 us
    all_to_all x1, starting transfers between devices, local(): lax.all_to_all(back.reshape(count, rows, full), 'space', 0, 0, tiled=True)  6.87 us
    ppermute x1, starting transfers between devices, local(): lax.ppermute(whole, 'tm', [((t + 1) % times, t) for t in range(times)])  5.65 us
    ppermute x1, waiting for transfers between devices, local(): other = lax.ppermute(other, 'space', others)  4.03 us
    ppermute x1, starting transfers between devices, local(): mate = lax.ppermute(mate, 'space', mates)  3.33 us
    all_to_all x1, waiting for transfers between devices, local(): lax.all_to_all(back.reshape(count, rows, full), 'space', 0, 0, tiled=True)  3.2 us
    ppermute x1, starting transfers between devices, local(): other = lax.ppermute(other, 'space', others)  1.91 us
  transfers between devices with their start and end apart: 6, of which 3 were waited for; matrix products, arithmetic and copies ran while one was open for 0% of the time, Pallas kernels for 39%

profile of v8, /device:TPU:1, one launch (start us, length us, event | category | flops | bytes accessed | tf_op | source)
XLA Modules:
  0.0 65.5 jit_solution(13332584654112973767)
XLA Ops:
  0.6 0.0 copy-start
  0.6 0.0 copy-start.1
  0.7 1.9 %edges.1 = (bf16[144,1024]{1,0:T(8,128)(2,1)S(1)}, bf16[144,1024]{1,0:T(8,128)(2,1)S(1)}) custom-call(f32[12,32,1024]{2,1,0:T(8,128)} %bitcast.24, f32[12,32,1024]{2,1,0:T(8,128)} %bitcast.27, f32[12,32,1024]{2,1,0:T(8,128)} %bitcast.31), custom_call_target="tpu_custom_call" | custom-call | tf_op jit(solution)/shard_map/edges/pallas_call | solution.py:440
  2.6 3.3 %collective-permute-start = (bf16[144,1024]{1,0:T(8,128)(2,1)S(1)}, bf16[144,1024]{1,0:T(8,128)(2,1)S(1)}, u32[]{:S(2)}, u32[]{:S(2)}) collective-permute-start(bf16[144,1024]{1,0:T(8,128)(2,1)S(1)} %get-tuple-element.9._after), channel_id=1, source_target_pairs={{0,1},{1,0},{2,3},{3,2},{4,5},{5,4},{6,7},{7,6},{8,9},{9,8},{10,11... | collective-permute-start | bytes 884744 | tf_op jit(solution)/shard_map/ppermute | solution.py:500
  5.9 1.9 %collective-permute-start.1 = (bf16[144,1024]{1,0:T(8,128)(2,1)S(1)}, bf16[144,1024]{1,0:T(8,128)(2,1)S(1)}, u32[]{:S(2)}, u32[]{:S(2)}) collective-permute-start(bf16[144,1024]{1,0:T(8,128)(2,1)S(1)} %get-tuple-element.11), channel_id=1, source_target_pairs={{0,0},{1,2},{2,1},{3,4},{4,3},{5,6},{6,5},{7,8},{8,7},{9,10},{10,9... | collective-permute-start | bytes 884744 | tf_op jit(solution)/shard_map/ppermute | solution.py:501
  7.9 2.0 %start.1 = (bf16[480,1024]{1,0:T(8,128)(2,1)}, bf16[1024,384]{1,0:T(8,128)(2,1)}) custom-call(f32[12,32,1024]{2,1,0:T(8,128)S(1)} %bitcast.26, bf16[1024,1024]{1,0:T(8,128)(2,1)S(1)} %copy-done.1, bf16[144,1024]{1,0:T(8,128)(2,1)S(1)} %get-tuple-element.9._after), custom_call_target="tpu_custom_call" | custom-call | tf_op jit(solution)/shard_map/start/pallas_call | solution.py:440
  9.9 4.0 %collective-permute-done.1._tail.other_ref = bf16[144,1024]{1,0:T(8,128)(2,1)S(1)} collective-permute-done((bf16[144,1024]{1,0:T(8,128)(2,1)S(1)}, bf16[144,1024]{1,0:T(8,128)(2,1)S(1)}, u32[]{:S(2)}, u32[]{:S(2)}) %collective-permute-start.1) | collective-permute-done | bytes 294944 | tf_op jit(solution)/shard_map/ppermute | solution.py:501
  13.9 7.4 %all-to-all-start = ((bf16[32,32,384]{2,1,0:T(8,128)(2,1)}), bf16[32,32,384]{2,1,0:T(8,128)(2,1)S(1)}, u32[]{:S(2)}, u32[]{:S(2)}) async-start(bf16[32,32,384]{2,1,0:T(8,128)(2,1)} %bitcast.7), calls=%async_computation | async-start | bytes 1572864 | tf_op jit(solution)/shard_map/all_to_all | solution.py:503
  21.3 0.7 %join.1 = bf16[480,1024]{1,0:T(8,128)(2,1)} custom-call(bf16[480,1024]{1,0:T(8,128)(2,1)} %get-tuple-element.13._whole_in, bf16[144,1024]{1,0:T(8,128)(2,1)S(1)} %collective-permute-done._head.mate_ref, bf16[144,1024]{1,0:T(8,128)(2,1)S(1)} %collective-permute-done.1._tail.other_ref), custom_call_target="tpu_custom_call", output_to_operand_aliasing={{}: (0, {})} | custom-call | tf_op jit(solution)/shard_map/join/pallas_call | solution.py:440
  22.1 5.7 %collective-permute-start.3 = (bf16[480,1024]{1,0:T(8,128)(2,1)}, bf16[480,1024]{1,0:T(8,128)(2,1)S(1)}, u32[]{:S(2)}, u32[]{:S(2)}) collective-permute-start(bf16[480,1024]{1,0:T(8,128)(2,1)} %join.1), channel_id=1, source_target_pairs={{32,0},{64,32},{96,64},{128,96},{160,128},{192,160},{224,192},{0,2... | collective-permute-start | bytes 2949128 | tf_op jit(solution)/shard_map/ppermute | solution.py:513
  27.7 6.8 %forward.1 = bf16[384,1024]{1,0:T(8,128)(2,1)} custom-call(f32[12,32,1024]{2,1,0:T(8,128)} %bitcast.28, f32[12,32,1024]{2,1,0:T(8,128)} %bitcast.32, bf16[144,1024]{1,0:T(8,128)(2,1)S(1)} %collective-permute-done._head.mate_ref, bf16[144,1024]{1,0:T(8,128)(2,1)S(1)} %collective-permute-done.1._tail.other_ref), custom_call_target="tpu_custom_call" | custom-call | tf_op jit(solution)/shard_map/forward/pallas_call | solution.py:440
  34.5 0.1 collective-permute-start.2
  34.6 0.9 %all-to-all-done.came_ref = bf16[32,32,384]{2,1,0:T(8,128)(2,1)S(1)} async-done(((bf16[32,32,384]{2,1,0:T(8,128)(2,1)}), bf16[32,32,384]{2,1,0:T(8,128)(2,1)S(1)}, u32[]{:S(2)}, u32[]{:S(2)}) %all-to-all-start) | async-done | bytes 786464 | tf_op jit(solution)/shard_map/all_to_all | solution.py:503
  35.6 4.7 %latitude.1._after = bf16[1024,384]{1,0:T(8,128)(2,1)} custom-call(bf16[32,32,384]{2,1,0:T(8,128)(2,1)S(1)} %all-to-all-done.came_ref, f32[384,1024]{1,0:T(8,128)} %bitcast.34, bf16[1024,1024]{1,0:T(8,128)(2,1)} %constant.9.clone.turned_hbm), custom_call_target="tpu_custom_call" | custom-call | tf_op jit(solution)/shard_map/latitude/pallas_call | solution.py:440
  40.3 0.0 copy-start.2
  40.3 0.0 copy-start.3
  40.3 0.0 copy-start.4
  40.4 0.0 copy-start.5
  40.4 0.0 copy-start.6
  40.4 6.9 %all-to-all-start.1 = ((bf16[32,32,384]{2,1,0:T(8,128)(2,1)}), bf16[32,32,384]{2,1,0:T(8,128)(2,1)S(1)}, u32[]{:S(2)}, u32[]{:S(2)}) async-start(bf16[32,32,384]{2,1,0:T(8,128)(2,1)} %bitcast.10), calls=%async_computation.1 | async-start | bytes 1572864 | tf_op jit(solution)/shard_map/all_to_all | solution.py:541
  47.3 3.2 %observe.1 = (f32[384,64]{1,0:T(8,128)S(1)}, f32[1,512]{1,0:T(1,128)}) custom-call(f32[12,32,1024]{2,1,0:T(8,128)} %bitcast.29, s32[1,512]{1,0:T(1,128)S(1)} %copy-done.4, f32[1,512]{1,0:T(1,128)S(1)} %copy-done.5, f32[1,512]{1,0:T(1,128)S(1)} %copy-done.6, bf16[1024,64]{1,0:T(8,128)(2,1)S(1)} %copy-done.2, bf16[96,384]{1,0:T(8,128)(2,1)S(1)} %copy-done.3, ...), custom_call_target="tpu_custom_call" | custom-call | tf_op jit(solution)/shard_map/observe/pallas_call | solution.py:440
  50.5 7.7 %backward.1 = f32[12,32,1024]{2,1,0:T(8,128)} custom-call(bf16[480,1024]{1,0:T(8,128)(2,1)S(1)} %collective-permute-done.3.coming_ref, f32[12,32,1024]{2,1,0:T(8,128)} %bitcast.33, bf16[144,1024]{1,0:T(8,128)(2,1)S(1)} %collective-permute-done._head.mate_ref, bf16[144,1024]{1,0:T(8,128)(2,1)S(1)} %collective-permute-done.1._tail.other_ref, ...), custom_call_target="tpu_custom_call" | custom-call | tf_op jit(solution)/shard_map/backward/pallas_call | solution.py:440
  58.3 3.2 %all-to-all-done.1.came_ref = bf16[32,32,384]{2,1,0:T(8,128)(2,1)S(1)} async-done(((bf16[32,32,384]{2,1,0:T(8,128)(2,1)}), bf16[32,32,384]{2,1,0:T(8,128)(2,1)S(1)}, u32[]{:S(2)}, u32[]{:S(2)}) %all-to-all-start.1) | async-done | bytes 786464 | tf_op jit(solution)/shard_map/all_to_all | solution.py:541
  61.5 4.0 %finish.1 = f32[384,1024]{1,0:T(8,128)} custom-call(bf16[32,32,384]{2,1,0:T(8,128)(2,1)S(1)} %all-to-all-done.1.came_ref, f32[384,1024]{1,0:T(8,128)} %bitcast.30, bf16[384,1024]{1,0:T(8,128)(2,1)S(1)} %collective-permute-done.2.prev_ref, bf16[1024,1024]{1,0:T(8,128)(2,1)} %constant.8.clone.table_ref.table_hbm), custom_call_target="tpu_custom_call" | custom-call | tf_op jit(solution)/shard_map/finish/pallas_call | solution.py:440
  (11 shorter events, 0.0 us)
Async XLA Ops:
  0.6 7.2 %copy-start = (f32[1,32,12,1024]{3,1,2,0:T(8,128)S(1)}, f32[1,32,12,1024]{3,1,2,0:T(8,128)}, u32[]{:S(2)}) copy-start(f32[1,32,12,1024]{3,1,2,0:T(8,128)} %param.12) | copy-start | bytes 4718596
  0.6 7.2 %copy-start.1 = (bf16[1024,1024]{1,0:T(8,128)(2,1)S(1)}, bf16[1024,1024]{1,0:T(8,128)(2,1)}, u32[]{:S(2)}) copy-start(bf16[1024,1024]{1,0:T(8,128)(2,1)} %constant.8.clone.table_ref.table_hbm) | copy-start | bytes 6291460
  2.6 7.3 %collective-permute-start = (bf16[144,1024]{1,0:T(8,128)(2,1)S(1)}, bf16[144,1024]{1,0:T(8,128)(2,1)S(1)}, u32[]{:S(2)}, u32[]{:S(2)}) collective-permute-start(bf16[144,1024]{1,0:T(8,128)(2,1)S(1)} %get-tuple-element.9._after), channel_id=1, source_target_pairs={{0,1},{1,0},{2,3},{3,2},{4,5},{5,4},{6,7},{7,6},{8,9},{9,8},{10,11... | collective-permute-start | bytes 884744 | tf_op jit(solution)/shard_map/ppermute | solution.py:500
  5.9 8.0 %collective-permute-start.1 = (bf16[144,1024]{1,0:T(8,128)(2,1)S(1)}, bf16[144,1024]{1,0:T(8,128)(2,1)S(1)}, u32[]{:S(2)}, u32[]{:S(2)}) collective-permute-start(bf16[144,1024]{1,0:T(8,128)(2,1)S(1)} %get-tuple-element.11), channel_id=1, source_target_pairs={{0,0},{1,2},{2,1},{3,4},{4,3},{5,6},{6,5},{7,8},{8,7},{9,10},{10,9... | collective-permute-start | bytes 884744 | tf_op jit(solution)/shard_map/ppermute | solution.py:501
  13.9 21.6 %all-to-all-start = ((bf16[32,32,384]{2,1,0:T(8,128)(2,1)}), bf16[32,32,384]{2,1,0:T(8,128)(2,1)S(1)}, u32[]{:S(2)}, u32[]{:S(2)}) async-start(bf16[32,32,384]{2,1,0:T(8,128)(2,1)} %bitcast.7), calls=%async_computation | async-start | bytes 1572864 | tf_op jit(solution)/shard_map/all_to_all | solution.py:503
  22.1 28.5 %collective-permute-start.3 = (bf16[480,1024]{1,0:T(8,128)(2,1)}, bf16[480,1024]{1,0:T(8,128)(2,1)S(1)}, u32[]{:S(2)}, u32[]{:S(2)}) collective-permute-start(bf16[480,1024]{1,0:T(8,128)(2,1)} %join.1), channel_id=1, source_target_pairs={{32,0},{64,32},{96,64},{128,96},{160,128},{192,160},{224,192},{0,2... | collective-permute-start | bytes 2949128 | tf_op jit(solution)/shard_map/ppermute | solution.py:513
  34.5 23.7 %collective-permute-start.2 = (bf16[384,1024]{1,0:T(8,128)(2,1)}, bf16[384,1024]{1,0:T(8,128)(2,1)S(1)}, u32[]{:S(2)}, u32[]{:S(2)}) collective-permute-start(bf16[384,1024]{1,0:T(8,128)(2,1)} %forward.1), channel_id=1, source_target_pairs={{0,32},{32,64},{64,96},{96,128},{128,160},{160,192},{192,224},{224... | collective-permute-start | bytes 2359304 | tf_op jit(solution)/shard_map/ppermute | solution.py:528
  40.3 6.9 %copy-start.2 = (bf16[1024,64]{1,0:T(8,128)(2,1)S(1)}, bf16[1024,64]{1,0:T(8,128)(2,1)}, u32[]{:S(2)}) copy-start(bf16[1024,64]{1,0:T(8,128)(2,1)} %constant.10.clone.cols_hbm) | copy-start | bytes 393220
  40.3 6.9 %copy-start.3 = (bf16[96,384]{1,0:T(8,128)(2,1)S(1)}, bf16[96,384]{1,0:T(8,128)(2,1)}, u32[]{:S(2)}) copy-start(bf16[96,384]{1,0:T(8,128)(2,1)} %constant.11.clone.lines_hbm) | copy-start | bytes 221188
  40.3 6.9 %copy-start.4 = (s32[1,512]{1,0:T(1,128)S(1)}, s32[1,512]{1,0:T(1,128)}, u32[]{:S(2)}) copy-start(s32[1,512]{1,0:T(1,128)} %index_ref.1) | copy-start | bytes 6148
  40.4 6.9 %copy-start.5 = (f32[1,512]{1,0:T(1,128)S(1)}, f32[1,512]{1,0:T(1,128)}, u32[]{:S(2)}) copy-start(f32[1,512]{1,0:T(1,128)} %dual_ref.1) | copy-start | bytes 6148
  40.4 6.9 %copy-start.6 = (f32[1,512]{1,0:T(1,128)S(1)}, f32[1,512]{1,0:T(1,128)}, u32[]{:S(2)}) copy-start(f32[1,512]{1,0:T(1,128)} %variance_ref.1) | copy-start | bytes 6148
  40.4 21.1 %all-to-all-start.1 = ((bf16[32,32,384]{2,1,0:T(8,128)(2,1)}), bf16[32,32,384]{2,1,0:T(8,128)(2,1)S(1)}, u32[]{:S(2)}, u32[]{:S(2)}) async-start(bf16[32,32,384]{2,1,0:T(8,128)(2,1)} %bitcast.10), calls=%async_computation.1 | async-start | bytes 1572864 | tf_op jit(solution)/shard_map/all_to_all | solution.py:541

commit v9 on v8

--- a/solution.py
+++ b/solution.py
@@ -69,7 +69,7 @@
     return jnp.where(lax.axis_index("space") % 2 == 0, even, odd)
 
 
-def edge_kernel(mult_hbm, incr_hbm, wind_hbm, mate_ref, other_ref, edge_ref, sems):
+def edge_kernel(mult_hbm, incr_hbm, wind_hbm, other_ref, mate_ref, edge_ref, sems):
     levels, rows, width = mult_hbm.shape
     half = levels // 2
     copies = Copies(sems)
@@ -477,7 +477,7 @@
         return pltpu.SemaphoreType.DMA(dims)
 
     field = (levels, rows, width)
-    mate, other = call(
+    other, mate = call(
         edge_kernel,
         (shape(levels * 12, width), shape(levels * 12, width)),
         (mult, incr, wind),
@@ -489,7 +489,7 @@
     whole, spec = call(
         start_kernel,
         (shape(full + levels * 8, width), shape(width, full)),
-        (mult, table, mate),
+        (mult, table, other),
         [short(full, width), short(width, full), sems(3)],
         "start",
         near=(0,1,2),
@@ -497,9 +497,9 @@
     )
     mates = [(i, i ^ 1) for i in range(count)]
     others = [(i, min(max(((i + 1) ^ 1) - 1, 0), count - 1)) for i in range(count)]
+    other = lax.ppermute(other, "space", others)
     mate = lax.ppermute(mate, "space", mates)
-    other = lax.ppermute(other, "space", others)
-    spec = call(order_kernel, shape(width, full), (spec, mate, other), [], "order", {0: 0}, near=(1, 2))
+    spec = call(order_kernel, shape(width, full), (spec, other, mate), [], "order", {0: 0}, near=(1, 2))
     came = lax.all_to_all(spec.reshape(count, waves, full), "space", 0, 0, tiled=True)
     whole = call(
         join_kernel,

time: 65.9 us -> 65.1 us (0.988)
  waiting for transfers between devices: 8.19 us -> 6.37 us
  starting transfers between devices: 25.2 us -> 26.3 us
    ppermute x1, starting transfers between devices: 3.33 us -> 0.09 us  [local(): mate = lax.ppermute(mate, 'space', mates)]
    ppermute x1, starting transfers between devices: 1.91 us -> 4.59 us  [local(): other = lax.ppermute(other, 'space', others)]
    ppermute x1, waiting for transfers between devices: 4.03 us -> 2.21 us  [local(): other = lax.ppermute(other, 'space', others)]
    all_to_all x1, starting transfers between devices: 7.39 us -> 9.01 us  [local(): lax.all_to_all(spec.reshape(count, waves, full), 'space', 0, 0, tiled=True)]
where the time goes in v9:
time: 65.1 us; the launch traced here: 64.8 us
  Pallas kernels  31.2 us (48%)
  starting transfers between devices  26.3 us (40%)
  waiting for transfers between devices  6.37 us (10%)
  between operations  0.85 us (1%)
    pallas_call x9, Pallas kernels, call(): pl.pallas_call(kernel, out_shape=outs, in_specs=[place(i, a) for i, a in...  31.2 us
    all_to_all x1, starting transfers between devices, local(): lax.all_to_all(spec.reshape(count, waves, full), 'space', 0, 0, tiled=True)  9.01 us
    all_to_all x1, starting transfers between devices, local(): lax.all_to_all(back.reshape(count, rows, full), 'space', 0, 0, tiled=True)  6.87 us
    ppermute x1, starting transfers between devices, local(): lax.ppermute(whole, 'tm', [((t + 1) % times, t) for t in range(times)])  5.65 us
    ppermute x1, starting transfers between devices, local(): other = lax.ppermute(other, 'space', others)  4.59 us
    all_to_all x1, waiting for transfers between devices, local(): lax.all_to_all(back.reshape(count, rows, full), 'space', 0, 0, tiled=True)  3.2 us
    ppermute x1, waiting for transfers between devices, local(): other = lax.ppermute(other, 'space', others)  2.21 us
  transfers between devices with their start and end apart: 6, of which 3 were waited for; matrix products, arithmetic and copies ran while one was open for 0% of the time, Pallas kernels for 39%

profile of v9, /device:TPU:1, one launch (start us, length us, event | category | flops | bytes accessed | tf_op | source)
XLA Modules:
  0.0 64.8 jit_solution(9834202291812393444)
XLA Ops:
  0.6 0.0 copy-start
  0.6 0.0 copy-start.1
  0.7 1.9 %edges.1 = (bf16[144,1024]{1,0:T(8,128)(2,1)S(1)}, bf16[144,1024]{1,0:T(8,128)(2,1)S(1)}) custom-call(f32[12,32,1024]{2,1,0:T(8,128)} %bitcast.24, f32[12,32,1024]{2,1,0:T(8,128)} %bitcast.27, f32[12,32,1024]{2,1,0:T(8,128)} %bitcast.31), custom_call_target="tpu_custom_call" | custom-call | tf_op jit(solution)/shard_map/edges/pallas_call | solution.py:440
  2.6 4.6 %collective-permute-start = (bf16[144,1024]{1,0:T(8,128)(2,1)S(1)}, bf16[144,1024]{1,0:T(8,128)(2,1)S(1)}, u32[]{:S(2)}, u32[]{:S(2)}) collective-permute-start(bf16[144,1024]{1,0:T(8,128)(2,1)S(1)} %get-tuple-element.9._after), channel_id=1, source_target_pairs={{0,0},{1,2},{2,1},{3,4},{4,3},{5,6},{6,5},{7,8},{8,7},{9,10},{10,9... | collective-permute-start | bytes 884744 | tf_op jit(solution)/shard_map/ppermute | solution.py:500
  7.2 0.1 collective-permute-start.1
  7.3 2.0 %start.1 = (bf16[480,1024]{1,0:T(8,128)(2,1)}, bf16[1024,384]{1,0:T(8,128)(2,1)}) custom-call(f32[12,32,1024]{2,1,0:T(8,128)S(1)} %bitcast.26, bf16[1024,1024]{1,0:T(8,128)(2,1)S(1)} %copy-done.1, bf16[144,1024]{1,0:T(8,128)(2,1)S(1)} %get-tuple-element.9._after), custom_call_target="tpu_custom_call" | custom-call | tf_op jit(solution)/shard_map/start/pallas_call | solution.py:440
  9.4 2.2 %collective-permute-done._head.other_ref = bf16[144,1024]{1,0:T(8,128)(2,1)S(1)} collective-permute-done((bf16[144,1024]{1,0:T(8,128)(2,1)S(1)}, bf16[144,1024]{1,0:T(8,128)(2,1)S(1)}, u32[]{:S(2)}, u32[]{:S(2)}) %collective-permute-start) | collective-permute-done | bytes 294944 | tf_op jit(solution)/shard_map/ppermute | solution.py:500
  11.6 9.0 %all-to-all-start = ((bf16[32,32,384]{2,1,0:T(8,128)(2,1)}), bf16[32,32,384]{2,1,0:T(8,128)(2,1)S(1)}, u32[]{:S(2)}, u32[]{:S(2)}) async-start(bf16[32,32,384]{2,1,0:T(8,128)(2,1)} %bitcast.7), calls=%async_computation | async-start | bytes 1572864 | tf_op jit(solution)/shard_map/all_to_all | solution.py:503
  20.6 0.7 %join.1 = bf16[480,1024]{1,0:T(8,128)(2,1)} custom-call(bf16[480,1024]{1,0:T(8,128)(2,1)} %get-tuple-element.13._whole_in, bf16[144,1024]{1,0:T(8,128)(2,1)S(1)} %collective-permute-done.1._tail.mate_ref, bf16[144,1024]{1,0:T(8,128)(2,1)S(1)} %collective-permute-done._head.other_ref), custom_call_target="tpu_custom_call", output_to_operand_aliasing={{}: (0, {})} | custom-call | tf_op jit(solution)/shard_map/join/pallas_call | solution.py:440
  21.3 5.7 %collective-permute-start.3 = (bf16[480,1024]{1,0:T(8,128)(2,1)}, bf16[480,1024]{1,0:T(8,128)(2,1)S(1)}, u32[]{:S(2)}, u32[]{:S(2)}) collective-permute-start(bf16[480,1024]{1,0:T(8,128)(2,1)} %join.1), channel_id=1, source_target_pairs={{32,0},{64,32},{96,64},{128,96},{160,128},{192,160},{224,192},{0,2... | collective-permute-start | bytes 2949128 | tf_op jit(solution)/shard_map/ppermute | solution.py:513
  27.0 6.8 %forward.1 = bf16[384,1024]{1,0:T(8,128)(2,1)} custom-call(f32[12,32,1024]{2,1,0:T(8,128)} %bitcast.28, f32[12,32,1024]{2,1,0:T(8,128)} %bitcast.32, bf16[144,1024]{1,0:T(8,128)(2,1)S(1)} %collective-permute-done.1._tail.mate_ref, bf16[144,1024]{1,0:T(8,128)(2,1)S(1)} %collective-permute-done._head.other_ref), custom_call_target="tpu_custom_call" | custom-call | tf_op jit(solution)/shard_map/forward/pallas_call | solution.py:440
  33.8 0.1 collective-permute-start.2
  33.9 0.9 %all-to-all-done.came_ref = bf16[32,32,384]{2,1,0:T(8,128)(2,1)S(1)} async-done(((bf16[32,32,384]{2,1,0:T(8,128)(2,1)}), bf16[32,32,384]{2,1,0:T(8,128)(2,1)S(1)}, u32[]{:S(2)}, u32[]{:S(2)}) %all-to-all-start) | async-done | bytes 786464 | tf_op jit(solution)/shard_map/all_to_all | solution.py:503
  34.8 4.7 %latitude.1._after = bf16[1024,384]{1,0:T(8,128)(2,1)} custom-call(bf16[32,32,384]{2,1,0:T(8,128)(2,1)S(1)} %all-to-all-done.came_ref, f32[384,1024]{1,0:T(8,128)} %bitcast.34, bf16[1024,1024]{1,0:T(8,128)(2,1)} %constant.9.clone.turned_hbm), custom_call_target="tpu_custom_call" | custom-call | tf_op jit(solution)/shard_map/latitude/pallas_call | solution.py:440
  39.6 0.0 copy-start.2
  39.6 0.0 copy-start.3
  39.6 0.0 copy-start.4
  39.6 0.0 copy-start.5
  39.6 0.0 copy-start.6
  39.6 6.9 %all-to-all-start.1 = ((bf16[32,32,384]{2,1,0:T(8,128)(2,1)}), bf16[32,32,384]{2,1,0:T(8,128)(2,1)S(1)}, u32[]{:S(2)}, u32[]{:S(2)}) async-start(bf16[32,32,384]{2,1,0:T(8,128)(2,1)} %bitcast.10), calls=%async_computation.1 | async-start | bytes 1572864 | tf_op jit(solution)/shard_map/all_to_all | solution.py:541
  46.6 3.2 %observe.1 = (f32[384,64]{1,0:T(8,128)S(1)}, f32[1,512]{1,0:T(1,128)}) custom-call(f32[12,32,1024]{2,1,0:T(8,128)} %bitcast.29, s32[1,512]{1,0:T(1,128)S(1)} %copy-done.4, f32[1,512]{1,0:T(1,128)S(1)} %copy-done.5, f32[1,512]{1,0:T(1,128)S(1)} %copy-done.6, bf16[1024,64]{1,0:T(8,128)(2,1)S(1)} %copy-done.2, bf16[96,384]{1,0:T(8,128)(2,1)S(1)} %copy-done.3, ...), custom_call_target="tpu_custom_call" | custom-call | tf_op jit(solution)/shard_map/observe/pallas_call | solution.py:440
  49.8 7.7 %backward.1 = f32[12,32,1024]{2,1,0:T(8,128)} custom-call(bf16[480,1024]{1,0:T(8,128)(2,1)S(1)} %collective-permute-done.3.coming_ref, f32[12,32,1024]{2,1,0:T(8,128)} %bitcast.33, bf16[144,1024]{1,0:T(8,128)(2,1)S(1)} %collective-permute-done.1._tail.mate_ref, bf16[144,1024]{1,0:T(8,128)(2,1)S(1)} %collective-permute-done._head.other_ref, ...), custom_call_target="tpu_custom_call" | custom-call | tf_op jit(solution)/shard_map/backward/pallas_call | solution.py:440
  57.5 3.2 %all-to-all-done.1.came_ref = bf16[32,32,384]{2,1,0:T(8,128)(2,1)S(1)} async-done(((bf16[32,32,384]{2,1,0:T(8,128)(2,1)}), bf16[32,32,384]{2,1,0:T(8,128)(2,1)S(1)}, u32[]{:S(2)}, u32[]{:S(2)}) %all-to-all-start.1) | async-done | bytes 786464 | tf_op jit(solution)/shard_map/all_to_all | solution.py:541
  60.7 4.0 %finish.1 = f32[384,1024]{1,0:T(8,128)} custom-call(bf16[32,32,384]{2,1,0:T(8,128)(2,1)S(1)} %all-to-all-done.1.came_ref, f32[384,1024]{1,0:T(8,128)} %bitcast.30, bf16[384,1024]{1,0:T(8,128)(2,1)S(1)} %collective-permute-done.2.prev_ref, bf16[1024,1024]{1,0:T(8,128)(2,1)} %constant.8.clone.table_ref.table_hbm), custom_call_target="tpu_custom_call" | custom-call | tf_op jit(solution)/shard_map/finish/pallas_call | solution.py:440
  (11 shorter events, 0.0 us)
Async XLA Ops:
  0.6 6.7 %copy-start = (f32[1,32,12,1024]{3,1,2,0:T(8,128)S(1)}, f32[1,32,12,1024]{3,1,2,0:T(8,128)}, u32[]{:S(2)}) copy-start(f32[1,32,12,1024]{3,1,2,0:T(8,128)} %param.12) | copy-start | bytes 4718596
  0.6 6.7 %copy-start.1 = (bf16[1024,1024]{1,0:T(8,128)(2,1)S(1)}, bf16[1024,1024]{1,0:T(8,128)(2,1)}, u32[]{:S(2)}) copy-start(bf16[1024,1024]{1,0:T(8,128)(2,1)} %constant.8.clone.table_ref.table_hbm) | copy-start | bytes 6291460
  2.6 9.0 %collective-permute-start = (bf16[144,1024]{1,0:T(8,128)(2,1)S(1)}, bf16[144,1024]{1,0:T(8,128)(2,1)S(1)}, u32[]{:S(2)}, u32[]{:S(2)}) collective-permute-start(bf16[144,1024]{1,0:T(8,128)(2,1)S(1)} %get-tuple-element.9._after), channel_id=1, source_target_pairs={{0,0},{1,2},{2,1},{3,4},{4,3},{5,6},{6,5},{7,8},{8,7},{9,10},{10,9... | collective-permute-start | bytes 884744 | tf_op jit(solution)/shard_map/ppermute | solution.py:500
  7.2 4.4 %collective-permute-start.1 = (bf16[144,1024]{1,0:T(8,128)(2,1)S(1)}, bf16[144,1024]{1,0:T(8,128)(2,1)S(1)}, u32[]{:S(2)}, u32[]{:S(2)}) collective-permute-start(bf16[144,1024]{1,0:T(8,128)(2,1)S(1)} %get-tuple-element.11), channel_id=1, source_target_pairs={{0,1},{1,0},{2,3},{3,2},{4,5},{5,4},{6,7},{7,6},{8,9},{9,8},{10,11... | collective-permute-start | bytes 884744 | tf_op jit(solution)/shard_map/ppermute | solution.py:501
  11.6 23.2 %all-to-all-start = ((bf16[32,32,384]{2,1,0:T(8,128)(2,1)}), bf16[32,32,384]{2,1,0:T(8,128)(2,1)S(1)}, u32[]{:S(2)}, u32[]{:S(2)}) async-start(bf16[32,32,384]{2,1,0:T(8,128)(2,1)} %bitcast.7), calls=%async_computation | async-start | bytes 1572864 | tf_op jit(solution)/shard_map/all_to_all | solution.py:503
  21.3 28.5 %collective-permute-start.3 = (bf16[480,1024]{1,0:T(8,128)(2,1)}, bf16[480,1024]{1,0:T(8,128)(2,1)S(1)}, u32[]{:S(2)}, u32[]{:S(2)}) collective-permute-start(bf16[480,1024]{1,0:T(8,128)(2,1)} %join.1), channel_id=1, source_target_pairs={{32,0},{64,32},{96,64},{128,96},{160,128},{192,160},{224,192},{0,2... | collective-permute-start | bytes 2949128 | tf_op jit(solution)/shard_map/ppermute | solution.py:513
  33.8 23.7 %collective-permute-start.2 = (bf16[384,1024]{1,0:T(8,128)(2,1)}, bf16[384,1024]{1,0:T(8,128)(2,1)S(1)}, u32[]{:S(2)}, u32[]{:S(2)}) collective-permute-start(bf16[384,1024]{1,0:T(8,128)(2,1)} %forward.1), channel_id=1, source_target_pairs={{0,32},{32,64},{64,96},{96,128},{128,160},{160,192},{192,224},{224... | collective-permute-start | bytes 2359304 | tf_op jit(solution)/shard_map/ppermute | solution.py:528
  39.6 6.9 %copy-start.2 = (bf16[1024,64]{1,0:T(8,128)(2,1)S(1)}, bf16[1024,64]{1,0:T(8,128)(2,1)}, u32[]{:S(2)}) copy-start(bf16[1024,64]{1,0:T(8,128)(2,1)} %constant.10.clone.cols_hbm) | copy-start | bytes 393220
  39.6 6.9 %copy-start.3 = (bf16[96,384]{1,0:T(8,128)(2,1)S(1)}, bf16[96,384]{1,0:T(8,128)(2,1)}, u32[]{:S(2)}) copy-start(bf16[96,384]{1,0:T(8,128)(2,1)} %constant.11.clone.lines_hbm) | copy-start | bytes 221188
  39.6 6.9 %copy-start.4 = (s32[1,512]{1,0:T(1,128)S(1)}, s32[1,512]{1,0:T(1,128)}, u32[]{:S(2)}) copy-start(s32[1,512]{1,0:T(1,128)} %index_ref.1) | copy-start | bytes 6148
  39.6 6.9 %copy-start.5 = (f32[1,512]{1,0:T(1,128)S(1)}, f32[1,512]{1,0:T(1,128)}, u32[]{:S(2)}) copy-start(f32[1,512]{1,0:T(1,128)} %dual_ref.1) | copy-start | bytes 6148
  39.6 6.9 %copy-start.6 = (f32[1,512]{1,0:T(1,128)S(1)}, f32[1,512]{1,0:T(1,128)}, u32[]{:S(2)}) copy-start(f32[1,512]{1,0:T(1,128)} %variance_ref.1) | copy-start | bytes 6148
  39.6 21.1 %all-to-all-start.1 = ((bf16[32,32,384]{2,1,0:T(8,128)(2,1)}), bf16[32,32,384]{2,1,0:T(8,128)(2,1)S(1)}, u32[]{:S(2)}, u32[]{:S(2)}) async-start(bf16[32,32,384]{2,1,0:T(8,128)(2,1)} %bitcast.10), calls=%async_computation.1 | async-start | bytes 1572864 | tf_op jit(solution)/shard_map/all_to_all | solution.py:541
